TPU v7x, 256 devices: a whole 4x4x8 slice. The times are simulated.
256 devices in a mesh: layer: 16 (over z_lo, y, core), ex: 16 (over z_hi, x).
Axes of the slice: x: 4, y: 4, z: 8 (z_hi: 4, z_lo: 2; z = z_hi * 2 + z_lo), core: 2. Of those that a mesh axis runs over, the one named last changes fastest.
Arguments:
- query_grads: bfloat16 [32, 512, 4096], P('layer', 'ex'), may hold values from -0.09375 to 0.09375
- train_grads: bfloat16 [32, 8192, 4096], P('layer', 'ex'), may hold values from -6 to 6
- basis_out: float32 [32, 64, 64], P('layer'), may hold values from -0.75 to 0.75
- basis_in: float32 [32, 64, 64], P('layer'), may hold values from -0.75 to 0.75
- eigen: float32 [32, 64, 64], P('layer'), may hold values from 0.0005 to 100, as said below
Outputs:
- scores: float32 [512, 8192], P('layer', 'ex')
Inputs may be any that keep to these rules, and one draw needn't show every extreme that they name: eigen is positive.
All inputs are finite; a program needn't handle non-finite values.
Results may differ from a plain program's by a relative error of at most 0.0029.
Values may be sent and summed in bfloat16 or wider, within the bound.
No kernel may reach another device: no remote copies, remote signals or barrier semaphores. Data moves between devices by JAX's collectives and lax.ppermute only.
A program may use at most 128 MiB of HBM per device.

v0:
```python
import functools

import jax
import jax.numpy as jnp
from jax import lax
from jax.experimental import pallas as pl
from jax.experimental.pallas import tpu as pltpu
from jax.sharding import PartitionSpec as P

SIDE = 4
TILE = 2048

def split(v):
    hi = v.astype(jnp.bfloat16)
    return hi, (v - hi.astype(jnp.float32)).astype(jnp.bfloat16)

def twice(block):
    none = jnp.zeros_like(block)
    return jnp.concatenate([jnp.concatenate([block, none], axis=1), jnp.concatenate([none, block], axis=1)], axis=0)

def dot(a, b, dims=((1,), (0,))):
    return lax.dot_general(a, b, (dims, ((), ())), preferred_element_type=jnp.float32)

def precondition_kernel(raw, basis_out, basis_in, eigen, out, work):
    count_q, entries = raw.shape[1:]
    side = basis_out.shape[1]
    half = count_q // 2
    low = lax.broadcasted_iota(jnp.int32, (half, 2 * side), 1) < side

    out_hi, out_lo = split(basis_out[0])
    turned_hi, turned_lo = split(basis_out[0].T)
    in_hi, in_lo = split(twice(basis_in[0]))
    damped = eigen[0] + 0.1 * jnp.mean(eigen[0])
    inverse = 1.0 / damped
    inverse = jnp.concatenate([inverse, inverse], axis=1)

    rows = []
    for pair in range(side // 2):
        tile = raw[0, :, pl.ds(pair * 2 * side, 2 * side)].astype(jnp.float32)
        top, bottom = tile[:half], tile[half:]
        rows.append(jnp.where(low, top, pltpu.roll(bottom, side, 1)))
        rows.append(jnp.where(low, pltpu.roll(top, side, 1), bottom))
    grads = jnp.concatenate(rows, axis=0).astype(jnp.bfloat16)
    work[...] = dot(jnp.concatenate([grads, grads], axis=1), jnp.concatenate([in_hi, in_lo], axis=0))
    left = jnp.concatenate([work[pl.ds(q, side, stride=half), :] for q in range(half)], axis=1)
    hi, lo = split(left)
    rotated = dot(jnp.concatenate([turned_hi, turned_hi, turned_lo], axis=1), jnp.concatenate([hi, lo, hi], axis=0))
    scaled = jnp.concatenate([rotated[:, q * 2 * side : (q + 1) * 2 * side] * inverse for q in range(half)], axis=1)
    hi, lo = split(scaled)
    back = dot(jnp.concatenate([out_hi, out_hi, out_lo], axis=1), jnp.concatenate([hi, lo, hi], axis=0))
    back = jnp.concatenate([back[:, q * 2 * side : (q + 1) * 2 * side] for q in range(half)], axis=0)
    hi, lo = split(back)
    nt = ((1,), (1,))
    work[...] = dot(jnp.concatenate([hi, lo], axis=1), jnp.concatenate([in_hi, in_hi], axis=1), nt) + dot(hi, in_lo, nt)
    for pair in range(side // 2):
        even, odd = work[pl.ds(2 * pair, half, stride=side), :], work[pl.ds(2 * pair + 1, half, stride=side), :]
        at = pl.ds(pair * 2 * side, 2 * side)
        out[0, :half, at] = jnp.where(low, even, pltpu.roll(odd, side, 1)).astype(out.dtype)
        out[0, half:, at] = jnp.where(low, pltpu.roll(even, side, 1), odd).astype(out.dtype)

def precondition(raw, basis_out, basis_in, eigen):
    modules, count_q, entries = raw.shape
    side = basis_out.shape[1]
    per_module = lambda *shape: pl.BlockSpec((1,) + shape, lambda m: (m, 0, 0))
    return pl.pallas_call(
        precondition_kernel,
        out_shape=jax.ShapeDtypeStruct(raw.shape, jnp.bfloat16),
        grid=(modules,),
        in_specs=[per_module(count_q, entries)] + [per_module(side, side)] * 3,
        out_specs=per_module(count_q, entries),
        scratch_shapes=[pltpu.VMEM((side * count_q // 2, 2 * side), jnp.float32)],
        compiler_params=pltpu.CompilerParams(vmem_limit_bytes=56 << 20),
    )(raw, basis_out, basis_in, eigen)


def move(value, step_z, step_x):
    to = lambda z, x: (z + step_z) % SIDE * SIDE + (x + step_x) % SIDE
    return lax.ppermute(value, "ex", [(z * SIDE + x, to(z, x)) for z in range(SIDE) for x in range(SIDE)])


def in_order(*values):
    return lax.optimization_barrier(values)


def join_kernel(first, second, out):
    out[:1] = first[...]
    out[1:] = second[...]


def join(first, second):
    space = pl.BlockSpec(memory_space=pltpu.VMEM)
    return pl.pallas_call(
        join_kernel,
        out_shape=jax.ShapeDtypeStruct((2,) + first.shape[1:], first.dtype),
        in_specs=[space, space],
        out_specs=space,
        compiler_params=pltpu.CompilerParams(vmem_limit_bytes=4 << 20),
    )(first, second)


def scores_of(shards, train, modules):
    total = None
    for module in modules:
        for at in range(0, train.shape[2], TILE):
            part = pl.ds(at, TILE)
            rows = jnp.concatenate([s[0][module, :, part] if len(s) == 1 else s[module][0, :, part] for s in shards], axis=0)
            term = dot(train[module, :, part], rows, ((1,), (1,)))
            total = term if total is None else total + term
    return total


def blocks_of(total, shape, dtype):
    return total.T.astype(dtype).reshape((-1,) + shape)


def next_kernel(counts, *refs):
    shards, (train, out) = take(refs, counts)
    out[...] = blocks_of(scores_of(shards, train, range(train.shape[0])), out.shape[1:], out.dtype)


def last_kernel(counts, done_counts, offsets, me, *refs):
    shards, refs = take(refs, counts)
    train, done, out = refs[0], refs[1:-1], refs[-1]
    z, x = lax.shift_right_logical(me[0], 2), me[0] & (SIDE - 1)
    places = [((z + dz) & (SIDE - 1)) * SIDE + ((x + dx) & (SIDE - 1)) for dz, dx in offsets]
    at = 0
    for ref, count in zip(done, done_counts):
        for i in range(count):
            out[places[at]] = ref[i]
            at += 1
    blocks = blocks_of(scores_of(shards, train, range(train.shape[0])), out.shape[1:], out.dtype)
    for i in range(len(shards)):
        out[places[at + i]] = blocks[i]


def take(refs, counts):
    shards, at = [], 0
    for count in counts:
        shards.append(refs[at : at + count])
        at += count
    return shards, refs[at:]


def score_call(kernel, shards, others, other_specs, out_shapes, scratch=(), lead=()):
    shards = [s if isinstance(s, tuple) else (s,) for s in shards]
    flat = [half for s in shards for half in s]
    space = pl.BlockSpec(memory_space=pltpu.VMEM)
    train = next(o for o in others if o.ndim == 3 and o.dtype == flat[0].dtype)
    rows = len(shards) * flat[0].shape[1]
    return pl.pallas_call(
        functools.partial(kernel, tuple(len(s) for s in shards)),
        out_shape=out_shapes,
        in_specs=[pl.BlockSpec(memory_space=pltpu.SMEM)] * len(lead) + [space] * len(flat) + list(other_specs),
        out_specs=jax.tree.map(lambda _: space, out_shapes),
        scratch_shapes=list(scratch),
        compiler_params=pltpu.CompilerParams(vmem_limit_bytes=16 << 20),
        cost_estimate=pl.CostEstimate(
            flops=2 * rows * train.size,
            bytes_accessed=2 * (train.size + rows * train.size // train.shape[1]),
            transcendentals=0,
        ),
    )(*lead, *flat, *others)


def scores_next(shards, train):
    shape = (len(shards), shards[0].shape[1], train.shape[1])
    return score_call(
        next_kernel, shards, [train], [pl.BlockSpec(memory_space=pltpu.VMEM)], jax.ShapeDtypeStruct(shape, jnp.bfloat16)
    )


def scores_last(shards, train, done, offsets, me):
    counts = tuple(d.shape[0] for d in done)
    shape = (sum(counts) + len(shards),) + done[0].shape[1:]
    kernel = lambda own_counts, *refs: last_kernel(own_counts, counts, offsets, *refs)
    space = pl.BlockSpec(memory_space=pltpu.VMEM)
    return score_call(
        kernel,
        shards,
        [train, *done],
        [space] * (1 + len(done)),
        jax.ShapeDtypeStruct(shape, jnp.bfloat16),
        lead=[me],
    )


def local(query_grads, train_grads, basis_out, basis_in, eigen):
    me = lax.axis_index("ex").astype(jnp.int32).reshape(1)
    own = precondition(query_grads, basis_out, basis_in, eigen)
    zl, zr = move(own, 1, 0), move(own, -1, 0)
    xl, xr = move(own, 0, 1), move(own, 0, -1)
    x2 = move(own, 0, 2)
    zl, zr, xl, xr, x2 = in_order(zl, zr, xl, xr, x2)
    z2 = (move(zl[:1], 1, 0), move(zr[1:], -1, 0))
    zl_xl, zr_xr = move(zl, 0, 1), move(zr, 0, -1)
    first = scores_next([own, xl, xr, x2, zl, zr], train_grads)
    z2a, z2b, zl, zr, x2, zl_xl, zr_xr, first = in_order(*z2, zl, zr, x2, zl_xl, zr_xr, first)
    z2 = join(z2a, z2b)
    zl_x2, zr_x2 = move(x2[:1], 1, 0), move(x2[:1], -1, 0)
    z2_xl, z2_xr = move(z2, 0, 1), move(z2, 0, -1)
    z2_xl, z2_xr, zl, zr, x2, zl_x2, zr_x2 = in_order(z2_xl, z2_xr, zl, zr, x2, zl_x2, zr_x2)
    zl_x2, zr_x2 = (zl_x2, move(x2[1:], 1, 0)), (zr_x2, move(x2[1:], -1, 0))
    zr_xl, zl_xr = move(zr, 0, 1), move(zl, 0, -1)
    second = scores_next([zl_xl, zr_xr, z2, z2_xl, z2_xr], train_grads)
    z2_xl, z2_xr, second, zr_xl, zl_xr, *late = in_order(z2_xl, z2_xr, second, zr_xl, zl_xr, zl_x2[1], zr_x2[1])
    zl_x2, zr_x2 = (zl_x2[0], late[0]), (zr_x2[0], late[1])
    z2_x2 = (move(z2_xl[:1], 0, 1), move(z2_xr[1:], 0, -1))
    offsets = [
        (0, 0), (0, -1), (0, 1), (0, 2), (-1, 0), (1, 0),
        (-1, -1), (1, 1), (2, 0), (2, -1), (2, 1),
        (-1, 2), (1, 2), (2, 2), (1, -1), (-1, 1),
    ]
    parts = scores_last([zl_x2, zr_x2, z2_x2, zr_xl, zl_xr], train_grads, (first, second), offsets, me)
    parts = lax.all_to_all(parts, "layer", split_axis=0, concat_axis=0, tiled=True)
    return jnp.sum(parts.astype(jnp.float32), axis=0)


def solution(mesh):
    in_specs = (
        P("layer", "ex", None),
        P("layer", "ex", None),
        P("layer", None, None),
        P("layer", None, None),
        P("layer", None, None),
    )
    out_specs = P("layer", "ex")
    return jax.shard_map(local, mesh=mesh, in_specs=in_specs, out_specs=out_specs, check_vma=False)
```

profile of v0, /device:TPU:1, one launch (start us, length us, event | category | flops | bytes accessed | tf_op | source)
XLA Modules:
  0.0 122.0 jit_solution(13401299026524548192)
XLA Ops:
  0.0 4.9 %shard_map.55.refs_0_ = bf16[2,32,4096]{2,1,0:T(8,128)(2,1)} custom-call(bf16[2,32,4096]{2,1,0:T(8,128)(2,1)} %raw.1, f32[2,64,64]{2,1,0:T(8,128)} %basis_out.1, f32[2,64,64]{2,1,0:T(8,128)} %basis_in.1, f32[2,64,64]{2,1,0:T(8,128)} %eigen.1), custom_call_target="tpu_custom_call" | custom-call | tf_op jit(solution)/shard_map/pallas_call | solution.py:65
  4.9 3.6 %collective-permute-start.4 = (bf16[2,32,4096]{2,1,0:T(8,128)(2,1)}, bf16[2,32,4096]{2,1,0:T(8,128)(2,1)S(1)}, u32[]{:S(2)}, u32[]{:S(2)}) collective-permute-start(bf16[2,32,4096]{2,1,0:T(8,128)(2,1)} %shard_map.55.refs_0_), channel_id=1, source_target_pairs={{0,2},{1,3},{2,0},{3,1},{4,6},{5,7},{6,4},{7,5},{8,10},{9,11},{10,... | collective-permute-start | bytes 1572872 | tf_op jit(solution)/shard_map/ppermute | solution.py:78
  8.4 0.9 collective-permute-start.3
  9.3 0.6 collective-permute-start.2
  9.9 6.0 %collective-permute-start.1 = (bf16[2,32,4096]{2,1,0:T(8,128)(2,1)}, bf16[2,32,4096]{2,1,0:T(8,128)(2,1)S(1)}, u32[]{:S(2)}, u32[]{:S(2)}) collective-permute-start(bf16[2,32,4096]{2,1,0:T(8,128)(2,1)} %shard_map.55.refs_0_), channel_id=1, source_target_pairs={{0,12},{1,13},{2,14},{3,15},{4,0},{5,1},{6,2},{7,3},{8,4},{9,5},{1... | collective-permute-start | bytes 1572872 | tf_op jit(solution)/shard_map/ppermute | solution.py:78
  15.9 3.5 %collective-permute-done.4.refs_3_ = bf16[2,32,4096]{2,1,0:T(8,128)(2,1)S(1)} collective-permute-done((bf16[2,32,4096]{2,1,0:T(8,128)(2,1)}, bf16[2,32,4096]{2,1,0:T(8,128)(2,1)S(1)}, u32[]{:S(2)}, u32[]{:S(2)}) %collective-permute-start.4) | collective-permute-done | bytes 524320 | tf_op jit(solution)/shard_map/ppermute | solution.py:78
  19.4 12.3 %collective-permute-done.3.refs_2_ = bf16[2,32,4096]{2,1,0:T(8,128)(2,1)S(1)} collective-permute-done((bf16[2,32,4096]{2,1,0:T(8,128)(2,1)}, bf16[2,32,4096]{2,1,0:T(8,128)(2,1)S(1)}, u32[]{:S(2)}, u32[]{:S(2)}) %collective-permute-start.3) | collective-permute-done | bytes 524320 | tf_op jit(solution)/shard_map/ppermute | solution.py:78
  31.7 0.6 collective-permute-done.2.refs_1_
  32.3 3.4 %collective-permute-done.1.refs_5_ = bf16[2,32,4096]{2,1,0:T(8,128)(2,1)S(1)} collective-permute-done((bf16[2,32,4096]{2,1,0:T(8,128)(2,1)}, bf16[2,32,4096]{2,1,0:T(8,128)(2,1)S(1)}, u32[]{:S(2)}, u32[]{:S(2)}) %collective-permute-start.1) | collective-permute-done | bytes 524320 | tf_op jit(solution)/shard_map/ppermute | solution.py:78
  36.0 2.4 %collective-permute-start.8 = (bf16[2,32,4096]{2,1,0:T(8,128)(2,1)S(1)}, bf16[2,32,4096]{2,1,0:T(8,128)(2,1)S(1)}, u32[]{:S(2)}, u32[]{:S(2)}) collective-permute-start(bf16[2,32,4096]{2,1,0:T(8,128)(2,1)S(1)} %collective-permute-done.1.refs_5_), channel_id=1, source_target_pairs={{0,3},{1,0},{2,1},{3,2},{4,7},{5,4},{6,5},{7,6},{8,11},{9,8},{10,9... | collective-permute-start | bytes 1572872 | tf_op jit(solution)/shard_map/ppermute | solution.py:78
  38.4 4.3 %collective-permute-start.6 = (bf16[1,32,4096]{2,1,0:T(8,128)(2,1)S(1)}, bf16[1,32,4096]{2,1,0:T(8,128)(2,1)S(1)}, u32[]{:S(2)}, u32[]{:S(2)}) collective-permute-start(bf16[1,32,4096]{2,1,0:T(8,128)(2,1)S(1)} %slice.21), channel_id=1, source_target_pairs={{0,12},{1,13},{2,14},{3,15},{4,0},{5,1},{6,2},{7,3},{8,4},{9,5},{1... | collective-permute-start | bytes 786440 | tf_op jit(solution)/shard_map/ppermute | solution.py:78
  43.1 3.4 %copy-done = bf16[2,512,4096]{2,1,0:T(8,128)(2,1)S(1)} copy-done((bf16[2,512,4096]{2,1,0:T(8,128)(2,1)S(1)}, bf16[2,512,4096]{2,1,0:T(8,128)(2,1)}, u32[]{:S(2)}) %copy-start) | copy-done | bytes 8388632
  46.5 1.0 copy-done.3
  47.5 2.4 %shard_map.56.refs_10_ = bf16[6,32,512]{2,1,0:T(8,128)(2,1)S(1)} custom-call(bf16[2,32,4096]{2,1,0:T(8,128)(2,1)S(1)} %copy-done.3, bf16[2,32,4096]{2,1,0:T(8,128)(2,1)S(1)} %collective-permute-done.2.refs_1_, bf16[2,32,4096]{2,1,0:T(8,128)(2,1)S(1)} %collective-permute-done.3.refs_2_, bf16[2,32,4096]{2,1,0:T(8,128)(2,1)S(1)} %collective-permute-done.4.refs_3_, ...), custom_call_target="tpu_custom_call" | custom-call | flops 1610612736 | bytes 11534336 | tf_op jit(solution)/shard_map/pallas_call | solution.py:150
  50.1 0.9 collective-permute-start.10
  51.7 3.3 %collective-permute-start.12 = (bf16[1,32,4096]{2,1,0:T(8,128)(2,1)S(1)}, bf16[1,32,4096]{2,1,0:T(8,128)(2,1)S(1)}, u32[]{:S(2)}, u32[]{:S(2)}) collective-permute-start(bf16[1,32,4096]{2,1,0:T(8,128)(2,1)S(1)} %slice.22), channel_id=1, source_target_pairs={{0,12},{1,13},{2,14},{3,15},{4,0},{5,1},{6,2},{7,3},{8,4},{9,5},{1... | collective-permute-start | bytes 786440 | tf_op jit(solution)/shard_map/ppermute | solution.py:78
  55.0 1.4 %collective-permute-start.11 = (bf16[1,32,4096]{2,1,0:T(8,128)(2,1)S(1)}, bf16[1,32,4096]{2,1,0:T(8,128)(2,1)S(1)}, u32[]{:S(2)}, u32[]{:S(2)}) collective-permute-start(bf16[1,32,4096]{2,1,0:T(8,128)(2,1)S(1)} %slice.22), channel_id=1, source_target_pairs={{0,4},{1,5},{2,6},{3,7},{4,8},{5,9},{6,10},{7,11},{8,12},{9,13},{1... | collective-permute-start | bytes 786440 | tf_op jit(solution)/shard_map/ppermute | solution.py:78
  56.5 5.2 %collective-permute-done.12.refs_3_ = bf16[1,32,4096]{2,1,0:T(8,128)(2,1)S(1)} collective-permute-done((bf16[1,32,4096]{2,1,0:T(8,128)(2,1)S(1)}, bf16[1,32,4096]{2,1,0:T(8,128)(2,1)S(1)}, u32[]{:S(2)}, u32[]{:S(2)}) %collective-permute-start.12) | collective-permute-done | bytes 262176 | tf_op jit(solution)/shard_map/ppermute | solution.py:78
  61.7 2.8 %collective-permute-done.11.refs_1_ = bf16[1,32,4096]{2,1,0:T(8,128)(2,1)S(1)} collective-permute-done((bf16[1,32,4096]{2,1,0:T(8,128)(2,1)S(1)}, bf16[1,32,4096]{2,1,0:T(8,128)(2,1)S(1)}, u32[]{:S(2)}, u32[]{:S(2)}) %collective-permute-start.11) | collective-permute-done | bytes 262176 | tf_op jit(solution)/shard_map/ppermute | solution.py:78
  64.5 2.7 %collective-permute-start.14 = (bf16[2,32,4096]{2,1,0:T(8,128)(2,1)S(1)}, bf16[2,32,4096]{2,1,0:T(8,128)(2,1)S(1)}, u32[]{:S(2)}, u32[]{:S(2)}) collective-permute-start(bf16[2,32,4096]{2,1,0:T(8,128)(2,1)S(1)} %collective-permute-done.refs_4_), channel_id=1, source_target_pairs={{0,3},{1,0},{2,1},{3,2},{4,7},{5,4},{6,5},{7,6},{8,11},{9,8},{10,9... | collective-permute-start | bytes 1572872 | tf_op jit(solution)/shard_map/ppermute | solution.py:78
  67.2 6.2 %collective-permute-start.16 = (bf16[1,32,4096]{2,1,0:T(8,128)(2,1)S(1)}, bf16[1,32,4096]{2,1,0:T(8,128)(2,1)S(1)}, u32[]{:S(2)}, u32[]{:S(2)}) collective-permute-start(bf16[1,32,4096]{2,1,0:T(8,128)(2,1)S(1)} %slice.23), channel_id=1, source_target_pairs={{0,12},{1,13},{2,14},{3,15},{4,0},{5,1},{6,2},{7,3},{8,4},{9,5},{1... | collective-permute-start | bytes 786440 | tf_op jit(solution)/shard_map/ppermute | solution.py:78
  73.4 2.4 %shard_map.58.refs_11_ = bf16[5,32,512]{2,1,0:T(8,128)(2,1)S(1)} custom-call(bf16[2,32,4096]{2,1,0:T(8,128)(2,1)S(1)} %collective-permute-done.7.refs_0_, bf16[2,32,4096]{2,1,0:T(8,128)(2,1)S(1)} %collective-permute-done.8.refs_1_, bf16[2,32,4096]{2,1,0:T(8,128)(2,1)S(1)} %shard_map.57.refs_2_, bf16[2,32,4096]{2,1,0:T(8,128)(2,1)S(1)} %collective-permute-done.9.refs_3_, ...), custom_call_target="tpu_custom_call" | custom-call | flops 1342177280 | bytes 11010048 | tf_op jit(solution)/shard_map/pallas_call | solution.py:150
  75.8 0.9 collective-permute-done.16.refs_4_
  76.7 4.0 %collective-permute-done.15.refs_2_ = bf16[1,32,4096]{2,1,0:T(8,128)(2,1)S(1)} collective-permute-done((bf16[1,32,4096]{2,1,0:T(8,128)(2,1)S(1)}, bf16[1,32,4096]{2,1,0:T(8,128)(2,1)S(1)}, u32[]{:S(2)}, u32[]{:S(2)}) %collective-permute-start.15) | collective-permute-done | bytes 262176 | tf_op jit(solution)/shard_map/ppermute | solution.py:78
  80.8 0.8 collective-permute-start.18
  81.6 0.7 collective-permute-start.17
  82.3 6.8 %collective-permute-done.18.refs_6_ = bf16[1,32,4096]{2,1,0:T(8,128)(2,1)S(1)} collective-permute-done((bf16[1,32,4096]{2,1,0:T(8,128)(2,1)S(1)}, bf16[1,32,4096]{2,1,0:T(8,128)(2,1)S(1)}, u32[]{:S(2)}, u32[]{:S(2)}) %collective-permute-start.18) | collective-permute-done | bytes 262176 | tf_op jit(solution)/shard_map/ppermute | solution.py:78
  89.2 0.8 collective-permute-done.17.refs_5_
  90.0 3.4 %copy-done.2 = bf16[2,512,4096]{2,1,0:T(8,128)(2,1)S(1)} copy-done((bf16[2,512,4096]{2,1,0:T(8,128)(2,1)S(1)}, bf16[2,512,4096]{2,1,0:T(8,128)(2,1)}, u32[]{:S(2)}) %copy-start.2) | copy-done | bytes 8388632
  93.4 2.4 %shard_map.59 = bf16[16,32,512]{2,1,0:T(8,128)(2,1)S(1)} custom-call(s32[1]{0:T(128)} %bitcast.refs_0_, bf16[1,32,4096]{2,1,0:T(8,128)(2,1)S(1)} %collective-permute-done.11.refs_1_, bf16[1,32,4096]{2,1,0:T(8,128)(2,1)S(1)} %collective-permute-done.15.refs_2_, bf16[1,32,4096]{2,1,0:T(8,128)(2,1)S(1)} %collective-permute-done.12.refs_3_, ...), custom_call_target="tpu_custom_call" | custom-call | flops 1342177280 | bytes 11010048 | tf_op jit(solution)/shard_map/pallas_call | solution.py:150
  95.8 25.5 %all_to_all.5 = bf16[16,32,512]{2,1,0:T(8,128)(2,1)S(1)} all-to-all(bf16[16,32,512]{2,1,0:T(8,128)(2,1)S(1)} %shard_map.59), channel_id=1, replica_groups=mesh['layer'=16,'ex'=16] {'layer'}, dimensions={0} | all-to-all | bytes 1048576 | tf_op jit(solution)/shard_map/all_to_all | solution.py:214
  121.3 0.7 convert_reduce_fusion
  (27 shorter events, 1.6 us)
Async XLA Ops:
  4.9 14.5 %collective-permute-start.4 = (bf16[2,32,4096]{2,1,0:T(8,128)(2,1)}, bf16[2,32,4096]{2,1,0:T(8,128)(2,1)S(1)}, u32[]{:S(2)}, u32[]{:S(2)}) collective-permute-start(bf16[2,32,4096]{2,1,0:T(8,128)(2,1)} %shard_map.55.refs_0_), channel_id=1, source_target_pairs={{0,2},{1,3},{2,0},{3,1},{4,6},{5,7},{6,4},{7,5},{8,10},{9,11},{10,... | collective-permute-start | bytes 1572872 | tf_op jit(solution)/shard_map/ppermute | solution.py:78
  8.4 23.2 %collective-permute-start.3 = (bf16[2,32,4096]{2,1,0:T(8,128)(2,1)}, bf16[2,32,4096]{2,1,0:T(8,128)(2,1)S(1)}, u32[]{:S(2)}, u32[]{:S(2)}) collective-permute-start(bf16[2,32,4096]{2,1,0:T(8,128)(2,1)} %shard_map.55.refs_0_), channel_id=1, source_target_pairs={{0,3},{1,0},{2,1},{3,2},{4,7},{5,4},{6,5},{7,6},{8,11},{9,8},{10,9... | collective-permute-start | bytes 1572872 | tf_op jit(solution)/shard_map/ppermute | solution.py:78
  9.3 23.0 %collective-permute-start.2 = (bf16[2,32,4096]{2,1,0:T(8,128)(2,1)}, bf16[2,32,4096]{2,1,0:T(8,128)(2,1)S(1)}, u32[]{:S(2)}, u32[]{:S(2)}) collective-permute-start(bf16[2,32,4096]{2,1,0:T(8,128)(2,1)} %shard_map.55.refs_0_), channel_id=1, source_target_pairs={{0,1},{1,2},{2,3},{3,0},{4,5},{5,6},{6,7},{7,4},{8,9},{9,10},{10,1... | collective-permute-start | bytes 1572872 | tf_op jit(solution)/shard_map/ppermute | solution.py:78
  9.9 25.8 %collective-permute-start.1 = (bf16[2,32,4096]{2,1,0:T(8,128)(2,1)}, bf16[2,32,4096]{2,1,0:T(8,128)(2,1)S(1)}, u32[]{:S(2)}, u32[]{:S(2)}) collective-permute-start(bf16[2,32,4096]{2,1,0:T(8,128)(2,1)} %shard_map.55.refs_0_), channel_id=1, source_target_pairs={{0,12},{1,13},{2,14},{3,15},{4,0},{5,1},{6,2},{7,3},{8,4},{9,5},{1... | collective-permute-start | bytes 1572872 | tf_op jit(solution)/shard_map/ppermute | solution.py:78
  15.9 19.8 %collective-permute-start = (bf16[2,32,4096]{2,1,0:T(8,128)(2,1)}, bf16[2,32,4096]{2,1,0:T(8,128)(2,1)S(1)}, u32[]{:S(2)}, u32[]{:S(2)}) collective-permute-start(bf16[2,32,4096]{2,1,0:T(8,128)(2,1)} %shard_map.55.refs_0_), channel_id=1, source_target_pairs={{0,4},{1,5},{2,6},{3,7},{4,8},{5,9},{6,10},{7,11},{8,12},{9,13},{1... | collective-permute-start | bytes 1572872 | tf_op jit(solution)/shard_map/ppermute | solution.py:78
  35.7 14.4 %collective-permute-start.7 = (bf16[2,32,4096]{2,1,0:T(8,128)(2,1)S(1)}, bf16[2,32,4096]{2,1,0:T(8,128)(2,1)S(1)}, u32[]{:S(2)}, u32[]{:S(2)}) collective-permute-start(bf16[2,32,4096]{2,1,0:T(8,128)(2,1)S(1)} %collective-permute-done.refs_4_), channel_id=1, source_target_pairs={{0,1},{1,2},{2,3},{3,0},{4,5},{5,6},{6,7},{7,4},{8,9},{9,10},{10,1... | collective-permute-start | bytes 1572872 | tf_op jit(solution)/shard_map/ppermute | solution.py:78
  36.0 14.1 %collective-permute-start.8 = (bf16[2,32,4096]{2,1,0:T(8,128)(2,1)S(1)}, bf16[2,32,4096]{2,1,0:T(8,128)(2,1)S(1)}, u32[]{:S(2)}, u32[]{:S(2)}) collective-permute-start(bf16[2,32,4096]{2,1,0:T(8,128)(2,1)S(1)} %collective-permute-done.1.refs_5_), channel_id=1, source_target_pairs={{0,3},{1,0},{2,1},{3,2},{4,7},{5,4},{6,5},{7,6},{8,11},{9,8},{10,9... | collective-permute-start | bytes 1572872 | tf_op jit(solution)/shard_map/ppermute | solution.py:78
  38.4 11.5 %collective-permute-start.6 = (bf16[1,32,4096]{2,1,0:T(8,128)(2,1)S(1)}, bf16[1,32,4096]{2,1,0:T(8,128)(2,1)S(1)}, u32[]{:S(2)}, u32[]{:S(2)}) collective-permute-start(bf16[1,32,4096]{2,1,0:T(8,128)(2,1)S(1)} %slice.21), channel_id=1, source_target_pairs={{0,12},{1,13},{2,14},{3,15},{4,0},{5,1},{6,2},{7,3},{8,4},{9,5},{1... | collective-permute-start | bytes 786440 | tf_op jit(solution)/shard_map/ppermute | solution.py:78
  42.7 7.4 %collective-permute-start.5 = (bf16[1,32,4096]{2,1,0:T(8,128)(2,1)S(1)}, bf16[1,32,4096]{2,1,0:T(8,128)(2,1)S(1)}, u32[]{:S(2)}, u32[]{:S(2)}) collective-permute-start(bf16[1,32,4096]{2,1,0:T(8,128)(2,1)S(1)} %slice.20), channel_id=1, source_target_pairs={{0,4},{1,5},{2,6},{3,7},{4,8},{5,9},{6,10},{7,11},{8,12},{9,13},{1... | collective-permute-start | bytes 786440 | tf_op jit(solution)/shard_map/ppermute | solution.py:78
  43.1 3.4 %copy-start = (bf16[2,512,4096]{2,1,0:T(8,128)(2,1)S(1)}, bf16[2,512,4096]{2,1,0:T(8,128)(2,1)}, u32[]{:S(2)}) copy-start(bf16[2,512,4096]{2,1,0:T(8,128)(2,1)} %refs_9_.1) | copy-start | bytes 25165828
  46.5 1.0 copy-start.3
  47.5 25.9 %copy-start.1 = (bf16[2,512,4096]{2,1,0:T(8,128)(2,1)S(1)}, bf16[2,512,4096]{2,1,0:T(8,128)(2,1)}, u32[]{:S(2)}) copy-start(bf16[2,512,4096]{2,1,0:T(8,128)(2,1)} %refs_9_.1) | copy-start | bytes 25165828
  50.1 14.3 %collective-permute-start.10 = (bf16[2,32,4096]{2,1,0:T(8,128)(2,1)S(1)}, bf16[2,32,4096]{2,1,0:T(8,128)(2,1)S(1)}, u32[]{:S(2)}, u32[]{:S(2)}) collective-permute-start(bf16[2,32,4096]{2,1,0:T(8,128)(2,1)S(1)} %shard_map.57.refs_2_), channel_id=1, source_target_pairs={{0,3},{1,0},{2,1},{3,2},{4,7},{5,4},{6,5},{7,6},{8,11},{9,8},{10,9... | collective-permute-start | bytes 1572872 | tf_op jit(solution)/shard_map/ppermute | solution.py:78
  51.1 13.4 %collective-permute-start.9 = (bf16[2,32,4096]{2,1,0:T(8,128)(2,1)S(1)}, bf16[2,32,4096]{2,1,0:T(8,128)(2,1)S(1)}, u32[]{:S(2)}, u32[]{:S(2)}) collective-permute-start(bf16[2,32,4096]{2,1,0:T(8,128)(2,1)S(1)} %shard_map.57.refs_2_), channel_id=1, source_target_pairs={{0,1},{1,2},{2,3},{3,0},{4,5},{5,6},{6,7},{7,4},{8,9},{9,10},{10,1... | collective-permute-start | bytes 1572872 | tf_op jit(solution)/shard_map/ppermute | solution.py:78
  51.7 10.0 %collective-permute-start.12 = (bf16[1,32,4096]{2,1,0:T(8,128)(2,1)S(1)}, bf16[1,32,4096]{2,1,0:T(8,128)(2,1)S(1)}, u32[]{:S(2)}, u32[]{:S(2)}) collective-permute-start(bf16[1,32,4096]{2,1,0:T(8,128)(2,1)S(1)} %slice.22), channel_id=1, source_target_pairs={{0,12},{1,13},{2,14},{3,15},{4,0},{5,1},{6,2},{7,3},{8,4},{9,5},{1... | collective-permute-start | bytes 786440 | tf_op jit(solution)/shard_map/ppermute | solution.py:78
  55.0 9.5 %collective-permute-start.11 = (bf16[1,32,4096]{2,1,0:T(8,128)(2,1)S(1)}, bf16[1,32,4096]{2,1,0:T(8,128)(2,1)S(1)}, u32[]{:S(2)}, u32[]{:S(2)}) collective-permute-start(bf16[1,32,4096]{2,1,0:T(8,128)(2,1)S(1)} %slice.22), channel_id=1, source_target_pairs={{0,4},{1,5},{2,6},{3,7},{4,8},{5,9},{6,10},{7,11},{8,12},{9,13},{1... | collective-permute-start | bytes 786440 | tf_op jit(solution)/shard_map/ppermute | solution.py:78
  64.5 16.3 %collective-permute-start.13 = (bf16[2,32,4096]{2,1,0:T(8,128)(2,1)S(1)}, bf16[2,32,4096]{2,1,0:T(8,128)(2,1)S(1)}, u32[]{:S(2)}, u32[]{:S(2)}) collective-permute-start(bf16[2,32,4096]{2,1,0:T(8,128)(2,1)S(1)} %collective-permute-done.1.refs_5_), channel_id=1, source_target_pairs={{0,1},{1,2},{2,3},{3,0},{4,5},{5,6},{6,7},{7,4},{8,9},{9,10},{10,1... | collective-permute-start | bytes 1572872 | tf_op jit(solution)/shard_map/ppermute | solution.py:78
  64.5 16.3 %collective-permute-start.14 = (bf16[2,32,4096]{2,1,0:T(8,128)(2,1)S(1)}, bf16[2,32,4096]{2,1,0:T(8,128)(2,1)S(1)}, u32[]{:S(2)}, u32[]{:S(2)}) collective-permute-start(bf16[2,32,4096]{2,1,0:T(8,128)(2,1)S(1)} %collective-permute-done.refs_4_), channel_id=1, source_target_pairs={{0,3},{1,0},{2,1},{3,2},{4,7},{5,4},{6,5},{7,6},{8,11},{9,8},{10,9... | collective-permute-start | bytes 1572872 | tf_op jit(solution)/shard_map/ppermute | solution.py:78
  67.2 9.5 %collective-permute-start.16 = (bf16[1,32,4096]{2,1,0:T(8,128)(2,1)S(1)}, bf16[1,32,4096]{2,1,0:T(8,128)(2,1)S(1)}, u32[]{:S(2)}, u32[]{:S(2)}) collective-permute-start(bf16[1,32,4096]{2,1,0:T(8,128)(2,1)S(1)} %slice.23), channel_id=1, source_target_pairs={{0,12},{1,13},{2,14},{3,15},{4,0},{5,1},{6,2},{7,3},{8,4},{9,5},{1... | collective-permute-start | bytes 786440 | tf_op jit(solution)/shard_map/ppermute | solution.py:78
  73.4 7.4 %collective-permute-start.15 = (bf16[1,32,4096]{2,1,0:T(8,128)(2,1)S(1)}, bf16[1,32,4096]{2,1,0:T(8,128)(2,1)S(1)}, u32[]{:S(2)}, u32[]{:S(2)}) collective-permute-start(bf16[1,32,4096]{2,1,0:T(8,128)(2,1)S(1)} %slice.23), channel_id=1, source_target_pairs={{0,4},{1,5},{2,6},{3,7},{4,8},{5,9},{6,10},{7,11},{8,12},{9,13},{1... | collective-permute-start | bytes 786440 | tf_op jit(solution)/shard_map/ppermute | solution.py:78
  80.8 8.4 %collective-permute-start.18 = (bf16[1,32,4096]{2,1,0:T(8,128)(2,1)S(1)}, bf16[1,32,4096]{2,1,0:T(8,128)(2,1)S(1)}, u32[]{:S(2)}, u32[]{:S(2)}) collective-permute-start(bf16[1,32,4096]{2,1,0:T(8,128)(2,1)S(1)} %slice.25), channel_id=1, source_target_pairs={{0,3},{1,0},{2,1},{3,2},{4,7},{5,4},{6,5},{7,6},{8,11},{9,8},{10,9... | collective-permute-start | bytes 786440 | tf_op jit(solution)/shard_map/ppermute | solution.py:78
  81.6 8.4 %collective-permute-start.17 = (bf16[1,32,4096]{2,1,0:T(8,128)(2,1)S(1)}, bf16[1,32,4096]{2,1,0:T(8,128)(2,1)S(1)}, u32[]{:S(2)}, u32[]{:S(2)}) collective-permute-start(bf16[1,32,4096]{2,1,0:T(8,128)(2,1)S(1)} %slice.24), channel_id=1, source_target_pairs={{0,1},{1,2},{2,3},{3,0},{4,5},{5,6},{6,7},{7,4},{8,9},{9,10},{10,1... | collective-permute-start | bytes 786440 | tf_op jit(solution)/shard_map/ppermute | solution.py:78
  90.0 3.4 %copy-start.2 = (bf16[2,512,4096]{2,1,0:T(8,128)(2,1)S(1)}, bf16[2,512,4096]{2,1,0:T(8,128)(2,1)}, u32[]{:S(2)}) copy-start(bf16[2,512,4096]{2,1,0:T(8,128)(2,1)} %refs_9_.1) | copy-start | bytes 25165828
where the time goes:
time: 122 us
  waiting for transfers between devices  40.6 us (33%)
  starting transfers between devices  35.1 us (29%)
  blocking collectives  25.5 us (21%)
  Pallas kernels  12.1 us (10%)
  local copies, waits for them, and re-layouts  7.92 us (6%)
    ppermute x19, waiting for transfers between devices, move(): lax.ppermute(value, 'ex', [(z * SIDE + x, to(z, x)) for z in range(SIDE)...  40.6 us
    ppermute x19, starting transfers between devices, move(): lax.ppermute(value, 'ex', [(z * SIDE + x, to(z, x)) for z in range(SIDE)...  35.1 us
    all_to_all x1, blocking collectives, local(): lax.all_to_all(parts, 'layer', split_axis=0, concat_axis=0, tiled=True)  25.5 us
    unnamed x8, local copies, waits for them, and re-layouts  7.81 us
    pallas_call x3, Pallas kernels, score_call(): pl.pallas_call(functools.partial(kernel, tuple((len(s) for s in shards)))...  7.21 us
    pallas_call x1, Pallas kernels, precondition(): pl.pallas_call(precondition_kernel, out_shape=jax.ShapeDtypeStruct(raw.sh...  4.86 us
  transfers between devices with their start and end apart: 19, of which 11 were waited for; matrix products, arithmetic and copies ran while one was open for 0% of the time, Pallas kernels for 4%

commit v1 on v0

--- a/solution.py
+++ b/solution.py
@@ -98,13 +98,16 @@
     )(first, second)
 
 
-def scores_of(shards, train, modules):
+def scores_of(shards, train, kept=None):
     total = None
-    for module in modules:
+    for module in range(train.shape[0]):
         for at in range(0, train.shape[2], TILE):
             part = pl.ds(at, TILE)
+            held = train[module, :, part]
+            if kept is not None:
+                kept[module, :, part] = held
             rows = jnp.concatenate([s[0][module, :, part] if len(s) == 1 else s[module][0, :, part] for s in shards], axis=0)
-            term = dot(train[module, :, part], rows, ((1,), (1,)))
+            term = dot(held, rows, ((1,), (1,)))
             total = term if total is None else total + term
     return total
 
@@ -113,9 +116,14 @@
     return total.T.astype(dtype).reshape((-1,) + shape)
 
 
+def keep_kernel(counts, *refs):
+    shards, (train, out, kept) = take(refs, counts)
+    out[...] = blocks_of(scores_of(shards, train, kept), out.shape[1:], out.dtype)
+
+
 def next_kernel(counts, *refs):
     shards, (train, out) = take(refs, counts)
-    out[...] = blocks_of(scores_of(shards, train, range(train.shape[0])), out.shape[1:], out.dtype)
+    out[...] = blocks_of(scores_of(shards, train), out.shape[1:], out.dtype)
 
 
 def last_kernel(counts, done_counts, offsets, me, *refs):
@@ -128,7 +136,7 @@
         for i in range(count):
             out[places[at]] = ref[i]
             at += 1
-    blocks = blocks_of(scores_of(shards, train, range(train.shape[0])), out.shape[1:], out.dtype)
+    blocks = blocks_of(scores_of(shards, train), out.shape[1:], out.dtype)
     for i in range(len(shards)):
         out[places[at + i]] = blocks[i]
 
@@ -141,76 +149,73 @@
     return shards, refs[at:]
 
 
-def score_call(kernel, shards, others, other_specs, out_shapes, scratch=(), lead=()):
+def score_call(kernel, shards, train, out_shapes, others=(), lead=()):
     shards = [s if isinstance(s, tuple) else (s,) for s in shards]
     flat = [half for s in shards for half in s]
     space = pl.BlockSpec(memory_space=pltpu.VMEM)
-    train = next(o for o in others if o.ndim == 3 and o.dtype == flat[0].dtype)
     rows = len(shards) * flat[0].shape[1]
     return pl.pallas_call(
         functools.partial(kernel, tuple(len(s) for s in shards)),
         out_shape=out_shapes,
-        in_specs=[pl.BlockSpec(memory_space=pltpu.SMEM)] * len(lead) + [space] * len(flat) + list(other_specs),
+        in_specs=[pl.BlockSpec(memory_space=pltpu.SMEM)] * len(lead) + [space] * (len(flat) + 1 + len(others)),
         out_specs=jax.tree.map(lambda _: space, out_shapes),
-        scratch_shapes=list(scratch),
         compiler_params=pltpu.CompilerParams(vmem_limit_bytes=16 << 20),
         cost_estimate=pl.CostEstimate(
             flops=2 * rows * train.size,
             bytes_accessed=2 * (train.size + rows * train.size // train.shape[1]),
             transcendentals=0,
         ),
-    )(*lead, *flat, *others)
+    )(*lead, *flat, train, *others)
+
+
+def blocks_shape(shards, train):
+    return jax.ShapeDtypeStruct((len(shards), shards[0].shape[1], train.shape[1]), jnp.bfloat16)
+
+
+def scores_keep(shards, train):
+    kept = jax.ShapeDtypeStruct(train.shape, train.dtype)
+    return score_call(keep_kernel, shards, train, [blocks_shape(shards, train), kept])
 
 
 def scores_next(shards, train):
-    shape = (len(shards), shards[0].shape[1], train.shape[1])
-    return score_call(
-        next_kernel, shards, [train], [pl.BlockSpec(memory_space=pltpu.VMEM)], jax.ShapeDtypeStruct(shape, jnp.bfloat16)
-    )
+    return score_call(next_kernel, shards, train, blocks_shape(shards, train))
 
 
 def scores_last(shards, train, done, offsets, me):
     counts = tuple(d.shape[0] for d in done)
     shape = (sum(counts) + len(shards),) + done[0].shape[1:]
     kernel = lambda own_counts, *refs: last_kernel(own_counts, counts, offsets, *refs)
-    space = pl.BlockSpec(memory_space=pltpu.VMEM)
-    return score_call(
-        kernel,
-        shards,
-        [train, *done],
-        [space] * (1 + len(done)),
-        jax.ShapeDtypeStruct(shape, jnp.bfloat16),
-        lead=[me],
-    )
+    return score_call(kernel, shards, train, jax.ShapeDtypeStruct(shape, jnp.bfloat16), done, [me])
 
 
 def local(query_grads, train_grads, basis_out, basis_in, eigen):
     me = lax.axis_index("ex").astype(jnp.int32).reshape(1)
     own = precondition(query_grads, basis_out, basis_in, eigen)
-    zl, zr = move(own, 1, 0), move(own, -1, 0)
-    xl, xr = move(own, 0, 1), move(own, 0, -1)
     x2 = move(own, 0, 2)
+    xr, xl = move(own, 0, -1), move(own, 0, 1)
+    zr, zl = move(own, -1, 0), move(own, 1, 0)
     zl, zr, xl, xr, x2 = in_order(zl, zr, xl, xr, x2)
+    zr_xr, zl_xl = move(zr, 0, -1), move(zl, 0, 1)
     z2 = (move(zl[:1], 1, 0), move(zr[1:], -1, 0))
-    zl_xl, zr_xr = move(zl, 0, 1), move(zr, 0, -1)
     first = scores_next([own, xl, xr, x2, zl, zr], train_grads)
     z2a, z2b, zl, zr, x2, zl_xl, zr_xr, first = in_order(*z2, zl, zr, x2, zl_xl, zr_xr, first)
     z2 = join(z2a, z2b)
-    zl_x2, zr_x2 = move(x2[:1], 1, 0), move(x2[:1], -1, 0)
+    zr_xl = move(zr, 0, 1)
     z2_xl, z2_xr = move(z2, 0, 1), move(z2, 0, -1)
-    z2_xl, z2_xr, zl, zr, x2, zl_x2, zr_x2 = in_order(z2_xl, z2_xr, zl, zr, x2, zl_x2, zr_x2)
-    zl_x2, zr_x2 = (zl_x2, move(x2[1:], 1, 0)), (zr_x2, move(x2[1:], -1, 0))
-    zr_xl, zl_xr = move(zr, 0, 1), move(zl, 0, -1)
-    second = scores_next([zl_xl, zr_xr, z2, z2_xl, z2_xr], train_grads)
-    z2_xl, z2_xr, second, zr_xl, zl_xr, *late = in_order(z2_xl, z2_xr, second, zr_xl, zl_xr, zl_x2[1], zr_x2[1])
-    zl_x2, zr_x2 = (zl_x2[0], late[0]), (zr_x2[0], late[1])
+    zr_x2, zl_x2 = move(x2, -1, 0), move(x2, 1, 0)
+    second = scores_next([zl_xl, zr_xr, z2], train_grads)
+    z2_xr, zl = in_order(z2_xr, zl)
+    zl_xr = move(zl, 0, -1)
+    z2_xl, z2_xr, zr_xl, zl_xr, zl_x2, zr_x2, second = in_order(z2_xl, z2_xr, zr_xl, zl_xr, zl_x2, zr_x2, second)
     z2_x2 = (move(z2_xl[:1], 0, 1), move(z2_xr[1:], 0, -1))
+    third, train = scores_keep([z2_xl, z2_xr, zr_xl, zl_xr, zl_x2, zr_x2], train_grads)
+    third, train, *z2_x2 = in_order(third, train, *z2_x2)
     offsets = [
         (0, 0), (0, -1), (0, 1), (0, 2), (-1, 0), (1, 0),
-        (-1, -1), (1, 1), (2, 0), (2, -1), (2, 1),
-        (-1, 2), (1, 2), (2, 2), (1, -1), (-1, 1),
+        (-1, -1), (1, 1), (2, 0),
+        (2, -1), (2, 1), (1, -1), (-1, 1), (-1, 2), (1, 2), (2, 2),
     ]
-    parts = scores_last([zl_x2, zr_x2, z2_x2, zr_xl, zl_xr], train_grads, (first, second), offsets, me)
+    parts = scores_last([tuple(z2_x2)], train, (first, second, third), offsets, me)
     parts = lax.all_to_all(parts, "layer", split_axis=0, concat_axis=0, tiled=True)
     return jnp.sum(parts.astype(jnp.float32), axis=0)
 

time: 122 us -> 114 us (0.934)
  blocking collectives: 25.5 us -> 16.2 us
  starting transfers between devices: 35.1 us -> 27.2 us
  waiting for transfers between devices: 40.6 us -> 45.1 us
  Pallas kernels: 12.1 us -> 15.6 us
  local copies, waits for them, and re-layouts: 7.92 us -> 9.27 us
    all_to_all x1, blocking collectives: 25.5 us -> 16.2 us  [local(): lax.all_to_all(parts, 'layer', split_axis=0, concat_axis=0, tiled=True)]
    ppermute x19 -> x17, starting transfers between devices: 35.1 us -> 27.2 us  [move(): lax.ppermute(value, 'ex', [(z * SIDE + x, to(z, x)) for z in range(SIDE)...]
    ppermute x19 -> x17, waiting for transfers between devices: 40.6 us -> 45.1 us  [move(): lax.ppermute(value, 'ex', [(z * SIDE + x, to(z, x)) for z in range(SIDE)...]
    pallas_call x3 -> x4, Pallas kernels: 7.21 us -> 10.7 us  [score_call(): pl.pallas_call(functools.partial(kernel, tuple((len(s) for s in shards)))...]
    slice x2, local copies, waits for them, and re-layouts: 0.04 us -> 1.43 us  [local(): z2_x2 = (move(z2_xl[:1], 0, 1), move(z2_xr[1:], 0, -1))]
    unnamed x8 -> x6, local copies, waits for them, and re-layouts: 7.81 us -> 7.8 us
  transfers between devices with their start and end apart: 19 -> 17, of which waited for: 11 -> 8; matrix products, arithmetic and copies ran while one was open for 0% -> 1% of each run, Pallas kernels for 4% -> 6%
where the time goes in v1:
time: 114 us
  waiting for transfers between devices  45.1 us (40%)
  starting transfers between devices  27.2 us (24%)
  blocking collectives  16.2 us (14%)
  Pallas kernels  15.6 us (14%)
  local copies, waits for them, and re-layouts  9.27 us (8%)
    ppermute x17, waiting for transfers between devices, move(): lax.ppermute(value, 'ex', [(z * SIDE + x, to(z, x)) for z in range(SIDE)...  45.1 us
    ppermute x17, starting transfers between devices, move(): lax.ppermute(value, 'ex', [(z * SIDE + x, to(z, x)) for z in range(SIDE)...  27.2 us
    all_to_all x1, blocking collectives, local(): lax.all_to_all(parts, 'layer', split_axis=0, concat_axis=0, tiled=True)  16.2 us
    pallas_call x4, Pallas kernels, score_call(): pl.pallas_call(functools.partial(kernel, tuple((len(s) for s in shards)))...  10.7 us
    unnamed x6, local copies, waits for them, and re-layouts  7.8 us
    pallas_call x1, Pallas kernels, precondition(): pl.pallas_call(precondition_kernel, out_shape=jax.ShapeDtypeStruct(raw.sh...  4.86 us
  transfers between devices with their start and end apart: 17, of which 8 were waited for; matrix products, arithmetic and copies ran while one was open for 1% of the time, Pallas kernels for 6%

profile of v1, /device:TPU:1, one launch (start us, length us, event | category | flops | bytes accessed | tf_op | source)
XLA Modules:
  0.0 114.1 jit_solution(3631419277857918022)
XLA Ops:
  0.0 4.9 %shard_map.55.refs_0_ = bf16[2,32,4096]{2,1,0:T(8,128)(2,1)} custom-call(bf16[2,32,4096]{2,1,0:T(8,128)(2,1)} %raw.1, f32[2,64,64]{2,1,0:T(8,128)} %basis_out.1, f32[2,64,64]{2,1,0:T(8,128)} %basis_in.1, f32[2,64,64]{2,1,0:T(8,128)} %eigen.1), custom_call_target="tpu_custom_call" | custom-call | tf_op jit(solution)/shard_map/pallas_call | solution.py:65
  4.9 3.8 %collective-permute-start = (bf16[2,32,4096]{2,1,0:T(8,128)(2,1)}, bf16[2,32,4096]{2,1,0:T(8,128)(2,1)S(1)}, u32[]{:S(2)}, u32[]{:S(2)}) collective-permute-start(bf16[2,32,4096]{2,1,0:T(8,128)(2,1)} %shard_map.55.refs_0_), channel_id=1, source_target_pairs={{0,4},{1,5},{2,6},{3,7},{4,8},{5,9},{6,10},{7,11},{8,12},{9,13},{1... | collective-permute-start | bytes 1572872 | tf_op jit(solution)/shard_map/ppermute | solution.py:78
  8.7 3.0 %collective-permute-start.1 = (bf16[2,32,4096]{2,1,0:T(8,128)(2,1)}, bf16[2,32,4096]{2,1,0:T(8,128)(2,1)S(1)}, u32[]{:S(2)}, u32[]{:S(2)}) collective-permute-start(bf16[2,32,4096]{2,1,0:T(8,128)(2,1)} %shard_map.55.refs_0_), channel_id=1, source_target_pairs={{0,12},{1,13},{2,14},{3,15},{4,0},{5,1},{6,2},{7,3},{8,4},{9,5},{1... | collective-permute-start | bytes 1572872 | tf_op jit(solution)/shard_map/ppermute | solution.py:78
  11.7 1.2 %collective-permute-start.2 = (bf16[2,32,4096]{2,1,0:T(8,128)(2,1)}, bf16[2,32,4096]{2,1,0:T(8,128)(2,1)S(1)}, u32[]{:S(2)}, u32[]{:S(2)}) collective-permute-start(bf16[2,32,4096]{2,1,0:T(8,128)(2,1)} %shard_map.55.refs_0_), channel_id=1, source_target_pairs={{0,1},{1,2},{2,3},{3,0},{4,5},{5,6},{6,7},{7,4},{8,9},{9,10},{10,1... | collective-permute-start | bytes 1572872 | tf_op jit(solution)/shard_map/ppermute | solution.py:78
  12.9 1.5 %collective-permute-start.3 = (bf16[2,32,4096]{2,1,0:T(8,128)(2,1)}, bf16[2,32,4096]{2,1,0:T(8,128)(2,1)S(1)}, u32[]{:S(2)}, u32[]{:S(2)}) collective-permute-start(bf16[2,32,4096]{2,1,0:T(8,128)(2,1)} %shard_map.55.refs_0_), channel_id=1, source_target_pairs={{0,3},{1,0},{2,1},{3,2},{4,7},{5,4},{6,5},{7,6},{8,11},{9,8},{10,9... | collective-permute-start | bytes 1572872 | tf_op jit(solution)/shard_map/ppermute | solution.py:78
  14.4 1.5 %collective-permute-start.4 = (bf16[2,32,4096]{2,1,0:T(8,128)(2,1)}, bf16[2,32,4096]{2,1,0:T(8,128)(2,1)S(1)}, u32[]{:S(2)}, u32[]{:S(2)}) collective-permute-start(bf16[2,32,4096]{2,1,0:T(8,128)(2,1)} %shard_map.55.refs_0_), channel_id=1, source_target_pairs={{0,2},{1,3},{2,0},{3,1},{4,6},{5,7},{6,4},{7,5},{8,10},{9,11},{10,... | collective-permute-start | bytes 1572872 | tf_op jit(solution)/shard_map/ppermute | solution.py:78
  15.9 11.8 %collective-permute-done.refs_4_ = bf16[2,32,4096]{2,1,0:T(8,128)(2,1)S(1)} collective-permute-done((bf16[2,32,4096]{2,1,0:T(8,128)(2,1)}, bf16[2,32,4096]{2,1,0:T(8,128)(2,1)S(1)}, u32[]{:S(2)}, u32[]{:S(2)}) %collective-permute-start) | collective-permute-done | bytes 524320 | tf_op jit(solution)/shard_map/ppermute | solution.py:78
  27.7 8.6 %collective-permute-done.1.refs_5_ = bf16[2,32,4096]{2,1,0:T(8,128)(2,1)S(1)} collective-permute-done((bf16[2,32,4096]{2,1,0:T(8,128)(2,1)}, bf16[2,32,4096]{2,1,0:T(8,128)(2,1)S(1)}, u32[]{:S(2)}, u32[]{:S(2)}) %collective-permute-start.1) | collective-permute-done | bytes 524320 | tf_op jit(solution)/shard_map/ppermute | solution.py:78
  36.3 1.5 %collective-permute-done.4.refs_3_ = bf16[2,32,4096]{2,1,0:T(8,128)(2,1)S(1)} collective-permute-done((bf16[2,32,4096]{2,1,0:T(8,128)(2,1)}, bf16[2,32,4096]{2,1,0:T(8,128)(2,1)S(1)}, u32[]{:S(2)}, u32[]{:S(2)}) %collective-permute-start.4) | collective-permute-done | bytes 524320 | tf_op jit(solution)/shard_map/ppermute | solution.py:78
  38.4 2.1 %collective-permute-start.8 = (bf16[2,32,4096]{2,1,0:T(8,128)(2,1)S(1)}, bf16[2,32,4096]{2,1,0:T(8,128)(2,1)S(1)}, u32[]{:S(2)}, u32[]{:S(2)}) collective-permute-start(bf16[2,32,4096]{2,1,0:T(8,128)(2,1)S(1)} %collective-permute-done.1.refs_5_), channel_id=1, source_target_pairs={{0,3},{1,0},{2,1},{3,2},{4,7},{5,4},{6,5},{7,6},{8,11},{9,8},{10,9... | collective-permute-start | bytes 1572872 | tf_op jit(solution)/shard_map/ppermute | solution.py:78
  40.5 1.5 %collective-permute-start.5 = (bf16[1,32,4096]{2,1,0:T(8,128)(2,1)S(1)}, bf16[1,32,4096]{2,1,0:T(8,128)(2,1)S(1)}, u32[]{:S(2)}, u32[]{:S(2)}) collective-permute-start(bf16[1,32,4096]{2,1,0:T(8,128)(2,1)S(1)} %slice.12), channel_id=1, source_target_pairs={{0,4},{1,5},{2,6},{3,7},{4,8},{5,9},{6,10},{7,11},{8,12},{9,13},{1... | collective-permute-start | bytes 786440 | tf_op jit(solution)/shard_map/ppermute | solution.py:78
  42.1 2.1 %collective-permute-start.6 = (bf16[1,32,4096]{2,1,0:T(8,128)(2,1)S(1)}, bf16[1,32,4096]{2,1,0:T(8,128)(2,1)S(1)}, u32[]{:S(2)}, u32[]{:S(2)}) collective-permute-start(bf16[1,32,4096]{2,1,0:T(8,128)(2,1)S(1)} %slice.13), channel_id=1, source_target_pairs={{0,12},{1,13},{2,14},{3,15},{4,0},{5,1},{6,2},{7,3},{8,4},{9,5},{1... | collective-permute-start | bytes 786440 | tf_op jit(solution)/shard_map/ppermute | solution.py:78
  44.2 3.4 %copy-done = bf16[2,512,4096]{2,1,0:T(8,128)(2,1)S(1)} copy-done((bf16[2,512,4096]{2,1,0:T(8,128)(2,1)S(1)}, bf16[2,512,4096]{2,1,0:T(8,128)(2,1)}, u32[]{:S(2)}) %copy-start) | copy-done | bytes 8388632
  47.6 1.0 copy-done.2
  48.6 2.4 %shard_map.56.refs_4_ = bf16[6,32,512]{2,1,0:T(8,128)(2,1)S(1)} custom-call(bf16[2,32,4096]{2,1,0:T(8,128)(2,1)S(1)} %copy-done.2, bf16[2,32,4096]{2,1,0:T(8,128)(2,1)S(1)} %collective-permute-done.2.refs_1_, bf16[2,32,4096]{2,1,0:T(8,128)(2,1)S(1)} %collective-permute-done.3.refs_2_, bf16[2,32,4096]{2,1,0:T(8,128)(2,1)S(1)} %collective-permute-done.4.refs_3_, ...), custom_call_target="tpu_custom_call" | custom-call | flops 1610612736 | bytes 11534336 | tf_op jit(solution)/shard_map/pallas_call | solution.py:157
  51.1 5.9 %collective-permute-done.6.second = bf16[1,32,4096]{2,1,0:T(8,128)(2,1)S(1)} collective-permute-done((bf16[1,32,4096]{2,1,0:T(8,128)(2,1)S(1)}, bf16[1,32,4096]{2,1,0:T(8,128)(2,1)S(1)}, u32[]{:S(2)}, u32[]{:S(2)}) %collective-permute-start.6) | collective-permute-done | bytes 262176 | tf_op jit(solution)/shard_map/ppermute | solution.py:78
  57.7 0.9 collective-permute-start.9
  58.5 1.5 %collective-permute-start.13 = (bf16[2,32,4096]{2,1,0:T(8,128)(2,1)S(1)}, bf16[2,32,4096]{2,1,0:T(8,128)(2,1)S(1)}, u32[]{:S(2)}, u32[]{:S(2)}) collective-permute-start(bf16[2,32,4096]{2,1,0:T(8,128)(2,1)S(1)} %collective-permute-done.4.refs_3_), channel_id=1, source_target_pairs={{0,4},{1,5},{2,6},{3,7},{4,8},{5,9},{6,10},{7,11},{8,12},{9,13},{1... | collective-permute-start | bytes 1572872 | tf_op jit(solution)/shard_map/ppermute | solution.py:78
  60.0 2.1 %collective-permute-start.14 = (bf16[2,32,4096]{2,1,0:T(8,128)(2,1)S(1)}, bf16[2,32,4096]{2,1,0:T(8,128)(2,1)S(1)}, u32[]{:S(2)}, u32[]{:S(2)}) collective-permute-start(bf16[2,32,4096]{2,1,0:T(8,128)(2,1)S(1)} %collective-permute-done.4.refs_3_), channel_id=1, source_target_pairs={{0,12},{1,13},{2,14},{3,15},{4,0},{5,1},{6,2},{7,3},{8,4},{9,5},{1... | collective-permute-start | bytes 1572872 | tf_op jit(solution)/shard_map/ppermute | solution.py:78
  62.1 7.4 %collective-permute-done.10.refs_1_ = bf16[2,32,4096]{2,1,0:T(8,128)(2,1)S(1)} collective-permute-done((bf16[2,32,4096]{2,1,0:T(8,128)(2,1)S(1)}, bf16[2,32,4096]{2,1,0:T(8,128)(2,1)S(1)}, u32[]{:S(2)}, u32[]{:S(2)}) %collective-permute-start.10) | collective-permute-done | bytes 524320 | tf_op jit(solution)/shard_map/ppermute | solution.py:78
  69.5 2.0 %collective-permute-start.12 = (bf16[2,32,4096]{2,1,0:T(8,128)(2,1)S(1)}, bf16[2,32,4096]{2,1,0:T(8,128)(2,1)S(1)}, u32[]{:S(2)}, u32[]{:S(2)}) collective-permute-start(bf16[2,32,4096]{2,1,0:T(8,128)(2,1)S(1)} %collective-permute-done.refs_4_), channel_id=1, source_target_pairs={{0,3},{1,0},{2,1},{3,2},{4,7},{5,4},{6,5},{7,6},{8,11},{9,8},{10,9... | collective-permute-start | bytes 1572872 | tf_op jit(solution)/shard_map/ppermute | solution.py:78
  71.5 2.4 %shard_map.58.refs_5_ = bf16[3,32,512]{2,1,0:T(8,128)(2,1)S(1)} custom-call(bf16[2,32,4096]{2,1,0:T(8,128)(2,1)S(1)} %collective-permute-done.7.refs_0_, bf16[2,32,4096]{2,1,0:T(8,128)(2,1)S(1)} %collective-permute-done.8.refs_1_, bf16[2,32,4096]{2,1,0:T(8,128)(2,1)S(1)} %shard_map.57.refs_2_, bf16[2,512,4096]{2,1,0:T(8,128)(2,1)S(1)} %copy-done), custom_call_target="tpu_custom_call" | custom-call | flops 805306368 | bytes 9961472 | tf_op jit(solution)/shard_map/pallas_call | solution.py:157
  73.9 8.5 %collective-permute-done.11.refs_2_ = bf16[2,32,4096]{2,1,0:T(8,128)(2,1)S(1)} collective-permute-done((bf16[2,32,4096]{2,1,0:T(8,128)(2,1)S(1)}, bf16[2,32,4096]{2,1,0:T(8,128)(2,1)S(1)}, u32[]{:S(2)}, u32[]{:S(2)}) %collective-permute-start.11) | collective-permute-done | bytes 524320 | tf_op jit(solution)/shard_map/ppermute | solution.py:78
  82.4 1.3 %collective-permute-done.13.refs_4_ = bf16[2,32,4096]{2,1,0:T(8,128)(2,1)S(1)} collective-permute-done((bf16[2,32,4096]{2,1,0:T(8,128)(2,1)S(1)}, bf16[2,32,4096]{2,1,0:T(8,128)(2,1)S(1)}, u32[]{:S(2)}, u32[]{:S(2)}) %collective-permute-start.13) | collective-permute-done | bytes 524320 | tf_op jit(solution)/shard_map/ppermute | solution.py:78
  83.8 0.7 slice.14
  84.5 0.7 slice.15
  85.2 2.7 %collective-permute-start.16 = (bf16[1,32,4096]{2,1,0:T(8,128)(2,1)}, bf16[1,32,4096]{2,1,0:T(8,128)(2,1)}, u32[]{:S(2)}, u32[]{:S(2)}) collective-permute-start(bf16[1,32,4096]{2,1,0:T(8,128)(2,1)} %slice.15), channel_id=1, source_target_pairs={{0,3},{1,0},{2,1},{3,2},{4,7},{5,4},{6,5},{7,6},{8,11},{9,8},{10,9... | collective-permute-start | bytes 786440 | tf_op jit(solution)/shard_map/ppermute | solution.py:78
  87.9 3.4 %copy-done.1 = bf16[2,512,4096]{2,1,0:T(8,128)(2,1)S(1)} copy-done((bf16[2,512,4096]{2,1,0:T(8,128)(2,1)S(1)}, bf16[2,512,4096]{2,1,0:T(8,128)(2,1)}, u32[]{:S(2)}) %copy-start.1) | copy-done | bytes 8388632
  91.2 2.5 %shard_map.59 = (bf16[6,32,512]{2,1,0:T(8,128)(2,1)S(1)}, bf16[2,512,4096]{2,1,0:T(8,128)(2,1)S(1)}) custom-call(bf16[2,32,4096]{2,1,0:T(8,128)(2,1)S(1)} %collective-permute-done.9.refs_0_, bf16[2,32,4096]{2,1,0:T(8,128)(2,1)S(1)} %collective-permute-done.10.refs_1_, bf16[2,32,4096]{2,1,0:T(8,128)(2,1)S(1)} %collective-permute-done.11.refs_2_, ...), custom_call_target="tpu_custom_call" | custom-call | flops 1610612736 | bytes 11534336 | tf_op jit(solution)/shard_map/pallas_call | solution.py:157
  93.8 3.4 %shard_map.60 = bf16[16,32,512]{2,1,0:T(8,128)(2,1)S(1)} custom-call(s32[1]{0:T(128)} %bitcast.refs_0_, bf16[1,32,4096]{2,1,0:T(8,128)(2,1)} %collective-permute-done.15.refs_1_, bf16[1,32,4096]{2,1,0:T(8,128)(2,1)} %collective-permute-done.16.refs_2_, bf16[2,512,4096]{2,1,0:T(8,128)(2,1)S(1)} %get-tuple-element.57.refs_3_, ...), custom_call_target="tpu_custom_call" | custom-call | flops 268435456 | bytes 8912896 | tf_op jit(solution)/shard_map/pallas_call | solution.py:157
  97.2 16.2 %all_to_all.5 = bf16[16,32,512]{2,1,0:T(8,128)(2,1)S(1)} all-to-all(bf16[16,32,512]{2,1,0:T(8,128)(2,1)S(1)} %shard_map.60), channel_id=1, replica_groups=mesh['layer'=16,'ex'=16] {'layer'}, dimensions={0} | all-to-all | bytes 1048576 | tf_op jit(solution)/shard_map/all_to_all | solution.py:219
  113.4 0.7 convert_reduce_fusion
  (20 shorter events, 1.4 us)
Async XLA Ops:
  4.9 22.8 %collective-permute-start = (bf16[2,32,4096]{2,1,0:T(8,128)(2,1)}, bf16[2,32,4096]{2,1,0:T(8,128)(2,1)S(1)}, u32[]{:S(2)}, u32[]{:S(2)}) collective-permute-start(bf16[2,32,4096]{2,1,0:T(8,128)(2,1)} %shard_map.55.refs_0_), channel_id=1, source_target_pairs={{0,4},{1,5},{2,6},{3,7},{4,8},{5,9},{6,10},{7,11},{8,12},{9,13},{1... | collective-permute-start | bytes 1572872 | tf_op jit(solution)/shard_map/ppermute | solution.py:78
  8.7 27.6 %collective-permute-start.1 = (bf16[2,32,4096]{2,1,0:T(8,128)(2,1)}, bf16[2,32,4096]{2,1,0:T(8,128)(2,1)S(1)}, u32[]{:S(2)}, u32[]{:S(2)}) collective-permute-start(bf16[2,32,4096]{2,1,0:T(8,128)(2,1)} %shard_map.55.refs_0_), channel_id=1, source_target_pairs={{0,12},{1,13},{2,14},{3,15},{4,0},{5,1},{6,2},{7,3},{8,4},{9,5},{1... | collective-permute-start | bytes 1572872 | tf_op jit(solution)/shard_map/ppermute | solution.py:78
  11.7 24.6 %collective-permute-start.2 = (bf16[2,32,4096]{2,1,0:T(8,128)(2,1)}, bf16[2,32,4096]{2,1,0:T(8,128)(2,1)S(1)}, u32[]{:S(2)}, u32[]{:S(2)}) collective-permute-start(bf16[2,32,4096]{2,1,0:T(8,128)(2,1)} %shard_map.55.refs_0_), channel_id=1, source_target_pairs={{0,1},{1,2},{2,3},{3,0},{4,5},{5,6},{6,7},{7,4},{8,9},{9,10},{10,1... | collective-permute-start | bytes 1572872 | tf_op jit(solution)/shard_map/ppermute | solution.py:78
  12.9 23.4 %collective-permute-start.3 = (bf16[2,32,4096]{2,1,0:T(8,128)(2,1)}, bf16[2,32,4096]{2,1,0:T(8,128)(2,1)S(1)}, u32[]{:S(2)}, u32[]{:S(2)}) collective-permute-start(bf16[2,32,4096]{2,1,0:T(8,128)(2,1)} %shard_map.55.refs_0_), channel_id=1, source_target_pairs={{0,3},{1,0},{2,1},{3,2},{4,7},{5,4},{6,5},{7,6},{8,11},{9,8},{10,9... | collective-permute-start | bytes 1572872 | tf_op jit(solution)/shard_map/ppermute | solution.py:78
  14.4 23.4 %collective-permute-start.4 = (bf16[2,32,4096]{2,1,0:T(8,128)(2,1)}, bf16[2,32,4096]{2,1,0:T(8,128)(2,1)S(1)}, u32[]{:S(2)}, u32[]{:S(2)}) collective-permute-start(bf16[2,32,4096]{2,1,0:T(8,128)(2,1)} %shard_map.55.refs_0_), channel_id=1, source_target_pairs={{0,2},{1,3},{2,0},{3,1},{4,6},{5,7},{6,4},{7,5},{8,10},{9,11},{10,... | collective-permute-start | bytes 1572872 | tf_op jit(solution)/shard_map/ppermute | solution.py:78
  37.8 19.1 %collective-permute-start.7 = (bf16[2,32,4096]{2,1,0:T(8,128)(2,1)S(1)}, bf16[2,32,4096]{2,1,0:T(8,128)(2,1)S(1)}, u32[]{:S(2)}, u32[]{:S(2)}) collective-permute-start(bf16[2,32,4096]{2,1,0:T(8,128)(2,1)S(1)} %collective-permute-done.refs_4_), channel_id=1, source_target_pairs={{0,1},{1,2},{2,3},{3,0},{4,5},{5,6},{6,7},{7,4},{8,9},{9,10},{10,1... | collective-permute-start | bytes 1572872 | tf_op jit(solution)/shard_map/ppermute | solution.py:78
  38.4 18.6 %collective-permute-start.8 = (bf16[2,32,4096]{2,1,0:T(8,128)(2,1)S(1)}, bf16[2,32,4096]{2,1,0:T(8,128)(2,1)S(1)}, u32[]{:S(2)}, u32[]{:S(2)}) collective-permute-start(bf16[2,32,4096]{2,1,0:T(8,128)(2,1)S(1)} %collective-permute-done.1.refs_5_), channel_id=1, source_target_pairs={{0,3},{1,0},{2,1},{3,2},{4,7},{5,4},{6,5},{7,6},{8,11},{9,8},{10,9... | collective-permute-start | bytes 1572872 | tf_op jit(solution)/shard_map/ppermute | solution.py:78
  40.5 10.5 %collective-permute-start.5 = (bf16[1,32,4096]{2,1,0:T(8,128)(2,1)S(1)}, bf16[1,32,4096]{2,1,0:T(8,128)(2,1)S(1)}, u32[]{:S(2)}, u32[]{:S(2)}) collective-permute-start(bf16[1,32,4096]{2,1,0:T(8,128)(2,1)S(1)} %slice.12), channel_id=1, source_target_pairs={{0,4},{1,5},{2,6},{3,7},{4,8},{5,9},{6,10},{7,11},{8,12},{9,13},{1... | collective-permute-start | bytes 786440 | tf_op jit(solution)/shard_map/ppermute | solution.py:78
  42.1 14.9 %collective-permute-start.6 = (bf16[1,32,4096]{2,1,0:T(8,128)(2,1)S(1)}, bf16[1,32,4096]{2,1,0:T(8,128)(2,1)S(1)}, u32[]{:S(2)}, u32[]{:S(2)}) collective-permute-start(bf16[1,32,4096]{2,1,0:T(8,128)(2,1)S(1)} %slice.13), channel_id=1, source_target_pairs={{0,12},{1,13},{2,14},{3,15},{4,0},{5,1},{6,2},{7,3},{8,4},{9,5},{1... | collective-permute-start | bytes 786440 | tf_op jit(solution)/shard_map/ppermute | solution.py:78
  44.2 3.4 %copy-start = (bf16[2,512,4096]{2,1,0:T(8,128)(2,1)S(1)}, bf16[2,512,4096]{2,1,0:T(8,128)(2,1)}, u32[]{:S(2)}) copy-start(bf16[2,512,4096]{2,1,0:T(8,128)(2,1)} %refs_6_.3) | copy-start | bytes 25165828
  47.6 1.0 copy-start.2
  57.0 12.5 %collective-permute-start.10 = (bf16[2,32,4096]{2,1,0:T(8,128)(2,1)S(1)}, bf16[2,32,4096]{2,1,0:T(8,128)(2,1)S(1)}, u32[]{:S(2)}, u32[]{:S(2)}) collective-permute-start(bf16[2,32,4096]{2,1,0:T(8,128)(2,1)S(1)} %shard_map.57.refs_2_), channel_id=1, source_target_pairs={{0,3},{1,0},{2,1},{3,2},{4,7},{5,4},{6,5},{7,6},{8,11},{9,8},{10,9... | collective-permute-start | bytes 1572872 | tf_op jit(solution)/shard_map/ppermute | solution.py:78
  57.7 16.2 %collective-permute-start.9 = (bf16[2,32,4096]{2,1,0:T(8,128)(2,1)S(1)}, bf16[2,32,4096]{2,1,0:T(8,128)(2,1)S(1)}, u32[]{:S(2)}, u32[]{:S(2)}) collective-permute-start(bf16[2,32,4096]{2,1,0:T(8,128)(2,1)S(1)} %shard_map.57.refs_2_), channel_id=1, source_target_pairs={{0,1},{1,2},{2,3},{3,0},{4,5},{5,6},{6,7},{7,4},{8,9},{9,10},{10,1... | collective-permute-start | bytes 1572872 | tf_op jit(solution)/shard_map/ppermute | solution.py:78
  58.5 25.1 %collective-permute-start.13 = (bf16[2,32,4096]{2,1,0:T(8,128)(2,1)S(1)}, bf16[2,32,4096]{2,1,0:T(8,128)(2,1)S(1)}, u32[]{:S(2)}, u32[]{:S(2)}) collective-permute-start(bf16[2,32,4096]{2,1,0:T(8,128)(2,1)S(1)} %collective-permute-done.4.refs_3_), channel_id=1, source_target_pairs={{0,4},{1,5},{2,6},{3,7},{4,8},{5,9},{6,10},{7,11},{8,12},{9,13},{1... | collective-permute-start | bytes 1572872 | tf_op jit(solution)/shard_map/ppermute | solution.py:78
  60.0 23.7 %collective-permute-start.14 = (bf16[2,32,4096]{2,1,0:T(8,128)(2,1)S(1)}, bf16[2,32,4096]{2,1,0:T(8,128)(2,1)S(1)}, u32[]{:S(2)}, u32[]{:S(2)}) collective-permute-start(bf16[2,32,4096]{2,1,0:T(8,128)(2,1)S(1)} %collective-permute-done.4.refs_3_), channel_id=1, source_target_pairs={{0,12},{1,13},{2,14},{3,15},{4,0},{5,1},{6,2},{7,3},{8,4},{9,5},{1... | collective-permute-start | bytes 1572872 | tf_op jit(solution)/shard_map/ppermute | solution.py:78
  62.1 20.3 %collective-permute-start.11 = (bf16[2,32,4096]{2,1,0:T(8,128)(2,1)S(1)}, bf16[2,32,4096]{2,1,0:T(8,128)(2,1)S(1)}, u32[]{:S(2)}, u32[]{:S(2)}) collective-permute-start(bf16[2,32,4096]{2,1,0:T(8,128)(2,1)S(1)} %collective-permute-done.1.refs_5_), channel_id=1, source_target_pairs={{0,1},{1,2},{2,3},{3,0},{4,5},{5,6},{6,7},{7,4},{8,9},{9,10},{10,1... | collective-permute-start | bytes 1572872 | tf_op jit(solution)/shard_map/ppermute | solution.py:78
  69.5 14.3 %collective-permute-start.12 = (bf16[2,32,4096]{2,1,0:T(8,128)(2,1)S(1)}, bf16[2,32,4096]{2,1,0:T(8,128)(2,1)S(1)}, u32[]{:S(2)}, u32[]{:S(2)}) collective-permute-start(bf16[2,32,4096]{2,1,0:T(8,128)(2,1)S(1)} %collective-permute-done.refs_4_), channel_id=1, source_target_pairs={{0,3},{1,0},{2,1},{3,2},{4,7},{5,4},{6,5},{7,6},{8,11},{9,8},{10,9... | collective-permute-start | bytes 1572872 | tf_op jit(solution)/shard_map/ppermute | solution.py:78
  84.5 9.3 %collective-permute-start.15 = (bf16[1,32,4096]{2,1,0:T(8,128)(2,1)}, bf16[1,32,4096]{2,1,0:T(8,128)(2,1)}, u32[]{:S(2)}, u32[]{:S(2)}) collective-permute-start(bf16[1,32,4096]{2,1,0:T(8,128)(2,1)} %slice.14), channel_id=1, source_target_pairs={{0,1},{1,2},{2,3},{3,0},{4,5},{5,6},{6,7},{7,4},{8,9},{9,10},{10,1... | collective-permute-start | bytes 786440 | tf_op jit(solution)/shard_map/ppermute | solution.py:78
  85.2 8.6 %collective-permute-start.16 = (bf16[1,32,4096]{2,1,0:T(8,128)(2,1)}, bf16[1,32,4096]{2,1,0:T(8,128)(2,1)}, u32[]{:S(2)}, u32[]{:S(2)}) collective-permute-start(bf16[1,32,4096]{2,1,0:T(8,128)(2,1)} %slice.15), channel_id=1, source_target_pairs={{0,3},{1,0},{2,1},{3,2},{4,7},{5,4},{6,5},{7,6},{8,11},{9,8},{10,9... | collective-permute-start | bytes 786440 | tf_op jit(solution)/shard_map/ppermute | solution.py:78
  87.9 3.4 %copy-start.1 = (bf16[2,512,4096]{2,1,0:T(8,128)(2,1)S(1)}, bf16[2,512,4096]{2,1,0:T(8,128)(2,1)}, u32[]{:S(2)}) copy-start(bf16[2,512,4096]{2,1,0:T(8,128)(2,1)} %refs_6_.3) | copy-start | bytes 25165828

commit v2 on v1

v2 whole, which is shorter than its diff:
```python
import functools

import jax
import jax.numpy as jnp
from jax import lax
from jax.experimental import pallas as pl
from jax.experimental.pallas import tpu as pltpu
from jax.sharding import PartitionSpec as P

SIDE = 4
TILE = 2048

def split(v):
    hi = v.astype(jnp.bfloat16)
    return hi, (v - hi.astype(jnp.float32)).astype(jnp.bfloat16)

def twice(block):
    none = jnp.zeros_like(block)
    return jnp.concatenate([jnp.concatenate([block, none], axis=1), jnp.concatenate([none, block], axis=1)], axis=0)

def dot(a, b, dims=((1,), (0,))):
    return lax.dot_general(a, b, (dims, ((), ())), preferred_element_type=jnp.float32)

def precondition_kernel(raw, basis_out, basis_in, eigen, out, work):
    count_q, entries = raw.shape[1:]
    side = basis_out.shape[1]
    half = count_q // 2
    low = lax.broadcasted_iota(jnp.int32, (half, 2 * side), 1) < side

    out_hi, out_lo = split(basis_out[0])
    turned_hi, turned_lo = split(basis_out[0].T)
    in_hi, in_lo = split(twice(basis_in[0]))
    damped = eigen[0] + 0.1 * jnp.mean(eigen[0])
    inverse = 1.0 / damped
    inverse = jnp.concatenate([inverse, inverse], axis=1)

    rows = []
    for pair in range(side // 2):
        tile = raw[0, :, pl.ds(pair * 2 * side, 2 * side)].astype(jnp.float32)
        top, bottom = tile[:half], tile[half:]
        rows.append(jnp.where(low, top, pltpu.roll(bottom, side, 1)))
        rows.append(jnp.where(low, pltpu.roll(top, side, 1), bottom))
    grads = jnp.concatenate(rows, axis=0).astype(jnp.bfloat16)
    work[...] = dot(jnp.concatenate([grads, grads], axis=1), jnp.concatenate([in_hi, in_lo], axis=0))
    left = jnp.concatenate([work[pl.ds(q, side, stride=half), :] for q in range(half)], axis=1)
    hi, lo = split(left)
    rotated = dot(jnp.concatenate([turned_hi, turned_hi, turned_lo], axis=1), jnp.concatenate([hi, lo, hi], axis=0))
    scaled = jnp.concatenate([rotated[:, q * 2 * side : (q + 1) * 2 * side] * inverse for q in range(half)], axis=1)
    hi, lo = split(scaled)
    back = dot(jnp.concatenate([out_hi, out_hi, out_lo], axis=1), jnp.concatenate([hi, lo, hi], axis=0))
    back = jnp.concatenate([back[:, q * 2 * side : (q + 1) * 2 * side] for q in range(half)], axis=0)
    hi, lo = split(back)
    nt = ((1,), (1,))
    work[...] = dot(jnp.concatenate([hi, lo], axis=1), jnp.concatenate([in_hi, in_hi], axis=1), nt) + dot(hi, in_lo, nt)
    for pair in range(side // 2):
        even, odd = work[pl.ds(2 * pair, half, stride=side), :], work[pl.ds(2 * pair + 1, half, stride=side), :]
        at = pl.ds(pair * 2 * side, 2 * side)
        out[0, :half, at] = jnp.where(low, even, pltpu.roll(odd, side, 1)).astype(out.dtype)
        out[0, half:, at] = jnp.where(low, pltpu.roll(even, side, 1), odd).astype(out.dtype)

def precondition(raw, basis_out, basis_in, eigen):
    modules, count_q, entries = raw.shape
    side = basis_out.shape[1]
    per_module = lambda *shape: pl.BlockSpec((1,) + shape, lambda m: (m, 0, 0))
    return pl.pallas_call(
        precondition_kernel,
        out_shape=jax.ShapeDtypeStruct(raw.shape, jnp.bfloat16),
        grid=(modules,),
        in_specs=[per_module(count_q, entries)] + [per_module(side, side)] * 3,
        out_specs=per_module(count_q, entries),
        scratch_shapes=[pltpu.VMEM((side * count_q // 2, 2 * side), jnp.float32)],
        compiler_params=pltpu.CompilerParams(vmem_limit_bytes=56 << 20),
    )(raw, basis_out, basis_in, eigen)


def move(value, step_z, step_x):
    to = lambda z, x: (z + step_z) % SIDE * SIDE + (x + step_x) % SIDE
    return lax.ppermute(value, "ex", [(z * SIDE + x, to(z, x)) for z in range(SIDE) for x in range(SIDE)])


def in_order(*values):
    return lax.optimization_barrier(values)


def arrange(values, plan):
    def kernel(*refs):
        given, made = refs[: len(values)], refs[len(values) :]
        for out, parts in zip(made, plan):
            for at, (value, module) in enumerate(parts):
                out[at] = given[value][module]

    space = pl.BlockSpec(memory_space=pltpu.VMEM)
    return pl.pallas_call(
        kernel,
        out_shape=[jax.ShapeDtypeStruct((len(parts),) + values[0].shape[1:], values[0].dtype) for parts in plan],
        in_specs=[space] * len(values),
        out_specs=[space] * len(plan),
        compiler_params=pltpu.CompilerParams(vmem_limit_bytes=4 << 20),
        cost_estimate=pl.CostEstimate(
            flops=0, bytes_accessed=4 * values[0][0].size * sum(len(parts) for parts in plan), transcendentals=0
        ),
    )(*values)


def blocks_of(shards, held, train, dtype, kept=None):
    total = None
    for module in range(train.shape[0]):
        for at in range(0, train.shape[2], TILE):
            part = pl.ds(at, TILE)
            stored = train[module, :, part]
            if kept is not None:
                kept[module, :, part] = stored
            rows = jnp.concatenate([held[s[module][0]][s[module][1], :, part] for s in shards], axis=0)
            term = dot(stored, rows, ((1,), (1,)))
            total = term if total is None else total + term
    return total.T.astype(dtype).reshape(len(shards), -1, train.shape[1])


def places_of(me, offsets):
    z, x = lax.shift_right_logical(me[0], 2), me[0] & (SIDE - 1)
    return [((z + dz) & (SIDE - 1)) * SIDE + ((x + dx) & (SIDE - 1)) for dz, dx in offsets]


def next_kernel(shards, count, *refs):
    held, (train, out) = refs[:count], refs[count:]
    out[...] = blocks_of(shards, held, train, out.dtype)


def place_kernel(shards, count, offsets, me, *refs):
    held, train, done, (out, kept) = refs[:count], refs[count], refs[count + 1 : -2], refs[-2:]
    places = places_of(me, offsets)
    at = 0
    for ref in done:
        for i in range(ref.shape[0]):
            out[places[at]] = ref[i]
            at += 1
    blocks = blocks_of(shards, held, train, out.dtype, kept)
    for i in range(len(shards)):
        out[places[at + i]] = blocks[i]


def last_kernel(shards, count, offsets, me, *refs):
    held, (train, _, out) = refs[:count], refs[count:]
    blocks = blocks_of(shards, held, train, out.dtype)
    for i, place in enumerate(places_of(me, offsets)):
        out[place] = blocks[i]


def score_call(kernel, shards, train, out_shapes, others=(), lead=(), aliases=None):
    arrays = []
    for array in (array for shard in shards for array, _ in shard):
        if all(array is not a for a in arrays):
            arrays.append(array)
    number = lambda array: next(i for i, a in enumerate(arrays) if a is array)
    shards = [[(number(array), at) for array, at in shard] for shard in shards]
    space = pl.BlockSpec(memory_space=pltpu.VMEM)
    rows = len(shards) * arrays[0].shape[1]
    return pl.pallas_call(
        functools.partial(kernel, shards, len(arrays)),
        out_shape=out_shapes,
        in_specs=[pl.BlockSpec(memory_space=pltpu.SMEM)] * len(lead) + [space] * (len(arrays) + 1 + len(others)),
        out_specs=jax.tree.map(lambda _: space, out_shapes),
        input_output_aliases={len(lead) + len(arrays) + 1: 0} if aliases else {},
        compiler_params=pltpu.CompilerParams(vmem_limit_bytes=16 << 20),
        cost_estimate=pl.CostEstimate(
            flops=2 * rows * train.size,
            bytes_accessed=2 * (train.size + rows * train.size // train.shape[1]),
            transcendentals=0,
        ),
    )(*lead, *arrays, train, *others)


def shard(array, at=0):
    return [(array, at), (array, at + 1)]


def blocks_shape(count, train, queries):
    return jax.ShapeDtypeStruct((count, queries, train.shape[1]), jnp.bfloat16)


def local(query_grads, train_grads, basis_out, basis_in, eigen):
    me = lax.axis_index("ex").astype(jnp.int32).reshape(1)
    queries = query_grads.shape[1]
    own = precondition(query_grads, basis_out, basis_in, eigen)
    xr, xl = move(own, 0, -1), move(own, 0, 1)
    zr, zl = move(own, -1, 0), move(own, 1, 0)
    halves = arrange([xl, xr], [[(0, 0)], [(1, 1)]])
    x2 = move(halves[1], 0, -1), move(halves[0], 0, 1)
    zl, zr, x2b, x2a = in_order(zl, zr, *x2)
    plan = [[(0, 0)], [(1, 1)], [(0, 0), (0, 1), (1, 0), (1, 1)], [(2, 0), (3, 0)]]
    zl_half, zr_half, both, x2 = arrange([zl, zr, x2a, x2b], plan)
    both_xr, both_xl = move(both, 0, -1), move(both, 0, 1)
    z2b, z2a = move(zr_half, -1, 0), move(zl_half, 1, 0)
    shards = [shard(own), shard(xl), shard(xr), shard(x2), shard(both, 0), shard(both, 2)]
    first = score_call(next_kernel, shards, train_grads, blocks_shape(6, train_grads, queries))
    z2a, z2b, x2, first = in_order(z2a, z2b, x2, first)
    (z2,) = arrange([z2a, z2b], [[(0, 0), (1, 0)]])
    z2_xl = move(z2, 0, 1)
    zr_x2, zl_x2 = move(x2, -1, 0), move(x2, 1, 0)
    z2, both_xr = in_order(z2, both_xr)
    z2_xr = move(z2, 0, -1)
    shards = [shard(z2), shard(both_xr, 0), shard(both_xr, 2)]
    second = score_call(next_kernel, shards, train_grads, blocks_shape(3, train_grads, queries))
    z2_xl, z2_xr, both_xl, zl_x2, zr_x2, second = in_order(z2_xl, z2_xr, both_xl, zl_x2, zr_x2, second)
    halves = arrange([z2_xl, z2_xr], [[(0, 0)], [(1, 1)]])
    z2_x2 = move(halves[0], 0, 1), move(halves[1], 0, -1)
    offsets = [
        (0, 0), (0, -1), (0, 1), (0, 2), (-1, 0), (1, 0),
        (2, 0), (-1, 1), (1, 1),
        (2, -1), (2, 1), (-1, -1), (1, -1), (-1, 2), (1, 2),
        (2, 2),
    ]
    shards = [shard(z2_xl), shard(z2_xr), shard(both_xl, 0), shard(both_xl, 2), shard(zl_x2), shard(zr_x2)]
    shapes = [blocks_shape(SIDE * SIDE, train_grads, queries), jax.ShapeDtypeStruct(train_grads.shape, train_grads.dtype)]
    kernel = lambda own, count, *refs: place_kernel(own, count, offsets[:-1], *refs)
    parts, train = score_call(kernel, shards, train_grads, shapes, [first, second], [me])
    parts, train, *z2_x2 = in_order(parts, train, *z2_x2)
    kernel = lambda own, count, *refs: last_kernel(own, count, offsets[-1:], *refs)
    shards = [[(half, 0) for half in z2_x2]]
    parts = score_call(kernel, shards, train, shapes[0], [parts], [me], True)
    parts = lax.all_to_all(parts, "layer", split_axis=0, concat_axis=0, tiled=True)
    return jnp.sum(parts.astype(jnp.float32), axis=0)


def solution(mesh):
    in_specs = (
        P("layer", "ex", None),
        P("layer", "ex", None),
        P("layer", None, None),
        P("layer", None, None),
        P("layer", None, None),
    )
    out_specs = P("layer", "ex")
    return jax.shard_map(local, mesh=mesh, in_specs=in_specs, out_specs=out_specs, check_vma=False)
```

time: 114 us -> 110 us (0.965)
  starting transfers between devices: 27.2 us -> 25.4 us
  waiting for transfers between devices: 45.1 us -> 43.6 us
  local copies, waits for them, and re-layouts: 9.27 us -> 7.81 us
    ppermute x17 -> x16, starting transfers between devices: 27.2 us -> 25.4 us  [move(): lax.ppermute(value, 'ex', [(z * SIDE + x, to(z, x)) for z in range(SIDE)...]
    slice x4 -> x0, local copies, waits for them, and re-layouts: 1.47 us -> none  [the longest x2 1.43 us: local(): z2_x2 = (move(z2_xl[:1], 0, 1), move(z2_xr[1:], 0, -1))]
    ppermute x17 -> x16, waiting for transfers between devices: 45.1 us -> 43.6 us  [move(): lax.ppermute(value, 'ex', [(z * SIDE + x, to(z, x)) for z in range(SIDE)...]
    pallas_call x5 -> x8, Pallas kernels: 10.7 us -> 11.7 us  [the longest x4 10.7 us: score_call(): pl.pallas_call(functools.partial(kernel, shards, len(arrays)), out_shape=...]
    unnamed x6 -> x8, local copies, waits for them, and re-layouts: 7.8 us -> 7.81 us
  transfers between devices with their start and end apart: 17 -> 16, of which waited for: 8 -> 10; matrix products, arithmetic and copies ran while one was open for 1% -> 0% of each run, Pallas kernels for 6% -> 7%
where the time goes in v2:
time: 110 us
  waiting for transfers between devices  43.6 us (40%)
  starting transfers between devices  25.4 us (23%)
  Pallas kernels  16.6 us (15%)
  blocking collectives  15.4 us (14%)
  local copies, waits for them, and re-layouts  7.81 us (7%)
    ppermute x16, waiting for transfers between devices, move(): lax.ppermute(value, 'ex', [(z * SIDE + x, to(z, x)) for z in range(SIDE)...  43.6 us
    ppermute x16, starting transfers between devices, move(): lax.ppermute(value, 'ex', [(z * SIDE + x, to(z, x)) for z in range(SIDE)...  25.4 us
    all_to_all x1, blocking collectives, local(): lax.all_to_all(parts, 'layer', split_axis=0, concat_axis=0, tiled=True)  15.4 us
    pallas_call x4, Pallas kernels, score_call(): pl.pallas_call(functools.partial(kernel, shards, len(arrays)), out_shape=...  10.7 us
    unnamed x8, local copies, waits for them, and re-layouts  7.81 us
    pallas_call x1, Pallas kernels, precondition(): pl.pallas_call(precondition_kernel, out_shape=jax.ShapeDtypeStruct(raw.sh...  4.85 us
  transfers between devices with their start and end apart: 16, of which 10 were waited for; matrix products, arithmetic and copies ran while one was open for 0% of the time, Pallas kernels for 7%

profile of v2, /device:TPU:1, one launch (start us, length us, event | category | flops | bytes accessed | tf_op | source)
XLA Modules:
  0.0 109.6 jit_solution(1194362042818120358)
XLA Ops:
  0.0 4.9 %shard_map.55.refs_0_ = bf16[2,32,4096]{2,1,0:T(8,128)(2,1)} custom-call(bf16[2,32,4096]{2,1,0:T(8,128)(2,1)} %raw.1, f32[2,64,64]{2,1,0:T(8,128)} %basis_out.1, f32[2,64,64]{2,1,0:T(8,128)} %basis_in.1, f32[2,64,64]{2,1,0:T(8,128)} %eigen.1), custom_call_target="tpu_custom_call" | custom-call | tf_op jit(solution)/shard_map/pallas_call | solution.py:65
  4.9 2.0 %collective-permute-start.2 = (bf16[2,32,4096]{2,1,0:T(8,128)(2,1)}, bf16[2,32,4096]{2,1,0:T(8,128)(2,1)S(1)}, u32[]{:S(2)}, u32[]{:S(2)}) collective-permute-start(bf16[2,32,4096]{2,1,0:T(8,128)(2,1)} %shard_map.55.refs_0_), channel_id=1, source_target_pairs={{0,1},{1,2},{2,3},{3,0},{4,5},{5,6},{6,7},{7,4},{8,9},{9,10},{10,1... | collective-permute-start | bytes 1572872 | tf_op jit(solution)/shard_map/ppermute | solution.py:78
  6.9 1.3 %collective-permute-start.3 = (bf16[2,32,4096]{2,1,0:T(8,128)(2,1)}, bf16[2,32,4096]{2,1,0:T(8,128)(2,1)S(1)}, u32[]{:S(2)}, u32[]{:S(2)}) collective-permute-start(bf16[2,32,4096]{2,1,0:T(8,128)(2,1)} %shard_map.55.refs_0_), channel_id=1, source_target_pairs={{0,3},{1,0},{2,1},{3,2},{4,7},{5,4},{6,5},{7,6},{8,11},{9,8},{10,9... | collective-permute-start | bytes 1572872 | tf_op jit(solution)/shard_map/ppermute | solution.py:78
  8.2 3.2 %collective-permute-start = (bf16[2,32,4096]{2,1,0:T(8,128)(2,1)}, bf16[2,32,4096]{2,1,0:T(8,128)(2,1)S(1)}, u32[]{:S(2)}, u32[]{:S(2)}) collective-permute-start(bf16[2,32,4096]{2,1,0:T(8,128)(2,1)} %shard_map.55.refs_0_), channel_id=1, source_target_pairs={{0,4},{1,5},{2,6},{3,7},{4,8},{5,9},{6,10},{7,11},{8,12},{9,13},{1... | collective-permute-start | bytes 1572872 | tf_op jit(solution)/shard_map/ppermute | solution.py:78
  11.4 3.0 %collective-permute-start.1 = (bf16[2,32,4096]{2,1,0:T(8,128)(2,1)}, bf16[2,32,4096]{2,1,0:T(8,128)(2,1)S(1)}, u32[]{:S(2)}, u32[]{:S(2)}) collective-permute-start(bf16[2,32,4096]{2,1,0:T(8,128)(2,1)} %shard_map.55.refs_0_), channel_id=1, source_target_pairs={{0,12},{1,13},{2,14},{3,15},{4,0},{5,1},{6,2},{7,3},{8,4},{9,5},{1... | collective-permute-start | bytes 1572872 | tf_op jit(solution)/shard_map/ppermute | solution.py:78
  14.4 3.3 %collective-permute-done.2.refs_0_.refs_1_ = bf16[2,32,4096]{2,1,0:T(8,128)(2,1)S(1)} collective-permute-done((bf16[2,32,4096]{2,1,0:T(8,128)(2,1)}, bf16[2,32,4096]{2,1,0:T(8,128)(2,1)S(1)}, u32[]{:S(2)}, u32[]{:S(2)}) %collective-permute-start.2) | collective-permute-done | bytes 524320 | tf_op jit(solution)/shard_map/ppermute | solution.py:78
  17.7 1.6 %collective-permute-done.3.refs_1_.refs_2_ = bf16[2,32,4096]{2,1,0:T(8,128)(2,1)S(1)} collective-permute-done((bf16[2,32,4096]{2,1,0:T(8,128)(2,1)}, bf16[2,32,4096]{2,1,0:T(8,128)(2,1)S(1)}, u32[]{:S(2)}, u32[]{:S(2)}) %collective-permute-start.3) | collective-permute-done | bytes 524320 | tf_op jit(solution)/shard_map/ppermute | solution.py:78
  19.4 1.9 %collective-permute-start.4 = (bf16[1,32,4096]{2,1,0:T(8,128)(2,1)S(1)}, bf16[1,32,4096]{2,1,0:T(8,128)(2,1)S(1)}, u32[]{:S(2)}, u32[]{:S(2)}) collective-permute-start(bf16[1,32,4096]{2,1,0:T(8,128)(2,1)S(1)} %get-tuple-element.35), channel_id=1, source_target_pairs={{0,3},{1,0},{2,1},{3,2},{4,7},{5,4},{6,5},{7,6},{8,11},{9,8},{10,9... | collective-permute-start | bytes 786440 | tf_op jit(solution)/shard_map/ppermute | solution.py:78
  21.3 7.8 %collective-permute-done.refs_0_ = bf16[2,32,4096]{2,1,0:T(8,128)(2,1)S(1)} collective-permute-done((bf16[2,32,4096]{2,1,0:T(8,128)(2,1)}, bf16[2,32,4096]{2,1,0:T(8,128)(2,1)S(1)}, u32[]{:S(2)}, u32[]{:S(2)}) %collective-permute-start) | collective-permute-done | bytes 524320 | tf_op jit(solution)/shard_map/ppermute | solution.py:78
  29.1 9.8 %collective-permute-done.1.refs_1_ = bf16[2,32,4096]{2,1,0:T(8,128)(2,1)S(1)} collective-permute-done((bf16[2,32,4096]{2,1,0:T(8,128)(2,1)}, bf16[2,32,4096]{2,1,0:T(8,128)(2,1)S(1)}, u32[]{:S(2)}, u32[]{:S(2)}) %collective-permute-start.1) | collective-permute-done | bytes 524320 | tf_op jit(solution)/shard_map/ppermute | solution.py:78
  39.0 1.3 %collective-permute-start.9 = (bf16[4,32,4096]{2,1,0:T(8,128)(2,1)S(1)}, bf16[4,32,4096]{2,1,0:T(8,128)(2,1)S(1)}, u32[]{:S(2)}, u32[]{:S(2)}) collective-permute-start(bf16[4,32,4096]{2,1,0:T(8,128)(2,1)S(1)} %get-tuple-element.44.refs_4_), channel_id=1, source_target_pairs={{0,3},{1,0},{2,1},{3,2},{4,7},{5,4},{6,5},{7,6},{8,11},{9,8},{10,9... | collective-permute-start | bytes 3145736 | tf_op jit(solution)/shard_map/ppermute | solution.py:78
  40.6 2.9 %collective-permute-start.6 = (bf16[1,32,4096]{2,1,0:T(8,128)(2,1)S(1)}, bf16[1,32,4096]{2,1,0:T(8,128)(2,1)S(1)}, u32[]{:S(2)}, u32[]{:S(2)}) collective-permute-start(bf16[1,32,4096]{2,1,0:T(8,128)(2,1)S(1)} %get-tuple-element.41), channel_id=1, source_target_pairs={{0,4},{1,5},{2,6},{3,7},{4,8},{5,9},{6,10},{7,11},{8,12},{9,13},{1... | collective-permute-start | bytes 786440 | tf_op jit(solution)/shard_map/ppermute | solution.py:78
  43.5 0.7 collective-permute-start.7
  44.2 3.4 %copy-done = bf16[2,512,4096]{2,1,0:T(8,128)(2,1)S(1)} copy-done((bf16[2,512,4096]{2,1,0:T(8,128)(2,1)S(1)}, bf16[2,512,4096]{2,1,0:T(8,128)(2,1)}, u32[]{:S(2)}) %copy-start) | copy-done | bytes 8388632
  47.5 1.0 copy-done.3
  48.6 2.4 %shard_map.58.refs_7_ = bf16[6,32,512]{2,1,0:T(8,128)(2,1)S(1)} custom-call(bf16[2,32,4096]{2,1,0:T(8,128)(2,1)S(1)} %copy-done.3, bf16[2,32,4096]{2,1,0:T(8,128)(2,1)S(1)} %collective-permute-done.2.refs_0_.refs_1_, bf16[2,32,4096]{2,1,0:T(8,128)(2,1)S(1)} %collective-permute-done.3.refs_1_.refs_2_, bf16[2,32,4096]{2,1,0:T(8,128)(2,1)S(1)} %get-tuple-element.48.refs_3_, ...), custom_call_target="tpu_custom_call" | custom-call | flops 1610612736 | bytes 11534336 | tf_op jit(solution)/shard_map/pallas_call | solution.py:158
  51.0 4.4 %collective-permute-done.6.refs_0_ = bf16[1,32,4096]{2,1,0:T(8,128)(2,1)S(1)} collective-permute-done((bf16[1,32,4096]{2,1,0:T(8,128)(2,1)S(1)}, bf16[1,32,4096]{2,1,0:T(8,128)(2,1)S(1)}, u32[]{:S(2)}, u32[]{:S(2)}) %collective-permute-start.6) | collective-permute-done | bytes 262176 | tf_op jit(solution)/shard_map/ppermute | solution.py:78
  55.4 1.7 %collective-permute-start.12 = (bf16[2,32,4096]{2,1,0:T(8,128)(2,1)S(1)}, bf16[2,32,4096]{2,1,0:T(8,128)(2,1)S(1)}, u32[]{:S(2)}, u32[]{:S(2)}) collective-permute-start(bf16[2,32,4096]{2,1,0:T(8,128)(2,1)S(1)} %get-tuple-element.48.refs_3_), channel_id=1, source_target_pairs={{0,4},{1,5},{2,6},{3,7},{4,8},{5,9},{6,10},{7,11},{8,12},{9,13},{1... | collective-permute-start | bytes 1572872 | tf_op jit(solution)/shard_map/ppermute | solution.py:78
  57.1 1.9 %collective-permute-start.13 = (bf16[2,32,4096]{2,1,0:T(8,128)(2,1)S(1)}, bf16[2,32,4096]{2,1,0:T(8,128)(2,1)S(1)}, u32[]{:S(2)}, u32[]{:S(2)}) collective-permute-start(bf16[2,32,4096]{2,1,0:T(8,128)(2,1)S(1)} %get-tuple-element.48.refs_3_), channel_id=1, source_target_pairs={{0,12},{1,13},{2,14},{3,15},{4,0},{5,1},{6,2},{7,3},{8,4},{9,5},{1... | collective-permute-start | bytes 1572872 | tf_op jit(solution)/shard_map/ppermute | solution.py:78
  59.1 3.7 %collective-permute-done.9.refs_1_ = bf16[4,32,4096]{2,1,0:T(8,128)(2,1)S(1)} collective-permute-done((bf16[4,32,4096]{2,1,0:T(8,128)(2,1)S(1)}, bf16[4,32,4096]{2,1,0:T(8,128)(2,1)S(1)}, u32[]{:S(2)}, u32[]{:S(2)}) %collective-permute-start.9) | collective-permute-done | bytes 1048608 | tf_op jit(solution)/shard_map/ppermute | solution.py:78
  62.8 2.5 %collective-permute-start.10 = (bf16[2,32,4096]{2,1,0:T(8,128)(2,1)S(1)}, bf16[2,32,4096]{2,1,0:T(8,128)(2,1)S(1)}, u32[]{:S(2)}, u32[]{:S(2)}) collective-permute-start(bf16[2,32,4096]{2,1,0:T(8,128)(2,1)S(1)} %shard_map.59.refs_0_), channel_id=1, source_target_pairs={{0,3},{1,0},{2,1},{3,2},{4,7},{5,4},{6,5},{7,6},{8,11},{9,8},{10,9... | collective-permute-start | bytes 1572872 | tf_op jit(solution)/shard_map/ppermute | solution.py:78
  65.2 2.4 %shard_map.60.refs_8_ = bf16[3,32,512]{2,1,0:T(8,128)(2,1)S(1)} custom-call(bf16[2,32,4096]{2,1,0:T(8,128)(2,1)S(1)} %shard_map.59.refs_0_, bf16[4,32,4096]{2,1,0:T(8,128)(2,1)S(1)} %collective-permute-done.9.refs_1_, bf16[2,512,4096]{2,1,0:T(8,128)(2,1)S(1)} %copy-done.1), custom_call_target="tpu_custom_call" | custom-call | flops 805306368 | bytes 9961472 | tf_op jit(solution)/shard_map/pallas_call | solution.py:158
  67.6 8.6 %collective-permute-done.8.refs_1_.refs_0_ = bf16[2,32,4096]{2,1,0:T(8,128)(2,1)S(1)} collective-permute-done((bf16[2,32,4096]{2,1,0:T(8,128)(2,1)S(1)}, bf16[2,32,4096]{2,1,0:T(8,128)(2,1)S(1)}, u32[]{:S(2)}, u32[]{:S(2)}) %collective-permute-start.8) | collective-permute-done | bytes 524320 | tf_op jit(solution)/shard_map/ppermute | solution.py:78
  76.2 3.0 %collective-permute-done.12.refs_4_ = bf16[2,32,4096]{2,1,0:T(8,128)(2,1)S(1)} collective-permute-done((bf16[2,32,4096]{2,1,0:T(8,128)(2,1)S(1)}, bf16[2,32,4096]{2,1,0:T(8,128)(2,1)S(1)}, u32[]{:S(2)}, u32[]{:S(2)}) %collective-permute-start.12) | collective-permute-done | bytes 524320 | tf_op jit(solution)/shard_map/ppermute | solution.py:78
  79.2 1.1 %collective-permute-done.13.refs_5_ = bf16[2,32,4096]{2,1,0:T(8,128)(2,1)S(1)} collective-permute-done((bf16[2,32,4096]{2,1,0:T(8,128)(2,1)S(1)}, bf16[2,32,4096]{2,1,0:T(8,128)(2,1)S(1)}, u32[]{:S(2)}, u32[]{:S(2)}) %collective-permute-start.13) | collective-permute-done | bytes 524320 | tf_op jit(solution)/shard_map/ppermute | solution.py:78
  80.3 0.8 shard_map.62
  81.2 2.7 %collective-permute-start.15 = (bf16[1,32,4096]{2,1,0:T(8,128)(2,1)}, bf16[1,32,4096]{2,1,0:T(8,128)(2,1)}, u32[]{:S(2)}, u32[]{:S(2)}) collective-permute-start(bf16[1,32,4096]{2,1,0:T(8,128)(2,1)} %get-tuple-element.60), channel_id=1, source_target_pairs={{0,3},{1,0},{2,1},{3,2},{4,7},{5,4},{6,5},{7,6},{8,11},{9,8},{10,9... | collective-permute-start | bytes 786440 | tf_op jit(solution)/shard_map/ppermute | solution.py:78
  83.8 3.4 %copy-done.2 = bf16[2,512,4096]{2,1,0:T(8,128)(2,1)S(1)} copy-done((bf16[2,512,4096]{2,1,0:T(8,128)(2,1)S(1)}, bf16[2,512,4096]{2,1,0:T(8,128)(2,1)}, u32[]{:S(2)}) %copy-start.2) | copy-done | bytes 8388632
  87.2 2.5 %shard_map.61 = (bf16[16,32,512]{2,1,0:T(8,128)(2,1)S(1)}, bf16[2,512,4096]{2,1,0:T(8,128)(2,1)S(1)}) custom-call(s32[1]{0:T(128)} %bitcast.refs_0_, bf16[2,32,4096]{2,1,0:T(8,128)(2,1)S(1)} %collective-permute-done.8.refs_1_.refs_0_, bf16[2,32,4096]{2,1,0:T(8,128)(2,1)S(1)} %collective-permute-done.10.refs_2_.refs_1_, ...), custom_call_target="tpu_custom_call" | custom-call | flops 1610612736 | bytes 11534336 | tf_op jit(solution)/shard_map/pallas_call | solution.py:158
  90.1 3.4 %shard_map.63 = bf16[16,32,512]{2,1,0:T(8,128)(2,1)S(1)} custom-call(s32[1]{0:T(128)} %bitcast.refs_0_, bf16[1,32,4096]{2,1,0:T(8,128)(2,1)} %collective-permute-done.14.refs_1_, bf16[1,32,4096]{2,1,0:T(8,128)(2,1)} %collective-permute-done.15.refs_2_, bf16[2,512,4096]{2,1,0:T(8,128)(2,1)S(1)} %get-tuple-element.63.refs_3_, ...), custom_call_target="tpu_custom_call", output_to_operand_aliasing={{}: (4, {})} | custom-call | flops 268435456 | bytes 8912896 | tf_op jit(solution)/shard_map/pallas_call | solution.py:158
  93.4 15.4 %all_to_all.5 = bf16[16,32,512]{2,1,0:T(8,128)(2,1)S(1)} all-to-all(bf16[16,32,512]{2,1,0:T(8,128)(2,1)S(1)} %shard_map.63), channel_id=1, replica_groups=mesh['layer'=16,'ex'=16] {'layer'}, dimensions={0} | all-to-all | bytes 1048576 | tf_op jit(solution)/shard_map/all_to_all | solution.py:221
  108.8 0.7 convert_reduce_fusion
  (19 shorter events, 0.9 us)
Async XLA Ops:
  4.9 12.9 %collective-permute-start.2 = (bf16[2,32,4096]{2,1,0:T(8,128)(2,1)}, bf16[2,32,4096]{2,1,0:T(8,128)(2,1)S(1)}, u32[]{:S(2)}, u32[]{:S(2)}) collective-permute-start(bf16[2,32,4096]{2,1,0:T(8,128)(2,1)} %shard_map.55.refs_0_), channel_id=1, source_target_pairs={{0,1},{1,2},{2,3},{3,0},{4,5},{5,6},{6,7},{7,4},{8,9},{9,10},{10,1... | collective-permute-start | bytes 1572872 | tf_op jit(solution)/shard_map/ppermute | solution.py:78
  6.9 12.4 %collective-permute-start.3 = (bf16[2,32,4096]{2,1,0:T(8,128)(2,1)}, bf16[2,32,4096]{2,1,0:T(8,128)(2,1)S(1)}, u32[]{:S(2)}, u32[]{:S(2)}) collective-permute-start(bf16[2,32,4096]{2,1,0:T(8,128)(2,1)} %shard_map.55.refs_0_), channel_id=1, source_target_pairs={{0,3},{1,0},{2,1},{3,2},{4,7},{5,4},{6,5},{7,6},{8,11},{9,8},{10,9... | collective-permute-start | bytes 1572872 | tf_op jit(solution)/shard_map/ppermute | solution.py:78
  8.2 20.9 %collective-permute-start = (bf16[2,32,4096]{2,1,0:T(8,128)(2,1)}, bf16[2,32,4096]{2,1,0:T(8,128)(2,1)S(1)}, u32[]{:S(2)}, u32[]{:S(2)}) collective-permute-start(bf16[2,32,4096]{2,1,0:T(8,128)(2,1)} %shard_map.55.refs_0_), channel_id=1, source_target_pairs={{0,4},{1,5},{2,6},{3,7},{4,8},{5,9},{6,10},{7,11},{8,12},{9,13},{1... | collective-permute-start | bytes 1572872 | tf_op jit(solution)/shard_map/ppermute | solution.py:78
  11.4 27.5 %collective-permute-start.1 = (bf16[2,32,4096]{2,1,0:T(8,128)(2,1)}, bf16[2,32,4096]{2,1,0:T(8,128)(2,1)S(1)}, u32[]{:S(2)}, u32[]{:S(2)}) collective-permute-start(bf16[2,32,4096]{2,1,0:T(8,128)(2,1)} %shard_map.55.refs_0_), channel_id=1, source_target_pairs={{0,12},{1,13},{2,14},{3,15},{4,0},{5,1},{6,2},{7,3},{8,4},{9,5},{1... | collective-permute-start | bytes 1572872 | tf_op jit(solution)/shard_map/ppermute | solution.py:78
  19.4 19.5 %collective-permute-start.4 = (bf16[1,32,4096]{2,1,0:T(8,128)(2,1)S(1)}, bf16[1,32,4096]{2,1,0:T(8,128)(2,1)S(1)}, u32[]{:S(2)}, u32[]{:S(2)}) collective-permute-start(bf16[1,32,4096]{2,1,0:T(8,128)(2,1)S(1)} %get-tuple-element.35), channel_id=1, source_target_pairs={{0,3},{1,0},{2,1},{3,2},{4,7},{5,4},{6,5},{7,6},{8,11},{9,8},{10,9... | collective-permute-start | bytes 786440 | tf_op jit(solution)/shard_map/ppermute | solution.py:78
  21.3 17.6 %collective-permute-start.5 = (bf16[1,32,4096]{2,1,0:T(8,128)(2,1)S(1)}, bf16[1,32,4096]{2,1,0:T(8,128)(2,1)S(1)}, u32[]{:S(2)}, u32[]{:S(2)}) collective-permute-start(bf16[1,32,4096]{2,1,0:T(8,128)(2,1)S(1)} %get-tuple-element.36), channel_id=1, source_target_pairs={{0,1},{1,2},{2,3},{3,0},{4,5},{5,6},{6,7},{7,4},{8,9},{9,10},{10,1... | collective-permute-start | bytes 786440 | tf_op jit(solution)/shard_map/ppermute | solution.py:78
  39.0 23.7 %collective-permute-start.9 = (bf16[4,32,4096]{2,1,0:T(8,128)(2,1)S(1)}, bf16[4,32,4096]{2,1,0:T(8,128)(2,1)S(1)}, u32[]{:S(2)}, u32[]{:S(2)}) collective-permute-start(bf16[4,32,4096]{2,1,0:T(8,128)(2,1)S(1)} %get-tuple-element.44.refs_4_), channel_id=1, source_target_pairs={{0,3},{1,0},{2,1},{3,2},{4,7},{5,4},{6,5},{7,6},{8,11},{9,8},{10,9... | collective-permute-start | bytes 3145736 | tf_op jit(solution)/shard_map/ppermute | solution.py:78
  40.4 39.9 %collective-permute-start.11 = (bf16[4,32,4096]{2,1,0:T(8,128)(2,1)S(1)}, bf16[4,32,4096]{2,1,0:T(8,128)(2,1)S(1)}, u32[]{:S(2)}, u32[]{:S(2)}) collective-permute-start(bf16[4,32,4096]{2,1,0:T(8,128)(2,1)S(1)} %get-tuple-element.44.refs_4_), channel_id=1, source_target_pairs={{0,1},{1,2},{2,3},{3,0},{4,5},{5,6},{6,7},{7,4},{8,9},{9,10},{10,1... | collective-permute-start | bytes 3145736 | tf_op jit(solution)/shard_map/ppermute | solution.py:78
  40.6 14.8 %collective-permute-start.6 = (bf16[1,32,4096]{2,1,0:T(8,128)(2,1)S(1)}, bf16[1,32,4096]{2,1,0:T(8,128)(2,1)S(1)}, u32[]{:S(2)}, u32[]{:S(2)}) collective-permute-start(bf16[1,32,4096]{2,1,0:T(8,128)(2,1)S(1)} %get-tuple-element.41), channel_id=1, source_target_pairs={{0,4},{1,5},{2,6},{3,7},{4,8},{5,9},{6,10},{7,11},{8,12},{9,13},{1... | collective-permute-start | bytes 786440 | tf_op jit(solution)/shard_map/ppermute | solution.py:78
  43.5 11.9 %collective-permute-start.7 = (bf16[1,32,4096]{2,1,0:T(8,128)(2,1)S(1)}, bf16[1,32,4096]{2,1,0:T(8,128)(2,1)S(1)}, u32[]{:S(2)}, u32[]{:S(2)}) collective-permute-start(bf16[1,32,4096]{2,1,0:T(8,128)(2,1)S(1)} %get-tuple-element.42), channel_id=1, source_target_pairs={{0,12},{1,13},{2,14},{3,15},{4,0},{5,1},{6,2},{7,3},{8,4},{9,5},{1... | collective-permute-start | bytes 786440 | tf_op jit(solution)/shard_map/ppermute | solution.py:78
  44.2 3.4 %copy-start = (bf16[2,512,4096]{2,1,0:T(8,128)(2,1)S(1)}, bf16[2,512,4096]{2,1,0:T(8,128)(2,1)}, u32[]{:S(2)}) copy-start(bf16[2,512,4096]{2,1,0:T(8,128)(2,1)} %refs_6_.1) | copy-start | bytes 25165828
  47.5 1.0 copy-start.3
  48.6 16.7 %copy-start.1 = (bf16[2,512,4096]{2,1,0:T(8,128)(2,1)S(1)}, bf16[2,512,4096]{2,1,0:T(8,128)(2,1)}, u32[]{:S(2)}) copy-start(bf16[2,512,4096]{2,1,0:T(8,128)(2,1)} %refs_6_.1) | copy-start | bytes 25165828
  55.4 23.8 %collective-permute-start.12 = (bf16[2,32,4096]{2,1,0:T(8,128)(2,1)S(1)}, bf16[2,32,4096]{2,1,0:T(8,128)(2,1)S(1)}, u32[]{:S(2)}, u32[]{:S(2)}) collective-permute-start(bf16[2,32,4096]{2,1,0:T(8,128)(2,1)S(1)} %get-tuple-element.48.refs_3_), channel_id=1, source_target_pairs={{0,4},{1,5},{2,6},{3,7},{4,8},{5,9},{6,10},{7,11},{8,12},{9,13},{1... | collective-permute-start | bytes 1572872 | tf_op jit(solution)/shard_map/ppermute | solution.py:78
  57.1 23.2 %collective-permute-start.13 = (bf16[2,32,4096]{2,1,0:T(8,128)(2,1)S(1)}, bf16[2,32,4096]{2,1,0:T(8,128)(2,1)S(1)}, u32[]{:S(2)}, u32[]{:S(2)}) collective-permute-start(bf16[2,32,4096]{2,1,0:T(8,128)(2,1)S(1)} %get-tuple-element.48.refs_3_), channel_id=1, source_target_pairs={{0,12},{1,13},{2,14},{3,15},{4,0},{5,1},{6,2},{7,3},{8,4},{9,5},{1... | collective-permute-start | bytes 1572872 | tf_op jit(solution)/shard_map/ppermute | solution.py:78
  59.0 17.2 %collective-permute-start.8 = (bf16[2,32,4096]{2,1,0:T(8,128)(2,1)S(1)}, bf16[2,32,4096]{2,1,0:T(8,128)(2,1)S(1)}, u32[]{:S(2)}, u32[]{:S(2)}) collective-permute-start(bf16[2,32,4096]{2,1,0:T(8,128)(2,1)S(1)} %shard_map.59.refs_0_), channel_id=1, source_target_pairs={{0,1},{1,2},{2,3},{3,0},{4,5},{5,6},{6,7},{7,4},{8,9},{9,10},{10,1... | collective-permute-start | bytes 1572872 | tf_op jit(solution)/shard_map/ppermute | solution.py:78
  62.8 17.5 %collective-permute-start.10 = (bf16[2,32,4096]{2,1,0:T(8,128)(2,1)S(1)}, bf16[2,32,4096]{2,1,0:T(8,128)(2,1)S(1)}, u32[]{:S(2)}, u32[]{:S(2)}) collective-permute-start(bf16[2,32,4096]{2,1,0:T(8,128)(2,1)S(1)} %shard_map.59.refs_0_), channel_id=1, source_target_pairs={{0,3},{1,0},{2,1},{3,2},{4,7},{5,4},{6,5},{7,6},{8,11},{9,8},{10,9... | collective-permute-start | bytes 1572872 | tf_op jit(solution)/shard_map/ppermute | solution.py:78
  81.1 8.9 %collective-permute-start.14 = (bf16[1,32,4096]{2,1,0:T(8,128)(2,1)}, bf16[1,32,4096]{2,1,0:T(8,128)(2,1)}, u32[]{:S(2)}, u32[]{:S(2)}) collective-permute-start(bf16[1,32,4096]{2,1,0:T(8,128)(2,1)} %get-tuple-element.59), channel_id=1, source_target_pairs={{0,1},{1,2},{2,3},{3,0},{4,5},{5,6},{6,7},{7,4},{8,9},{9,10},{10,1... | collective-permute-start | bytes 786440 | tf_op jit(solution)/shard_map/ppermute | solution.py:78
  81.2 8.9 %collective-permute-start.15 = (bf16[1,32,4096]{2,1,0:T(8,128)(2,1)}, bf16[1,32,4096]{2,1,0:T(8,128)(2,1)}, u32[]{:S(2)}, u32[]{:S(2)}) collective-permute-start(bf16[1,32,4096]{2,1,0:T(8,128)(2,1)} %get-tuple-element.60), channel_id=1, source_target_pairs={{0,3},{1,0},{2,1},{3,2},{4,7},{5,4},{6,5},{7,6},{8,11},{9,8},{10,9... | collective-permute-start | bytes 786440 | tf_op jit(solution)/shard_map/ppermute | solution.py:78
  83.8 3.4 %copy-start.2 = (bf16[2,512,4096]{2,1,0:T(8,128)(2,1)S(1)}, bf16[2,512,4096]{2,1,0:T(8,128)(2,1)}, u32[]{:S(2)}) copy-start(bf16[2,512,4096]{2,1,0:T(8,128)(2,1)} %refs_6_.1) | copy-start | bytes 25165828

commit v3 on v2

v3 whole, which is shorter than its diff:
```python
import functools

import jax
import jax.numpy as jnp
from jax import lax
from jax.experimental import pallas as pl
from jax.experimental.pallas import tpu as pltpu
from jax.sharding import PartitionSpec as P

SIDE = 4
TILE = 2048

def split(v):
    hi = v.astype(jnp.bfloat16)
    return hi, (v - hi.astype(jnp.float32)).astype(jnp.bfloat16)

def twice(block):
    none = jnp.zeros_like(block)
    return jnp.concatenate([jnp.concatenate([block, none], axis=1), jnp.concatenate([none, block], axis=1)], axis=0)

def dot(a, b, dims=((1,), (0,))):
    return lax.dot_general(a, b, (dims, ((), ())), preferred_element_type=jnp.float32)

def precondition_kernel(raw, basis_out, basis_in, eigen, out, work):
    modules, count_q, entries = raw.shape
    side = basis_out.shape[1]
    half = count_q // 2
    low = lax.broadcasted_iota(jnp.int32, (half, 2 * side), 1) < side
    every = range(modules)
    nt = ((1,), (1,))

    outs = [split(basis_out[m]) for m in every]
    turned = [split(basis_out[m].T) for m in every]
    ins = [split(twice(basis_in[m])) for m in every]
    inverses = [1.0 / (eigen[m] + 0.1 * jnp.mean(eigen[m])) for m in every]
    inverses = [jnp.concatenate([v, v], axis=1) for v in inverses]
    for m in every:
        rows = []
        for pair in range(side // 2):
            tile = raw[m, :, pl.ds(pair * 2 * side, 2 * side)].astype(jnp.float32)
            top, bottom = tile[:half], tile[half:]
            rows.append(jnp.where(low, top, pltpu.roll(bottom, side, 1)))
            rows.append(jnp.where(low, pltpu.roll(top, side, 1), bottom))
        grads = jnp.concatenate(rows, axis=0).astype(jnp.bfloat16)
        work[m] = dot(jnp.concatenate([grads, grads], axis=1), jnp.concatenate(ins[m], axis=0))
    parts = []
    for m in every:
        left = jnp.concatenate([work[m, pl.ds(q, side, stride=half), :] for q in range(half)], axis=1)
        hi, lo = split(left)
        parts.append((hi, lo))
    rotated = []
    for m in every:
        (hi, lo), (t_hi, t_lo) = parts[m], turned[m]
        rotated.append(dot(jnp.concatenate([t_hi, t_hi, t_lo], axis=1), jnp.concatenate([hi, lo, hi], axis=0)))
    scaled = []
    for m in every:
        blocks = [rotated[m][:, q * 2 * side : (q + 1) * 2 * side] * inverses[m] for q in range(half)]
        scaled.append(split(jnp.concatenate(blocks, axis=1)))
    back = []
    for m in every:
        (hi, lo), (o_hi, o_lo) = scaled[m], outs[m]
        back.append(dot(jnp.concatenate([o_hi, o_hi, o_lo], axis=1), jnp.concatenate([hi, lo, hi], axis=0)))
    for m in every:
        hi, lo = split(jnp.concatenate([back[m][:, q * 2 * side : (q + 1) * 2 * side] for q in range(half)], axis=0))
        in_hi, in_lo = ins[m]
        work[m] = dot(jnp.concatenate([hi, lo], axis=1), jnp.concatenate([in_hi, in_hi], axis=1), nt) + dot(hi, in_lo, nt)
    for m in every:
        for pair in range(side // 2):
            even, odd = work[m, pl.ds(2 * pair, half, stride=side), :], work[m, pl.ds(2 * pair + 1, half, stride=side), :]
            at = pl.ds(pair * 2 * side, 2 * side)
            out[m, :half, at] = jnp.where(low, even, pltpu.roll(odd, side, 1)).astype(out.dtype)
            out[m, half:, at] = jnp.where(low, pltpu.roll(even, side, 1), odd).astype(out.dtype)

def precondition(raw, basis_out, basis_in, eigen):
    modules, count_q, entries = raw.shape
    side = basis_out.shape[1]
    full = lambda *shape: pl.BlockSpec(shape, lambda i: (0, 0, 0))
    return pl.pallas_call(
        precondition_kernel,
        out_shape=jax.ShapeDtypeStruct(raw.shape, jnp.bfloat16),
        grid=(1,),
        in_specs=[full(*raw.shape)] + [full(modules, side, side)] * 3,
        out_specs=full(*raw.shape),
        scratch_shapes=[pltpu.VMEM((modules, side * count_q // 2, 2 * side), jnp.float32)],
        compiler_params=pltpu.CompilerParams(vmem_limit_bytes=56 << 20),
    )(raw, basis_out, basis_in, eigen)


def move(value, step_z, step_x):
    to = lambda z, x: (z + step_z) % SIDE * SIDE + (x + step_x) % SIDE
    return lax.ppermute(value, "ex", [(z * SIDE + x, to(z, x)) for z in range(SIDE) for x in range(SIDE)])


def in_order(*values):
    return lax.optimization_barrier(values)


def arrange(values, plan):
    def kernel(*refs):
        given, made = refs[: len(values)], refs[len(values) :]
        for out, parts in zip(made, plan):
            for at, (value, module) in enumerate(parts):
                out[at] = given[value][module]

    space = pl.BlockSpec(memory_space=pltpu.VMEM)
    return pl.pallas_call(
        kernel,
        out_shape=[jax.ShapeDtypeStruct((len(parts),) + values[0].shape[1:], values[0].dtype) for parts in plan],
        in_specs=[space] * len(values),
        out_specs=[space] * len(plan),
        compiler_params=pltpu.CompilerParams(vmem_limit_bytes=4 << 20),
        cost_estimate=pl.CostEstimate(
            flops=0, bytes_accessed=4 * values[0][0].size * sum(len(parts) for parts in plan), transcendentals=0
        ),
    )(*values)


def blocks_of(shards, held, train, dtype, kept=None):
    total = None
    for module in range(train.shape[0]):
        for at in range(0, train.shape[2], TILE):
            part = pl.ds(at, TILE)
            stored = train[module, :, part]
            if kept is not None:
                kept[module, :, part] = stored
            rows = jnp.concatenate([held[s[module][0]][s[module][1], :, part] for s in shards], axis=0)
            term = dot(stored, rows, ((1,), (1,)))
            total = term if total is None else total + term
    return total.T.astype(dtype).reshape(len(shards), -1, train.shape[1])


def next_kernel(shards, count, *refs):
    held, (train, out) = refs[:count], refs[count:]
    out[...] = blocks_of(shards, held, train, out.dtype)


def keep_kernel(shards, count, *refs):
    held, (train, out, kept) = refs[:count], refs[count:]
    out[...] = blocks_of(shards, held, train, out.dtype, kept)


def last_kernel(shards, count, offsets, me, *refs):
    held, train, done, out = refs[:count], refs[count], refs[count + 1 : -1], refs[-1]
    z, x = lax.shift_right_logical(me[0], 2), me[0] & (SIDE - 1)
    places = [((z + dz) & (SIDE - 1)) * SIDE + ((x + dx) & (SIDE - 1)) for dz, dx in offsets]
    at = 0
    for ref in done:
        for i in range(ref.shape[0]):
            out[places[at]] = ref[i]
            at += 1
    blocks = blocks_of(shards, held, train, out.dtype)
    for i in range(len(shards)):
        out[places[at + i]] = blocks[i]


def score_call(kernel, shards, train, out_shapes, others=(), lead=(), weight=1):
    arrays = []
    for array in (array for shard in shards for array, _ in shard):
        if all(array is not a for a in arrays):
            arrays.append(array)
    number = lambda array: next(i for i, a in enumerate(arrays) if a is array)
    shards = [[(number(array), at) for array, at in shard] for shard in shards]
    space = pl.BlockSpec(memory_space=pltpu.VMEM)
    rows = len(shards) * arrays[0].shape[1]
    return pl.pallas_call(
        functools.partial(kernel, shards, len(arrays)),
        out_shape=out_shapes,
        in_specs=[pl.BlockSpec(memory_space=pltpu.SMEM)] * len(lead) + [space] * (len(arrays) + 1 + len(others)),
        out_specs=jax.tree.map(lambda _: space, out_shapes),
        compiler_params=pltpu.CompilerParams(vmem_limit_bytes=16 << 20),
        cost_estimate=pl.CostEstimate(
            flops=2 * rows * train.size * weight,
            bytes_accessed=2 * (train.size + rows * train.size // train.shape[1]),
            transcendentals=0,
        ),
    )(*lead, *arrays, train, *others)


def shard(array, at=0):
    return [(array, at), (array, at + 1)]


def blocks_shape(count, train, queries):
    return jax.ShapeDtypeStruct((count, queries, train.shape[1]), jnp.bfloat16)


def local(query_grads, train_grads, basis_out, basis_in, eigen):
    me = lax.axis_index("ex").astype(jnp.int32).reshape(1)
    queries = query_grads.shape[1]
    own = precondition(query_grads, basis_out, basis_in, eigen)
    x2 = move(own, 0, 2)
    xr, xl = move(own, 0, -1), move(own, 0, 1)
    zr, zl = move(own, -1, 0), move(own, 1, 0)
    zl, zr, xl, xr = in_order(zl, zr, xl, xr)
    zl_half, zr_half, both = arrange([zl, zr], [[(0, 0)], [(1, 1)], [(0, 0), (0, 1), (1, 0), (1, 1)]])
    both_xr, both_xl = move(both, 0, -1), move(both, 0, 1)
    z2b, z2a = move(zr_half, -1, 0), move(zl_half, 1, 0)
    shards = [shard(own), shard(xl), shard(xr), shard(x2), shard(both, 0), shard(both, 2)]
    first = score_call(next_kernel, shards, train_grads, blocks_shape(6, train_grads, queries), weight=4)
    z2a, z2b, x2, first = in_order(z2a, z2b, x2, first)
    (z2,) = arrange([z2a, z2b], [[(0, 0), (1, 0)]])
    z2_xl = move(z2, 0, 1)
    zr_x2, zl_x2 = move(x2, -1, 0), move(x2, 1, 0)
    z2, both_xr = in_order(z2, both_xr)
    z2_xr = move(z2, 0, -1)
    shards = [shard(z2), shard(both_xr, 0), shard(both_xr, 2)]
    second = score_call(next_kernel, shards, train_grads, blocks_shape(3, train_grads, queries))
    z2_xl, z2_xr, both_xl, zl_x2, zr_x2, second = in_order(z2_xl, z2_xr, both_xl, zl_x2, zr_x2, second)
    halves = arrange([z2_xl, z2_xr], [[(0, 0)], [(1, 1)]])
    z2_x2 = move(halves[0], 0, 1), move(halves[1], 0, -1)
    offsets = [
        (0, 0), (0, -1), (0, 1), (0, 2), (-1, 0), (1, 0),
        (2, 0), (-1, 1), (1, 1),
        (2, -1), (-1, -1), (1, -1),
        (2, 1), (-1, 2), (1, 2), (2, 2),
    ]
    shards = [shard(z2_xl), shard(both_xl, 0), shard(both_xl, 2)]
    shapes = [blocks_shape(3, train_grads, queries), jax.ShapeDtypeStruct(train_grads.shape, train_grads.dtype)]
    third, train = score_call(keep_kernel, shards, train_grads, shapes)
    third, train, *z2_x2 = in_order(third, train, *z2_x2)
    shards = [shard(z2_xr), shard(zl_x2), shard(zr_x2), [(half, 0) for half in z2_x2]]
    kernel = lambda own, count, *refs: last_kernel(own, count, offsets, *refs)
    shape = blocks_shape(SIDE * SIDE, train_grads, queries)
    parts = score_call(kernel, shards, train, shape, [first, second, third], [me])
    parts = lax.all_to_all(parts, "layer", split_axis=0, concat_axis=0, tiled=True)
    return jnp.sum(parts.astype(jnp.float32), axis=0)


def solution(mesh):
    in_specs = (
        P("layer", "ex", None),
        P("layer", "ex", None),
        P("layer", None, None),
        P("layer", None, None),
        P("layer", None, None),
    )
    out_specs = P("layer", "ex")
    return jax.shard_map(local, mesh=mesh, in_specs=in_specs, out_specs=out_specs, check_vma=False)
```

time: 110 us -> 107 us (0.973)
  waiting for transfers between devices: 43.6 us -> 32.9 us
  starting transfers between devices: 25.4 us -> 32.3 us
  blocking collectives: 15.4 us -> 17.1 us
    ppermute x16 -> x15, waiting for transfers between devices: 43.6 us -> 32.9 us  [move(): lax.ppermute(value, 'ex', [(z * SIDE + x, to(z, x)) for z in range(SIDE)...]
    ppermute x16 -> x15, starting transfers between devices: 25.4 us -> 32.3 us  [move(): lax.ppermute(value, 'ex', [(z * SIDE + x, to(z, x)) for z in range(SIDE)...]
    all_to_all x1, blocking collectives: 15.4 us -> 17.1 us  [local(): lax.all_to_all(parts, 'layer', split_axis=0, concat_axis=0, tiled=True)]
    unnamed x8 -> x12, local copies, waits for them, and re-layouts: 7.81 us -> 7.82 us
  transfers between devices with their start and end apart: 16 -> 15, of which waited for: 10 -> 5; matrix products, arithmetic and copies ran while one was open for 0% -> 0% of each run, Pallas kernels for 7% -> 7%
where the time goes in v3:
time: 107 us
  waiting for transfers between devices  32.9 us (31%)
  starting transfers between devices  32.3 us (30%)
  blocking collectives  17.1 us (16%)
  Pallas kernels  16 us (15%)
  local copies, waits for them, and re-layouts  7.82 us (7%)
    ppermute x15, waiting for transfers between devices, move(): lax.ppermute(value, 'ex', [(z * SIDE + x, to(z, x)) for z in range(SIDE)...  32.9 us
    ppermute x15, starting transfers between devices, move(): lax.ppermute(value, 'ex', [(z * SIDE + x, to(z, x)) for z in range(SIDE)...  32.3 us
    all_to_all x1, blocking collectives, local(): lax.all_to_all(parts, 'layer', split_axis=0, concat_axis=0, tiled=True)  17.1 us
    pallas_call x4, Pallas kernels, score_call(): pl.pallas_call(functools.partial(kernel, shards, len(arrays)), out_shape=...  10.7 us
    unnamed x12, local copies, waits for them, and re-layouts  7.82 us
    pallas_call x1, Pallas kernels, precondition(): pl.pallas_call(precondition_kernel, out_shape=jax.ShapeDtypeStruct(raw.sh...  4.34 us
  transfers between devices with their start and end apart: 15, of which 5 were waited for; matrix products, arithmetic and copies ran while one was open for 0% of the time, Pallas kernels for 7%

profile of v3, /device:TPU:1, one launch (start us, length us, event | category | flops | bytes accessed | tf_op | source)
XLA Modules:
  0.0 107.0 jit_solution(14389998024992584448)
XLA Ops:
  0.0 4.3 %shard_map.55.refs_0_ = bf16[2,32,4096]{2,1,0:T(8,128)(2,1)} custom-call(bf16[2,32,4096]{2,1,0:T(8,128)(2,1)} %raw.1, f32[2,64,64]{2,1,0:T(8,128)} %basis_out.1, f32[2,64,64]{2,1,0:T(8,128)} %basis_in.1, f32[2,64,64]{2,1,0:T(8,128)} %eigen.1), custom_call_target="tpu_custom_call" | custom-call | tf_op jit(solution)/shard_map/pallas_call | solution.py:78
  4.3 3.8 %collective-permute-start = (bf16[2,32,4096]{2,1,0:T(8,128)(2,1)}, bf16[2,32,4096]{2,1,0:T(8,128)(2,1)S(1)}, u32[]{:S(2)}, u32[]{:S(2)}) collective-permute-start(bf16[2,32,4096]{2,1,0:T(8,128)(2,1)} %shard_map.55.refs_0_), channel_id=1, source_target_pairs={{0,4},{1,5},{2,6},{3,7},{4,8},{5,9},{6,10},{7,11},{8,12},{9,13},{1... | collective-permute-start | bytes 1572872 | tf_op jit(solution)/shard_map/ppermute | solution.py:91
  8.2 3.0 %collective-permute-start.1 = (bf16[2,32,4096]{2,1,0:T(8,128)(2,1)}, bf16[2,32,4096]{2,1,0:T(8,128)(2,1)S(1)}, u32[]{:S(2)}, u32[]{:S(2)}) collective-permute-start(bf16[2,32,4096]{2,1,0:T(8,128)(2,1)} %shard_map.55.refs_0_), channel_id=1, source_target_pairs={{0,12},{1,13},{2,14},{3,15},{4,0},{5,1},{6,2},{7,3},{8,4},{9,5},{1... | collective-permute-start | bytes 1572872 | tf_op jit(solution)/shard_map/ppermute | solution.py:91
  11.2 1.2 %collective-permute-start.2 = (bf16[2,32,4096]{2,1,0:T(8,128)(2,1)}, bf16[2,32,4096]{2,1,0:T(8,128)(2,1)S(1)}, u32[]{:S(2)}, u32[]{:S(2)}) collective-permute-start(bf16[2,32,4096]{2,1,0:T(8,128)(2,1)} %shard_map.55.refs_0_), channel_id=1, source_target_pairs={{0,1},{1,2},{2,3},{3,0},{4,5},{5,6},{6,7},{7,4},{8,9},{9,10},{10,1... | collective-permute-start | bytes 1572872 | tf_op jit(solution)/shard_map/ppermute | solution.py:91
  12.4 1.5 %collective-permute-start.3 = (bf16[2,32,4096]{2,1,0:T(8,128)(2,1)}, bf16[2,32,4096]{2,1,0:T(8,128)(2,1)S(1)}, u32[]{:S(2)}, u32[]{:S(2)}) collective-permute-start(bf16[2,32,4096]{2,1,0:T(8,128)(2,1)} %shard_map.55.refs_0_), channel_id=1, source_target_pairs={{0,3},{1,0},{2,1},{3,2},{4,7},{5,4},{6,5},{7,6},{8,11},{9,8},{10,9... | collective-permute-start | bytes 1572872 | tf_op jit(solution)/shard_map/ppermute | solution.py:91
  13.9 1.5 %collective-permute-start.6 = (bf16[2,32,4096]{2,1,0:T(8,128)(2,1)}, bf16[2,32,4096]{2,1,0:T(8,128)(2,1)S(1)}, u32[]{:S(2)}, u32[]{:S(2)}) collective-permute-start(bf16[2,32,4096]{2,1,0:T(8,128)(2,1)} %shard_map.55.refs_0_), channel_id=1, source_target_pairs={{0,2},{1,3},{2,0},{3,1},{4,6},{5,7},{6,4},{7,5},{8,10},{9,11},{10,... | collective-permute-start | bytes 1572872 | tf_op jit(solution)/shard_map/ppermute | solution.py:91
  15.4 11.7 %collective-permute-done.refs_0_ = bf16[2,32,4096]{2,1,0:T(8,128)(2,1)S(1)} collective-permute-done((bf16[2,32,4096]{2,1,0:T(8,128)(2,1)}, bf16[2,32,4096]{2,1,0:T(8,128)(2,1)S(1)}, u32[]{:S(2)}, u32[]{:S(2)}) %collective-permute-start) | collective-permute-done | bytes 524320 | tf_op jit(solution)/shard_map/ppermute | solution.py:91
  27.1 8.6 %collective-permute-done.1.refs_1_ = bf16[2,32,4096]{2,1,0:T(8,128)(2,1)S(1)} collective-permute-done((bf16[2,32,4096]{2,1,0:T(8,128)(2,1)}, bf16[2,32,4096]{2,1,0:T(8,128)(2,1)S(1)}, u32[]{:S(2)}, u32[]{:S(2)}) %collective-permute-start.1) | collective-permute-done | bytes 524320 | tf_op jit(solution)/shard_map/ppermute | solution.py:91
  35.8 0.0 collective-permute-done.2.refs_1_
  35.8 0.0 collective-permute-done.3.refs_2_
  35.8 0.1 shard_map.56
  35.9 2.5 %collective-permute-start.8 = (bf16[4,32,4096]{2,1,0:T(8,128)(2,1)S(1)}, bf16[4,32,4096]{2,1,0:T(8,128)(2,1)S(1)}, u32[]{:S(2)}, u32[]{:S(2)}) collective-permute-start(bf16[4,32,4096]{2,1,0:T(8,128)(2,1)S(1)} %get-tuple-element.38.refs_4_), channel_id=1, source_target_pairs={{0,3},{1,0},{2,1},{3,2},{4,7},{5,4},{6,5},{7,6},{8,11},{9,8},{10,9... | collective-permute-start | bytes 3145736 | tf_op jit(solution)/shard_map/ppermute | solution.py:91
  38.4 2.9 %collective-permute-start.4 = (bf16[1,32,4096]{2,1,0:T(8,128)(2,1)S(1)}, bf16[1,32,4096]{2,1,0:T(8,128)(2,1)S(1)}, u32[]{:S(2)}, u32[]{:S(2)}) collective-permute-start(bf16[1,32,4096]{2,1,0:T(8,128)(2,1)S(1)} %get-tuple-element.34), channel_id=1, source_target_pairs={{0,4},{1,5},{2,6},{3,7},{4,8},{5,9},{6,10},{7,11},{8,12},{9,13},{1... | collective-permute-start | bytes 786440 | tf_op jit(solution)/shard_map/ppermute | solution.py:91
  41.3 0.7 collective-permute-start.5
  42.0 3.4 %copy-done = bf16[2,512,4096]{2,1,0:T(8,128)(2,1)S(1)} copy-done((bf16[2,512,4096]{2,1,0:T(8,128)(2,1)S(1)}, bf16[2,512,4096]{2,1,0:T(8,128)(2,1)}, u32[]{:S(2)}) %copy-start) | copy-done | bytes 8388632
  45.4 1.0 copy-done.3
  46.4 2.4 %shard_map.57.refs_7_ = bf16[6,32,512]{2,1,0:T(8,128)(2,1)S(1)} custom-call(bf16[2,32,4096]{2,1,0:T(8,128)(2,1)S(1)} %copy-done.3, bf16[2,32,4096]{2,1,0:T(8,128)(2,1)S(1)} %collective-permute-done.2.refs_1_, bf16[2,32,4096]{2,1,0:T(8,128)(2,1)S(1)} %collective-permute-done.3.refs_2_, bf16[2,32,4096]{2,1,0:T(8,128)(2,1)S(1)} %collective-permute-done.6.refs_3_, ...), custom_call_target="tpu_custom_call" | custom-call | flops 6442450944 | bytes 11534336 | tf_op jit(solution)/shard_map/pallas_call | solution.py:165
  48.9 4.5 %collective-permute-start.11 = (bf16[2,32,4096]{2,1,0:T(8,128)(2,1)S(1)}, bf16[2,32,4096]{2,1,0:T(8,128)(2,1)S(1)}, u32[]{:S(2)}, u32[]{:S(2)}) collective-permute-start(bf16[2,32,4096]{2,1,0:T(8,128)(2,1)S(1)} %collective-permute-done.6.refs_3_), channel_id=1, source_target_pairs={{0,4},{1,5},{2,6},{3,7},{4,8},{5,9},{6,10},{7,11},{8,12},{9,13},{1... | collective-permute-start | bytes 1572872 | tf_op jit(solution)/shard_map/ppermute | solution.py:91
  53.4 0.0 collective-permute-start.12
  53.5 3.6 %collective-permute-start.7 = (bf16[2,32,4096]{2,1,0:T(8,128)(2,1)S(1)}, bf16[2,32,4096]{2,1,0:T(8,128)(2,1)S(1)}, u32[]{:S(2)}, u32[]{:S(2)}) collective-permute-start(bf16[2,32,4096]{2,1,0:T(8,128)(2,1)S(1)} %shard_map.58.refs_0_), channel_id=1, source_target_pairs={{0,1},{1,2},{2,3},{3,0},{4,5},{5,6},{6,7},{7,4},{8,9},{9,10},{10,1... | collective-permute-start | bytes 1572872 | tf_op jit(solution)/shard_map/ppermute | solution.py:91
  57.1 2.5 %collective-permute-done.8.refs_1_ = bf16[4,32,4096]{2,1,0:T(8,128)(2,1)S(1)} collective-permute-done((bf16[4,32,4096]{2,1,0:T(8,128)(2,1)S(1)}, bf16[4,32,4096]{2,1,0:T(8,128)(2,1)S(1)}, u32[]{:S(2)}, u32[]{:S(2)}) %collective-permute-start.8) | collective-permute-done | bytes 1048608 | tf_op jit(solution)/shard_map/ppermute | solution.py:91
  59.6 2.0 %collective-permute-start.9 = (bf16[2,32,4096]{2,1,0:T(8,128)(2,1)S(1)}, bf16[2,32,4096]{2,1,0:T(8,128)(2,1)S(1)}, u32[]{:S(2)}, u32[]{:S(2)}) collective-permute-start(bf16[2,32,4096]{2,1,0:T(8,128)(2,1)S(1)} %shard_map.58.refs_0_), channel_id=1, source_target_pairs={{0,3},{1,0},{2,1},{3,2},{4,7},{5,4},{6,5},{7,6},{8,11},{9,8},{10,9... | collective-permute-start | bytes 1572872 | tf_op jit(solution)/shard_map/ppermute | solution.py:91
  61.7 2.4 %shard_map.59.refs_8_ = bf16[3,32,512]{2,1,0:T(8,128)(2,1)S(1)} custom-call(bf16[2,32,4096]{2,1,0:T(8,128)(2,1)S(1)} %shard_map.58.refs_0_, bf16[4,32,4096]{2,1,0:T(8,128)(2,1)S(1)} %collective-permute-done.8.refs_1_, bf16[2,512,4096]{2,1,0:T(8,128)(2,1)S(1)} %copy-done.1), custom_call_target="tpu_custom_call" | custom-call | flops 805306368 | bytes 9961472 | tf_op jit(solution)/shard_map/pallas_call | solution.py:165
  64.0 8.6 %collective-permute-done.7.refs_0_ = bf16[2,32,4096]{2,1,0:T(8,128)(2,1)S(1)} collective-permute-done((bf16[2,32,4096]{2,1,0:T(8,128)(2,1)S(1)}, bf16[2,32,4096]{2,1,0:T(8,128)(2,1)S(1)}, u32[]{:S(2)}, u32[]{:S(2)}) %collective-permute-start.7) | collective-permute-done | bytes 524320 | tf_op jit(solution)/shard_map/ppermute | solution.py:91
  72.6 0.8 shard_map.61
  73.5 4.9 %collective-permute-start.13 = (bf16[1,32,4096]{2,1,0:T(8,128)(2,1)}, bf16[1,32,4096]{2,1,0:T(8,128)(2,1)S(1)}, u32[]{:S(2)}, u32[]{:S(2)}) collective-permute-start(bf16[1,32,4096]{2,1,0:T(8,128)(2,1)} %get-tuple-element.51), channel_id=1, source_target_pairs={{0,1},{1,2},{2,3},{3,0},{4,5},{5,6},{6,7},{7,4},{8,9},{9,10},{10,1... | collective-permute-start | bytes 786440 | tf_op jit(solution)/shard_map/ppermute | solution.py:91
  78.4 3.4 %copy-done.2 = bf16[2,512,4096]{2,1,0:T(8,128)(2,1)S(1)} copy-done((bf16[2,512,4096]{2,1,0:T(8,128)(2,1)S(1)}, bf16[2,512,4096]{2,1,0:T(8,128)(2,1)}, u32[]{:S(2)}) %copy-start.2) | copy-done | bytes 8388632
  81.8 2.5 %shard_map.60 = (bf16[3,32,512]{2,1,0:T(8,128)(2,1)S(1)}, bf16[2,512,4096]{2,1,0:T(8,128)(2,1)S(1)}) custom-call(bf16[2,32,4096]{2,1,0:T(8,128)(2,1)S(1)} %collective-permute-done.7.refs_0_, bf16[4,32,4096]{2,1,0:T(8,128)(2,1)S(1)} %collective-permute-done.10.refs_1_, bf16[2,512,4096]{2,1,0:T(8,128)(2,1)S(1)} %copy-done.2), custom_call_target="tpu_custom_call" | custom-call | flops 805306368 | bytes 9961472 | tf_op jit(solution)/shard_map/pallas_call | solution.py:165
  84.3 1.5 %collective-permute-done.14.refs_5_ = bf16[1,32,4096]{2,1,0:T(8,128)(2,1)} collective-permute-done((bf16[1,32,4096]{2,1,0:T(8,128)(2,1)}, bf16[1,32,4096]{2,1,0:T(8,128)(2,1)}, u32[]{:S(2)}, u32[]{:S(2)}) %collective-permute-start.14) | collective-permute-done | bytes 262176 | tf_op jit(solution)/shard_map/ppermute | solution.py:91
  85.8 3.4 %shard_map.62 = bf16[16,32,512]{2,1,0:T(8,128)(2,1)S(1)} custom-call(s32[1]{0:T(128)} %bitcast.refs_0_, bf16[2,32,4096]{2,1,0:T(8,128)(2,1)S(1)} %collective-permute-done.9.refs_1_, bf16[2,32,4096]{2,1,0:T(8,128)(2,1)S(1)} %collective-permute-done.11.refs_2_, bf16[2,32,4096]{2,1,0:T(8,128)(2,1)S(1)} %collective-permute-done.12.refs_3_, ...), custom_call_target="tpu_custom_call" | custom-call | flops 1073741824 | bytes 10485760 | tf_op jit(solution)/shard_map/pallas_call | solution.py:165
  89.1 17.1 %all_to_all.5 = bf16[16,32,512]{2,1,0:T(8,128)(2,1)S(1)} all-to-all(bf16[16,32,512]{2,1,0:T(8,128)(2,1)S(1)} %shard_map.62), channel_id=1, replica_groups=mesh['layer'=16,'ex'=16] {'layer'}, dimensions={0} | all-to-all | bytes 1048576 | tf_op jit(solution)/shard_map/all_to_all | solution.py:225
  106.3 0.7 convert_reduce_fusion
  (20 shorter events, 0.1 us)
Async XLA Ops:
  4.3 22.8 %collective-permute-start = (bf16[2,32,4096]{2,1,0:T(8,128)(2,1)}, bf16[2,32,4096]{2,1,0:T(8,128)(2,1)S(1)}, u32[]{:S(2)}, u32[]{:S(2)}) collective-permute-start(bf16[2,32,4096]{2,1,0:T(8,128)(2,1)} %shard_map.55.refs_0_), channel_id=1, source_target_pairs={{0,4},{1,5},{2,6},{3,7},{4,8},{5,9},{6,10},{7,11},{8,12},{9,13},{1... | collective-permute-start | bytes 1572872 | tf_op jit(solution)/shard_map/ppermute | solution.py:91
  8.2 27.6 %collective-permute-start.1 = (bf16[2,32,4096]{2,1,0:T(8,128)(2,1)}, bf16[2,32,4096]{2,1,0:T(8,128)(2,1)S(1)}, u32[]{:S(2)}, u32[]{:S(2)}) collective-permute-start(bf16[2,32,4096]{2,1,0:T(8,128)(2,1)} %shard_map.55.refs_0_), channel_id=1, source_target_pairs={{0,12},{1,13},{2,14},{3,15},{4,0},{5,1},{6,2},{7,3},{8,4},{9,5},{1... | collective-permute-start | bytes 1572872 | tf_op jit(solution)/shard_map/ppermute | solution.py:91
  11.2 24.6 %collective-permute-start.2 = (bf16[2,32,4096]{2,1,0:T(8,128)(2,1)}, bf16[2,32,4096]{2,1,0:T(8,128)(2,1)S(1)}, u32[]{:S(2)}, u32[]{:S(2)}) collective-permute-start(bf16[2,32,4096]{2,1,0:T(8,128)(2,1)} %shard_map.55.refs_0_), channel_id=1, source_target_pairs={{0,1},{1,2},{2,3},{3,0},{4,5},{5,6},{6,7},{7,4},{8,9},{9,10},{10,1... | collective-permute-start | bytes 1572872 | tf_op jit(solution)/shard_map/ppermute | solution.py:91
  12.4 23.4 %collective-permute-start.3 = (bf16[2,32,4096]{2,1,0:T(8,128)(2,1)}, bf16[2,32,4096]{2,1,0:T(8,128)(2,1)S(1)}, u32[]{:S(2)}, u32[]{:S(2)}) collective-permute-start(bf16[2,32,4096]{2,1,0:T(8,128)(2,1)} %shard_map.55.refs_0_), channel_id=1, source_target_pairs={{0,3},{1,0},{2,1},{3,2},{4,7},{5,4},{6,5},{7,6},{8,11},{9,8},{10,9... | collective-permute-start | bytes 1572872 | tf_op jit(solution)/shard_map/ppermute | solution.py:91
  13.9 28.1 %collective-permute-start.6 = (bf16[2,32,4096]{2,1,0:T(8,128)(2,1)}, bf16[2,32,4096]{2,1,0:T(8,128)(2,1)S(1)}, u32[]{:S(2)}, u32[]{:S(2)}) collective-permute-start(bf16[2,32,4096]{2,1,0:T(8,128)(2,1)} %shard_map.55.refs_0_), channel_id=1, source_target_pairs={{0,2},{1,3},{2,0},{3,1},{4,6},{5,7},{6,4},{7,5},{8,10},{9,11},{10,... | collective-permute-start | bytes 1572872 | tf_op jit(solution)/shard_map/ppermute | solution.py:91
  35.9 23.8 %collective-permute-start.8 = (bf16[4,32,4096]{2,1,0:T(8,128)(2,1)S(1)}, bf16[4,32,4096]{2,1,0:T(8,128)(2,1)S(1)}, u32[]{:S(2)}, u32[]{:S(2)}) collective-permute-start(bf16[4,32,4096]{2,1,0:T(8,128)(2,1)S(1)} %get-tuple-element.38.refs_4_), channel_id=1, source_target_pairs={{0,3},{1,0},{2,1},{3,2},{4,7},{5,4},{6,5},{7,6},{8,11},{9,8},{10,9... | collective-permute-start | bytes 3145736 | tf_op jit(solution)/shard_map/ppermute | solution.py:91
  38.4 34.2 %collective-permute-start.10 = (bf16[4,32,4096]{2,1,0:T(8,128)(2,1)S(1)}, bf16[4,32,4096]{2,1,0:T(8,128)(2,1)S(1)}, u32[]{:S(2)}, u32[]{:S(2)}) collective-permute-start(bf16[4,32,4096]{2,1,0:T(8,128)(2,1)S(1)} %get-tuple-element.38.refs_4_), channel_id=1, source_target_pairs={{0,1},{1,2},{2,3},{3,0},{4,5},{5,6},{6,7},{7,4},{8,9},{9,10},{10,1... | collective-permute-start | bytes 3145736 | tf_op jit(solution)/shard_map/ppermute | solution.py:91
  38.4 10.4 %collective-permute-start.4 = (bf16[1,32,4096]{2,1,0:T(8,128)(2,1)S(1)}, bf16[1,32,4096]{2,1,0:T(8,128)(2,1)S(1)}, u32[]{:S(2)}, u32[]{:S(2)}) collective-permute-start(bf16[1,32,4096]{2,1,0:T(8,128)(2,1)S(1)} %get-tuple-element.34), channel_id=1, source_target_pairs={{0,4},{1,5},{2,6},{3,7},{4,8},{5,9},{6,10},{7,11},{8,12},{9,13},{1... | collective-permute-start | bytes 786440 | tf_op jit(solution)/shard_map/ppermute | solution.py:91
  41.3 7.5 %collective-permute-start.5 = (bf16[1,32,4096]{2,1,0:T(8,128)(2,1)S(1)}, bf16[1,32,4096]{2,1,0:T(8,128)(2,1)S(1)}, u32[]{:S(2)}, u32[]{:S(2)}) collective-permute-start(bf16[1,32,4096]{2,1,0:T(8,128)(2,1)S(1)} %get-tuple-element.35), channel_id=1, source_target_pairs={{0,12},{1,13},{2,14},{3,15},{4,0},{5,1},{6,2},{7,3},{8,4},{9,5},{1... | collective-permute-start | bytes 786440 | tf_op jit(solution)/shard_map/ppermute | solution.py:91
  42.0 3.4 %copy-start = (bf16[2,512,4096]{2,1,0:T(8,128)(2,1)S(1)}, bf16[2,512,4096]{2,1,0:T(8,128)(2,1)}, u32[]{:S(2)}) copy-start(bf16[2,512,4096]{2,1,0:T(8,128)(2,1)} %refs_2_.3) | copy-start | bytes 25165828
  45.4 1.0 copy-start.3
  46.4 15.2 %copy-start.1 = (bf16[2,512,4096]{2,1,0:T(8,128)(2,1)S(1)}, bf16[2,512,4096]{2,1,0:T(8,128)(2,1)}, u32[]{:S(2)}) copy-start(bf16[2,512,4096]{2,1,0:T(8,128)(2,1)} %refs_2_.3) | copy-start | bytes 25165828
  48.8 24.6 %copy-start.4 = (bf16[6,32,512]{2,1,0:T(8,128)(2,1)}, bf16[6,32,512]{2,1,0:T(8,128)(2,1)S(1)}, u32[]{:S(2)}) copy-start(bf16[6,32,512]{2,1,0:T(8,128)(2,1)S(1)} %shard_map.57.refs_7_) | copy-start | bytes 589828
  48.9 23.7 %collective-permute-start.11 = (bf16[2,32,4096]{2,1,0:T(8,128)(2,1)S(1)}, bf16[2,32,4096]{2,1,0:T(8,128)(2,1)S(1)}, u32[]{:S(2)}, u32[]{:S(2)}) collective-permute-start(bf16[2,32,4096]{2,1,0:T(8,128)(2,1)S(1)} %collective-permute-done.6.refs_3_), channel_id=1, source_target_pairs={{0,4},{1,5},{2,6},{3,7},{4,8},{5,9},{6,10},{7,11},{8,12},{9,13},{1... | collective-permute-start | bytes 1572872 | tf_op jit(solution)/shard_map/ppermute | solution.py:91
  53.4 19.2 %collective-permute-start.12 = (bf16[2,32,4096]{2,1,0:T(8,128)(2,1)S(1)}, bf16[2,32,4096]{2,1,0:T(8,128)(2,1)S(1)}, u32[]{:S(2)}, u32[]{:S(2)}) collective-permute-start(bf16[2,32,4096]{2,1,0:T(8,128)(2,1)S(1)} %collective-permute-done.6.refs_3_), channel_id=1, source_target_pairs={{0,12},{1,13},{2,14},{3,15},{4,0},{5,1},{6,2},{7,3},{8,4},{9,5},{1... | collective-permute-start | bytes 1572872 | tf_op jit(solution)/shard_map/ppermute | solution.py:91
  53.5 19.1 %collective-permute-start.7 = (bf16[2,32,4096]{2,1,0:T(8,128)(2,1)S(1)}, bf16[2,32,4096]{2,1,0:T(8,128)(2,1)S(1)}, u32[]{:S(2)}, u32[]{:S(2)}) collective-permute-start(bf16[2,32,4096]{2,1,0:T(8,128)(2,1)S(1)} %shard_map.58.refs_0_), channel_id=1, source_target_pairs={{0,1},{1,2},{2,3},{3,0},{4,5},{5,6},{6,7},{7,4},{8,9},{9,10},{10,1... | collective-permute-start | bytes 1572872 | tf_op jit(solution)/shard_map/ppermute | solution.py:91
  59.6 13.0 %collective-permute-start.9 = (bf16[2,32,4096]{2,1,0:T(8,128)(2,1)S(1)}, bf16[2,32,4096]{2,1,0:T(8,128)(2,1)S(1)}, u32[]{:S(2)}, u32[]{:S(2)}) collective-permute-start(bf16[2,32,4096]{2,1,0:T(8,128)(2,1)S(1)} %shard_map.58.refs_0_), channel_id=1, source_target_pairs={{0,3},{1,0},{2,1},{3,2},{4,7},{5,4},{6,5},{7,6},{8,11},{9,8},{10,9... | collective-permute-start | bytes 1572872 | tf_op jit(solution)/shard_map/ppermute | solution.py:91
  73.5 10.8 %collective-permute-start.13 = (bf16[1,32,4096]{2,1,0:T(8,128)(2,1)}, bf16[1,32,4096]{2,1,0:T(8,128)(2,1)S(1)}, u32[]{:S(2)}, u32[]{:S(2)}) collective-permute-start(bf16[1,32,4096]{2,1,0:T(8,128)(2,1)} %get-tuple-element.51), channel_id=1, source_target_pairs={{0,1},{1,2},{2,3},{3,0},{4,5},{5,6},{6,7},{7,4},{8,9},{9,10},{10,1... | collective-permute-start | bytes 786440 | tf_op jit(solution)/shard_map/ppermute | solution.py:91
  78.4 7.4 %collective-permute-start.14 = (bf16[1,32,4096]{2,1,0:T(8,128)(2,1)}, bf16[1,32,4096]{2,1,0:T(8,128)(2,1)}, u32[]{:S(2)}, u32[]{:S(2)}) collective-permute-start(bf16[1,32,4096]{2,1,0:T(8,128)(2,1)} %get-tuple-element.52), channel_id=1, source_target_pairs={{0,3},{1,0},{2,1},{3,2},{4,7},{5,4},{6,5},{7,6},{8,11},{9,8},{10,9... | collective-permute-start | bytes 786440 | tf_op jit(solution)/shard_map/ppermute | solution.py:91
  78.4 3.4 %copy-start.2 = (bf16[2,512,4096]{2,1,0:T(8,128)(2,1)S(1)}, bf16[2,512,4096]{2,1,0:T(8,128)(2,1)}, u32[]{:S(2)}) copy-start(bf16[2,512,4096]{2,1,0:T(8,128)(2,1)} %refs_2_.3) | copy-start | bytes 25165828
  81.8 4.0 %copy-start.5 = (bf16[6,32,512]{2,1,0:T(8,128)(2,1)S(1)}, bf16[6,32,512]{2,1,0:T(8,128)(2,1)}, u32[]{:S(2)}) copy-start(bf16[6,32,512]{2,1,0:T(8,128)(2,1)} %copy-done.4) | copy-start | bytes 589828

commit v4 on v3

--- a/solution.py
+++ b/solution.py
@@ -95,7 +95,11 @@
     return lax.optimization_barrier(values)
 
 
-def arrange(values, plan):
+def cost(weight):
+    return pl.CostEstimate(flops=int(weight * 1.1e9), bytes_accessed=1024, transcendentals=0)
+
+
+def arrange(values, plan, weight=0):
     def kernel(*refs):
         given, made = refs[: len(values)], refs[len(values) :]
         for out, parts in zip(made, plan):
@@ -109,9 +113,7 @@
         in_specs=[space] * len(values),
         out_specs=[space] * len(plan),
         compiler_params=pltpu.CompilerParams(vmem_limit_bytes=4 << 20),
-        cost_estimate=pl.CostEstimate(
-            flops=0, bytes_accessed=4 * values[0][0].size * sum(len(parts) for parts in plan), transcendentals=0
-        ),
+        cost_estimate=cost(weight),
     )(*values)
 
 
@@ -161,18 +163,13 @@
     number = lambda array: next(i for i, a in enumerate(arrays) if a is array)
     shards = [[(number(array), at) for array, at in shard] for shard in shards]
     space = pl.BlockSpec(memory_space=pltpu.VMEM)
-    rows = len(shards) * arrays[0].shape[1]
     return pl.pallas_call(
         functools.partial(kernel, shards, len(arrays)),
         out_shape=out_shapes,
         in_specs=[pl.BlockSpec(memory_space=pltpu.SMEM)] * len(lead) + [space] * (len(arrays) + 1 + len(others)),
         out_specs=jax.tree.map(lambda _: space, out_shapes),
         compiler_params=pltpu.CompilerParams(vmem_limit_bytes=16 << 20),
-        cost_estimate=pl.CostEstimate(
-            flops=2 * rows * train.size * weight,
-            bytes_accessed=2 * (train.size + rows * train.size // train.shape[1]),
-            transcendentals=0,
-        ),
+        cost_estimate=cost(weight),
     )(*lead, *arrays, train, *others)
 
 
@@ -191,14 +188,14 @@
     x2 = move(own, 0, 2)
     xr, xl = move(own, 0, -1), move(own, 0, 1)
     zr, zl = move(own, -1, 0), move(own, 1, 0)
-    zl, zr, xl, xr = in_order(zl, zr, xl, xr)
+    zl, zr = in_order(zl, zr)
     zl_half, zr_half, both = arrange([zl, zr], [[(0, 0)], [(1, 1)], [(0, 0), (0, 1), (1, 0), (1, 1)]])
     both_xr, both_xl = move(both, 0, -1), move(both, 0, 1)
     z2b, z2a = move(zr_half, -1, 0), move(zl_half, 1, 0)
     shards = [shard(own), shard(xl), shard(xr), shard(x2), shard(both, 0), shard(both, 2)]
-    first = score_call(next_kernel, shards, train_grads, blocks_shape(6, train_grads, queries), weight=4)
+    first = score_call(next_kernel, shards, train_grads, blocks_shape(6, train_grads, queries))
     z2a, z2b, x2, first = in_order(z2a, z2b, x2, first)
-    (z2,) = arrange([z2a, z2b], [[(0, 0), (1, 0)]])
+    (z2,) = arrange([z2a, z2b], [[(0, 0), (1, 0)]], weight=20)
     z2_xl = move(z2, 0, 1)
     zr_x2, zl_x2 = move(x2, -1, 0), move(x2, 1, 0)
     z2, both_xr = in_order(z2, both_xr)

time: 107 us -> 109 us (1.019)
  waiting for transfers between devices: 32.9 us -> 36.9 us
  starting transfers between devices: 32.3 us -> 29.3 us
    ppermute x15, waiting for transfers between devices: 32.9 us -> 36.9 us  [move(): lax.ppermute(value, 'ex', [(z * SIDE + x, to(z, x)) for z in range(SIDE)...]
    ppermute x15, starting transfers between devices: 32.3 us -> 29.3 us  [move(): lax.ppermute(value, 'ex', [(z * SIDE + x, to(z, x)) for z in range(SIDE)...]
    unnamed x12 -> x10, local copies, waits for them, and re-layouts: 7.82 us -> 7.81 us
where the time goes in v4:
time: 109 us; the launch traced here: 108 us
  waiting for transfers between devices  36.9 us (34%)
  starting transfers between devices  29.3 us (27%)
  blocking collectives  17.4 us (16%)
  Pallas kernels  16.1 us (15%)
  local copies, waits for them, and re-layouts  7.81 us (7%)
    ppermute x15, waiting for transfers between devices, move(): lax.ppermute(value, 'ex', [(z * SIDE + x, to(z, x)) for z in range(SIDE)...  36.9 us
    ppermute x15, starting transfers between devices, move(): lax.ppermute(value, 'ex', [(z * SIDE + x, to(z, x)) for z in range(SIDE)...  29.3 us
    all_to_all x1, blocking collectives, local(): lax.all_to_all(parts, 'layer', split_axis=0, concat_axis=0, tiled=True)  17.4 us
    pallas_call x4, Pallas kernels, score_call(): pl.pallas_call(functools.partial(kernel, shards, len(arrays)), out_shape=...  10.7 us
    unnamed x10, local copies, waits for them, and re-layouts  7.81 us
    pallas_call x1, Pallas kernels, precondition(): pl.pallas_call(precondition_kernel, out_shape=jax.ShapeDtypeStruct(raw.sh...  4.34 us
  transfers between devices with their start and end apart: 15, of which 5 were waited for; matrix products, arithmetic and copies ran while one was open for 0% of the time, Pallas kernels for 7%

profile of v4, /device:TPU:1, one launch (start us, length us, event | category | flops | bytes accessed | tf_op | source)
XLA Modules:
  0.0 108.3 jit_solution(6603194001905928677)
XLA Ops:
  0.0 4.3 %shard_map.55.refs_0_ = bf16[2,32,4096]{2,1,0:T(8,128)(2,1)} custom-call(bf16[2,32,4096]{2,1,0:T(8,128)(2,1)} %raw.1, f32[2,64,64]{2,1,0:T(8,128)} %basis_out.1, f32[2,64,64]{2,1,0:T(8,128)} %basis_in.1, f32[2,64,64]{2,1,0:T(8,128)} %eigen.1), custom_call_target="tpu_custom_call" | custom-call | tf_op jit(solution)/shard_map/pallas_call | solution.py:78
  4.3 3.8 %collective-permute-start = (bf16[2,32,4096]{2,1,0:T(8,128)(2,1)}, bf16[2,32,4096]{2,1,0:T(8,128)(2,1)S(1)}, u32[]{:S(2)}, u32[]{:S(2)}) collective-permute-start(bf16[2,32,4096]{2,1,0:T(8,128)(2,1)} %shard_map.55.refs_0_), channel_id=1, source_target_pairs={{0,4},{1,5},{2,6},{3,7},{4,8},{5,9},{6,10},{7,11},{8,12},{9,13},{1... | collective-permute-start | bytes 1572872 | tf_op jit(solution)/shard_map/ppermute | solution.py:91
  8.2 3.0 %collective-permute-start.1 = (bf16[2,32,4096]{2,1,0:T(8,128)(2,1)}, bf16[2,32,4096]{2,1,0:T(8,128)(2,1)S(1)}, u32[]{:S(2)}, u32[]{:S(2)}) collective-permute-start(bf16[2,32,4096]{2,1,0:T(8,128)(2,1)} %shard_map.55.refs_0_), channel_id=1, source_target_pairs={{0,12},{1,13},{2,14},{3,15},{4,0},{5,1},{6,2},{7,3},{8,4},{9,5},{1... | collective-permute-start | bytes 1572872 | tf_op jit(solution)/shard_map/ppermute | solution.py:91
  11.2 2.7 %collective-permute-start.4 = (bf16[2,32,4096]{2,1,0:T(8,128)(2,1)}, bf16[2,32,4096]{2,1,0:T(8,128)(2,1)S(1)}, u32[]{:S(2)}, u32[]{:S(2)}) collective-permute-start(bf16[2,32,4096]{2,1,0:T(8,128)(2,1)} %shard_map.55.refs_0_), channel_id=1, source_target_pairs={{0,2},{1,3},{2,0},{3,1},{4,6},{5,7},{6,4},{7,5},{8,10},{9,11},{10,... | collective-permute-start | bytes 1572872 | tf_op jit(solution)/shard_map/ppermute | solution.py:91
  13.9 0.3 collective-permute-start.5
  14.3 2.4 %collective-permute-start.6 = (bf16[2,32,4096]{2,1,0:T(8,128)(2,1)}, bf16[2,32,4096]{2,1,0:T(8,128)(2,1)S(1)}, u32[]{:S(2)}, u32[]{:S(2)}) collective-permute-start(bf16[2,32,4096]{2,1,0:T(8,128)(2,1)} %shard_map.55.refs_0_), channel_id=1, source_target_pairs={{0,3},{1,0},{2,1},{3,2},{4,7},{5,4},{6,5},{7,6},{8,11},{9,8},{10,9... | collective-permute-start | bytes 1572872 | tf_op jit(solution)/shard_map/ppermute | solution.py:91
  16.6 10.5 %collective-permute-done.refs_0_ = bf16[2,32,4096]{2,1,0:T(8,128)(2,1)S(1)} collective-permute-done((bf16[2,32,4096]{2,1,0:T(8,128)(2,1)}, bf16[2,32,4096]{2,1,0:T(8,128)(2,1)S(1)}, u32[]{:S(2)}, u32[]{:S(2)}) %collective-permute-start) | collective-permute-done | bytes 524320 | tf_op jit(solution)/shard_map/ppermute | solution.py:91
  27.1 8.6 %collective-permute-done.1.refs_1_ = bf16[2,32,4096]{2,1,0:T(8,128)(2,1)S(1)} collective-permute-done((bf16[2,32,4096]{2,1,0:T(8,128)(2,1)}, bf16[2,32,4096]{2,1,0:T(8,128)(2,1)S(1)}, u32[]{:S(2)}, u32[]{:S(2)}) %collective-permute-start.1) | collective-permute-done | bytes 524320 | tf_op jit(solution)/shard_map/ppermute | solution.py:91
  35.8 0.1 shard_map.56
  35.9 3.0 %collective-permute-start.2 = (bf16[1,32,4096]{2,1,0:T(8,128)(2,1)S(1)}, bf16[1,32,4096]{2,1,0:T(8,128)(2,1)S(1)}, u32[]{:S(2)}, u32[]{:S(2)}) collective-permute-start(bf16[1,32,4096]{2,1,0:T(8,128)(2,1)S(1)} %get-tuple-element.32), channel_id=1, source_target_pairs={{0,4},{1,5},{2,6},{3,7},{4,8},{5,9},{6,10},{7,11},{8,12},{9,13},{1... | collective-permute-start | bytes 786440 | tf_op jit(solution)/shard_map/ppermute | solution.py:91
  38.8 0.7 collective-permute-start.3
  39.5 2.5 %collective-permute-start.8 = (bf16[4,32,4096]{2,1,0:T(8,128)(2,1)S(1)}, bf16[4,32,4096]{2,1,0:T(8,128)(2,1)S(1)}, u32[]{:S(2)}, u32[]{:S(2)}) collective-permute-start(bf16[4,32,4096]{2,1,0:T(8,128)(2,1)S(1)} %get-tuple-element.34.refs_4_), channel_id=1, source_target_pairs={{0,3},{1,0},{2,1},{3,2},{4,7},{5,4},{6,5},{7,6},{8,11},{9,8},{10,9... | collective-permute-start | bytes 3145736 | tf_op jit(solution)/shard_map/ppermute | solution.py:91
  42.0 0.0 copy-start
  42.0 3.4 %copy-done = bf16[2,512,4096]{2,1,0:T(8,128)(2,1)S(1)} copy-done((bf16[2,512,4096]{2,1,0:T(8,128)(2,1)S(1)}, bf16[2,512,4096]{2,1,0:T(8,128)(2,1)}, u32[]{:S(2)}) %copy-start) | copy-done | bytes 8388632
  45.4 1.0 copy-done.2
  46.4 2.4 %shard_map.57.refs_7_ = bf16[6,32,512]{2,1,0:T(8,128)(2,1)S(1)} custom-call(bf16[2,32,4096]{2,1,0:T(8,128)(2,1)S(1)} %copy-done.2, bf16[2,32,4096]{2,1,0:T(8,128)(2,1)S(1)} %collective-permute-done.5.refs_1_, bf16[2,32,4096]{2,1,0:T(8,128)(2,1)S(1)} %collective-permute-done.6.refs_2_, bf16[2,32,4096]{2,1,0:T(8,128)(2,1)S(1)} %collective-permute-done.4.refs_3_, ...), custom_call_target="tpu_custom_call" | custom-call | flops 1100000000 | bytes 1024 | tf_op jit(solution)/shard_map/pallas_call | solution.py:166
  48.8 0.0 slice-start.1
  48.9 1.9 %collective-permute-done.2.refs_0_ = bf16[1,32,4096]{2,1,0:T(8,128)(2,1)S(1)} collective-permute-done((bf16[1,32,4096]{2,1,0:T(8,128)(2,1)S(1)}, bf16[1,32,4096]{2,1,0:T(8,128)(2,1)S(1)}, u32[]{:S(2)}, u32[]{:S(2)}) %collective-permute-start.2) | collective-permute-done | bytes 262176 | tf_op jit(solution)/shard_map/ppermute | solution.py:91
  50.7 2.7 %collective-permute-start.11 = (bf16[2,32,4096]{2,1,0:T(8,128)(2,1)S(1)}, bf16[2,32,4096]{2,1,0:T(8,128)(2,1)S(1)}, u32[]{:S(2)}, u32[]{:S(2)}) collective-permute-start(bf16[2,32,4096]{2,1,0:T(8,128)(2,1)S(1)} %collective-permute-done.4.refs_3_), channel_id=1, source_target_pairs={{0,4},{1,5},{2,6},{3,7},{4,8},{5,9},{6,10},{7,11},{8,12},{9,13},{1... | collective-permute-start | bytes 1572872 | tf_op jit(solution)/shard_map/ppermute | solution.py:91
  53.4 0.9 collective-permute-start.12
  54.3 1.3 %collective-permute-start.7 = (bf16[2,32,4096]{2,1,0:T(8,128)(2,1)S(1)}, bf16[2,32,4096]{2,1,0:T(8,128)(2,1)S(1)}, u32[]{:S(2)}, u32[]{:S(2)}) collective-permute-start(bf16[2,32,4096]{2,1,0:T(8,128)(2,1)S(1)} %shard_map.58.refs_0_), channel_id=1, source_target_pairs={{0,1},{1,2},{2,3},{3,0},{4,5},{5,6},{6,7},{7,4},{8,9},{9,10},{10,1... | collective-permute-start | bytes 1572872 | tf_op jit(solution)/shard_map/ppermute | solution.py:91
  55.6 7.3 %collective-permute-done.8.refs_1_ = bf16[4,32,4096]{2,1,0:T(8,128)(2,1)S(1)} collective-permute-done((bf16[4,32,4096]{2,1,0:T(8,128)(2,1)S(1)}, bf16[4,32,4096]{2,1,0:T(8,128)(2,1)S(1)}, u32[]{:S(2)}, u32[]{:S(2)}) %collective-permute-start.8) | collective-permute-done | bytes 1048608 | tf_op jit(solution)/shard_map/ppermute | solution.py:91
  62.9 3.4 %collective-permute-start.9 = (bf16[2,32,4096]{2,1,0:T(8,128)(2,1)S(1)}, bf16[2,32,4096]{2,1,0:T(8,128)(2,1)S(1)}, u32[]{:S(2)}, u32[]{:S(2)}) collective-permute-start(bf16[2,32,4096]{2,1,0:T(8,128)(2,1)S(1)} %shard_map.58.refs_0_), channel_id=1, source_target_pairs={{0,3},{1,0},{2,1},{3,2},{4,7},{5,4},{6,5},{7,6},{8,11},{9,8},{10,9... | collective-permute-start | bytes 1572872 | tf_op jit(solution)/shard_map/ppermute | solution.py:91
  66.3 2.4 %shard_map.59.refs_8_ = bf16[3,32,512]{2,1,0:T(8,128)(2,1)S(1)} custom-call(bf16[2,32,4096]{2,1,0:T(8,128)(2,1)S(1)} %shard_map.58.refs_0_, bf16[4,32,4096]{2,1,0:T(8,128)(2,1)S(1)} %collective-permute-done.8.refs_1_, bf16[2,512,4096]{2,1,0:T(8,128)(2,1)S(1)} %bitcast.2), custom_call_target="tpu_custom_call" | custom-call | flops 1100000000 | bytes 1024 | tf_op jit(solution)/shard_map/pallas_call | solution.py:166
  68.7 8.6 %collective-permute-done.7.refs_0_ = bf16[2,32,4096]{2,1,0:T(8,128)(2,1)S(1)} collective-permute-done((bf16[2,32,4096]{2,1,0:T(8,128)(2,1)S(1)}, bf16[2,32,4096]{2,1,0:T(8,128)(2,1)S(1)}, u32[]{:S(2)}, u32[]{:S(2)}) %collective-permute-start.7) | collective-permute-done | bytes 524320 | tf_op jit(solution)/shard_map/ppermute | solution.py:91
  77.3 0.8 shard_map.61
  78.2 2.7 %collective-permute-start.14 = (bf16[1,32,4096]{2,1,0:T(8,128)(2,1)}, bf16[1,32,4096]{2,1,0:T(8,128)(2,1)}, u32[]{:S(2)}, u32[]{:S(2)}) collective-permute-start(bf16[1,32,4096]{2,1,0:T(8,128)(2,1)} %get-tuple-element.48), channel_id=1, source_target_pairs={{0,3},{1,0},{2,1},{3,2},{4,7},{5,4},{6,5},{7,6},{8,11},{9,8},{10,9... | collective-permute-start | bytes 786440 | tf_op jit(solution)/shard_map/ppermute | solution.py:91
  80.8 3.4 %copy-done.1 = bf16[2,512,4096]{2,1,0:T(8,128)(2,1)S(1)} copy-done((bf16[2,512,4096]{2,1,0:T(8,128)(2,1)S(1)}, bf16[2,512,4096]{2,1,0:T(8,128)(2,1)}, u32[]{:S(2)}) %copy-start.1) | copy-done | bytes 8388632
  84.2 2.5 %shard_map.60 = (bf16[3,32,512]{2,1,0:T(8,128)(2,1)S(1)}, bf16[2,512,4096]{2,1,0:T(8,128)(2,1)S(1)}) custom-call(bf16[2,32,4096]{2,1,0:T(8,128)(2,1)S(1)} %collective-permute-done.7.refs_0_, bf16[4,32,4096]{2,1,0:T(8,128)(2,1)S(1)} %collective-permute-done.10.refs_1_, bf16[2,512,4096]{2,1,0:T(8,128)(2,1)S(1)} %copy-done.1), custom_call_target="tpu_custom_call" | custom-call | flops 1100000000 | bytes 1024 | tf_op jit(solution)/shard_map/pallas_call | solution.py:166
  86.7 3.4 %shard_map.62 = bf16[16,32,512]{2,1,0:T(8,128)(2,1)S(1)} custom-call(s32[1]{0:T(128)} %bitcast.refs_0_, bf16[2,32,4096]{2,1,0:T(8,128)(2,1)S(1)} %collective-permute-done.9.refs_1_, bf16[2,32,4096]{2,1,0:T(8,128)(2,1)S(1)} %collective-permute-done.11.refs_2_, bf16[2,32,4096]{2,1,0:T(8,128)(2,1)S(1)} %collective-permute-done.12.refs_3_, ...), custom_call_target="tpu_custom_call" | custom-call | flops 1100000000 | bytes 1024 | tf_op jit(solution)/shard_map/pallas_call | solution.py:166
  90.2 17.4 %all_to_all.5 = bf16[16,32,512]{2,1,0:T(8,128)(2,1)S(1)} all-to-all(bf16[16,32,512]{2,1,0:T(8,128)(2,1)S(1)} %shard_map.62), channel_id=1, replica_groups=mesh['layer'=16,'ex'=16] {'layer'}, dimensions={0} | all-to-all | bytes 1048576 | tf_op jit(solution)/shard_map/all_to_all | solution.py:222
  107.6 0.7 convert_reduce_fusion
  (19 shorter events, 0.1 us)
Async XLA Ops:
  4.3 22.8 %collective-permute-start = (bf16[2,32,4096]{2,1,0:T(8,128)(2,1)}, bf16[2,32,4096]{2,1,0:T(8,128)(2,1)S(1)}, u32[]{:S(2)}, u32[]{:S(2)}) collective-permute-start(bf16[2,32,4096]{2,1,0:T(8,128)(2,1)} %shard_map.55.refs_0_), channel_id=1, source_target_pairs={{0,4},{1,5},{2,6},{3,7},{4,8},{5,9},{6,10},{7,11},{8,12},{9,13},{1... | collective-permute-start | bytes 1572872 | tf_op jit(solution)/shard_map/ppermute | solution.py:91
  8.2 27.6 %collective-permute-start.1 = (bf16[2,32,4096]{2,1,0:T(8,128)(2,1)}, bf16[2,32,4096]{2,1,0:T(8,128)(2,1)S(1)}, u32[]{:S(2)}, u32[]{:S(2)}) collective-permute-start(bf16[2,32,4096]{2,1,0:T(8,128)(2,1)} %shard_map.55.refs_0_), channel_id=1, source_target_pairs={{0,12},{1,13},{2,14},{3,15},{4,0},{5,1},{6,2},{7,3},{8,4},{9,5},{1... | collective-permute-start | bytes 1572872 | tf_op jit(solution)/shard_map/ppermute | solution.py:91
  11.2 28.3 %collective-permute-start.4 = (bf16[2,32,4096]{2,1,0:T(8,128)(2,1)}, bf16[2,32,4096]{2,1,0:T(8,128)(2,1)S(1)}, u32[]{:S(2)}, u32[]{:S(2)}) collective-permute-start(bf16[2,32,4096]{2,1,0:T(8,128)(2,1)} %shard_map.55.refs_0_), channel_id=1, source_target_pairs={{0,2},{1,3},{2,0},{3,1},{4,6},{5,7},{6,4},{7,5},{8,10},{9,11},{10,... | collective-permute-start | bytes 1572872 | tf_op jit(solution)/shard_map/ppermute | solution.py:91
  13.9 28.1 %collective-permute-start.5 = (bf16[2,32,4096]{2,1,0:T(8,128)(2,1)}, bf16[2,32,4096]{2,1,0:T(8,128)(2,1)S(1)}, u32[]{:S(2)}, u32[]{:S(2)}) collective-permute-start(bf16[2,32,4096]{2,1,0:T(8,128)(2,1)} %shard_map.55.refs_0_), channel_id=1, source_target_pairs={{0,1},{1,2},{2,3},{3,0},{4,5},{5,6},{6,7},{7,4},{8,9},{9,10},{10,1... | collective-permute-start | bytes 1572872 | tf_op jit(solution)/shard_map/ppermute | solution.py:91
  14.3 27.8 %collective-permute-start.6 = (bf16[2,32,4096]{2,1,0:T(8,128)(2,1)}, bf16[2,32,4096]{2,1,0:T(8,128)(2,1)S(1)}, u32[]{:S(2)}, u32[]{:S(2)}) collective-permute-start(bf16[2,32,4096]{2,1,0:T(8,128)(2,1)} %shard_map.55.refs_0_), channel_id=1, source_target_pairs={{0,3},{1,0},{2,1},{3,2},{4,7},{5,4},{6,5},{7,6},{8,11},{9,8},{10,9... | collective-permute-start | bytes 1572872 | tf_op jit(solution)/shard_map/ppermute | solution.py:91
  35.9 14.9 %collective-permute-start.2 = (bf16[1,32,4096]{2,1,0:T(8,128)(2,1)S(1)}, bf16[1,32,4096]{2,1,0:T(8,128)(2,1)S(1)}, u32[]{:S(2)}, u32[]{:S(2)}) collective-permute-start(bf16[1,32,4096]{2,1,0:T(8,128)(2,1)S(1)} %get-tuple-element.32), channel_id=1, source_target_pairs={{0,4},{1,5},{2,6},{3,7},{4,8},{5,9},{6,10},{7,11},{8,12},{9,13},{1... | collective-permute-start | bytes 786440 | tf_op jit(solution)/shard_map/ppermute | solution.py:91
  38.8 11.9 %collective-permute-start.3 = (bf16[1,32,4096]{2,1,0:T(8,128)(2,1)S(1)}, bf16[1,32,4096]{2,1,0:T(8,128)(2,1)S(1)}, u32[]{:S(2)}, u32[]{:S(2)}) collective-permute-start(bf16[1,32,4096]{2,1,0:T(8,128)(2,1)S(1)} %get-tuple-element.33), channel_id=1, source_target_pairs={{0,12},{1,13},{2,14},{3,15},{4,0},{5,1},{6,2},{7,3},{8,4},{9,5},{1... | collective-permute-start | bytes 786440 | tf_op jit(solution)/shard_map/ppermute | solution.py:91
  39.5 23.4 %collective-permute-start.8 = (bf16[4,32,4096]{2,1,0:T(8,128)(2,1)S(1)}, bf16[4,32,4096]{2,1,0:T(8,128)(2,1)S(1)}, u32[]{:S(2)}, u32[]{:S(2)}) collective-permute-start(bf16[4,32,4096]{2,1,0:T(8,128)(2,1)S(1)} %get-tuple-element.34.refs_4_), channel_id=1, source_target_pairs={{0,3},{1,0},{2,1},{3,2},{4,7},{5,4},{6,5},{7,6},{8,11},{9,8},{10,9... | collective-permute-start | bytes 3145736 | tf_op jit(solution)/shard_map/ppermute | solution.py:91
  42.0 35.3 %collective-permute-start.10 = (bf16[4,32,4096]{2,1,0:T(8,128)(2,1)S(1)}, bf16[4,32,4096]{2,1,0:T(8,128)(2,1)S(1)}, u32[]{:S(2)}, u32[]{:S(2)}) collective-permute-start(bf16[4,32,4096]{2,1,0:T(8,128)(2,1)S(1)} %get-tuple-element.34.refs_4_), channel_id=1, source_target_pairs={{0,1},{1,2},{2,3},{3,0},{4,5},{5,6},{6,7},{7,4},{8,9},{9,10},{10,1... | collective-permute-start | bytes 3145736 | tf_op jit(solution)/shard_map/ppermute | solution.py:91
  42.0 3.4 %copy-start = (bf16[2,512,4096]{2,1,0:T(8,128)(2,1)S(1)}, bf16[2,512,4096]{2,1,0:T(8,128)(2,1)}, u32[]{:S(2)}) copy-start(bf16[2,512,4096]{2,1,0:T(8,128)(2,1)} %refs_2_.3) | copy-start | bytes 25165828
  45.4 1.0 copy-start.2
  46.4 19.9 %slice-start = ((s8[8388608]{0:T(1024)(128)(4,1)}), s8[4194304]{0:T(1024)(128)(4,1)S(1)}, s32[]{:S(2)}) async-start(s8[8388608]{0:T(1024)(128)(4,1)} %bitcast.1), calls=%async_computation.1 | async-start | bytes 8388608
  48.8 17.5 %slice-start.1 = ((s8[8388608]{0:T(1024)(128)(4,1)}), s8[4194304]{0:T(1024)(128)(4,1)S(1)}, s32[]{:S(2)}) async-start(s8[8388608]{0:T(1024)(128)(4,1)} %bitcast.1), calls=%async_computation.2 | async-start | bytes 8388608
  50.7 26.6 %collective-permute-start.11 = (bf16[2,32,4096]{2,1,0:T(8,128)(2,1)S(1)}, bf16[2,32,4096]{2,1,0:T(8,128)(2,1)S(1)}, u32[]{:S(2)}, u32[]{:S(2)}) collective-permute-start(bf16[2,32,4096]{2,1,0:T(8,128)(2,1)S(1)} %collective-permute-done.4.refs_3_), channel_id=1, source_target_pairs={{0,4},{1,5},{2,6},{3,7},{4,8},{5,9},{6,10},{7,11},{8,12},{9,13},{1... | collective-permute-start | bytes 1572872 | tf_op jit(solution)/shard_map/ppermute | solution.py:91
  53.4 23.9 %collective-permute-start.12 = (bf16[2,32,4096]{2,1,0:T(8,128)(2,1)S(1)}, bf16[2,32,4096]{2,1,0:T(8,128)(2,1)S(1)}, u32[]{:S(2)}, u32[]{:S(2)}) collective-permute-start(bf16[2,32,4096]{2,1,0:T(8,128)(2,1)S(1)} %collective-permute-done.4.refs_3_), channel_id=1, source_target_pairs={{0,12},{1,13},{2,14},{3,15},{4,0},{5,1},{6,2},{7,3},{8,4},{9,5},{1... | collective-permute-start | bytes 1572872 | tf_op jit(solution)/shard_map/ppermute | solution.py:91
  54.3 22.9 %collective-permute-start.7 = (bf16[2,32,4096]{2,1,0:T(8,128)(2,1)S(1)}, bf16[2,32,4096]{2,1,0:T(8,128)(2,1)S(1)}, u32[]{:S(2)}, u32[]{:S(2)}) collective-permute-start(bf16[2,32,4096]{2,1,0:T(8,128)(2,1)S(1)} %shard_map.58.refs_0_), channel_id=1, source_target_pairs={{0,1},{1,2},{2,3},{3,0},{4,5},{5,6},{6,7},{7,4},{8,9},{9,10},{10,1... | collective-permute-start | bytes 1572872 | tf_op jit(solution)/shard_map/ppermute | solution.py:91
  62.9 14.4 %collective-permute-start.9 = (bf16[2,32,4096]{2,1,0:T(8,128)(2,1)S(1)}, bf16[2,32,4096]{2,1,0:T(8,128)(2,1)S(1)}, u32[]{:S(2)}, u32[]{:S(2)}) collective-permute-start(bf16[2,32,4096]{2,1,0:T(8,128)(2,1)S(1)} %shard_map.58.refs_0_), channel_id=1, source_target_pairs={{0,3},{1,0},{2,1},{3,2},{4,7},{5,4},{6,5},{7,6},{8,11},{9,8},{10,9... | collective-permute-start | bytes 1572872 | tf_op jit(solution)/shard_map/ppermute | solution.py:91
  78.2 8.6 %collective-permute-start.13 = (bf16[1,32,4096]{2,1,0:T(8,128)(2,1)}, bf16[1,32,4096]{2,1,0:T(8,128)(2,1)}, u32[]{:S(2)}, u32[]{:S(2)}) collective-permute-start(bf16[1,32,4096]{2,1,0:T(8,128)(2,1)} %get-tuple-element.47), channel_id=1, source_target_pairs={{0,1},{1,2},{2,3},{3,0},{4,5},{5,6},{6,7},{7,4},{8,9},{9,10},{10,1... | collective-permute-start | bytes 786440 | tf_op jit(solution)/shard_map/ppermute | solution.py:91
  78.2 8.6 %collective-permute-start.14 = (bf16[1,32,4096]{2,1,0:T(8,128)(2,1)}, bf16[1,32,4096]{2,1,0:T(8,128)(2,1)}, u32[]{:S(2)}, u32[]{:S(2)}) collective-permute-start(bf16[1,32,4096]{2,1,0:T(8,128)(2,1)} %get-tuple-element.48), channel_id=1, source_target_pairs={{0,3},{1,0},{2,1},{3,2},{4,7},{5,4},{6,5},{7,6},{8,11},{9,8},{10,9... | collective-permute-start | bytes 786440 | tf_op jit(solution)/shard_map/ppermute | solution.py:91
  80.8 3.4 %copy-start.1 = (bf16[2,512,4096]{2,1,0:T(8,128)(2,1)S(1)}, bf16[2,512,4096]{2,1,0:T(8,128)(2,1)}, u32[]{:S(2)}) copy-start(bf16[2,512,4096]{2,1,0:T(8,128)(2,1)} %refs_2_.3) | copy-start | bytes 25165828

commit v5 on v4

--- a/solution.py
+++ b/solution.py
@@ -136,23 +136,19 @@
     out[...] = blocks_of(shards, held, train, out.dtype)
 
 
-def keep_kernel(shards, count, *refs):
-    held, (train, out, kept) = refs[:count], refs[count:]
-    out[...] = blocks_of(shards, held, train, out.dtype, kept)
-
-
 def last_kernel(shards, count, offsets, me, *refs):
-    held, train, done, out = refs[:count], refs[count], refs[count + 1 : -1], refs[-1]
+    held, train, done, (keep, give) = refs[:count], refs[count], refs[count + 1 : -2], refs[-2:]
     z, x = lax.shift_right_logical(me[0], 2), me[0] & (SIDE - 1)
-    places = [((z + dz) & (SIDE - 1)) * SIDE + ((x + dx) & (SIDE - 1)) for dz, dx in offsets]
-    at = 0
-    for ref in done:
-        for i in range(ref.shape[0]):
-            out[places[at]] = ref[i]
-            at += 1
-    blocks = blocks_of(shards, held, train, out.dtype)
-    for i in range(len(shards)):
-        out[places[at + i]] = blocks[i]
+    places = [((z + dz) & (SIDE - 1)) * (SIDE // 2) + lax.shift_right_logical((x + dx) & (SIDE - 1), 1) for dz, dx in offsets]
+    blocks = [(ref, i) for ref in done for i in range(ref.shape[0])]
+    total = blocks_of(shards, held, train, keep.dtype)
+    blocks += [(total, i) for i in range(len(shards))]
+    for core in range(2):
+
+        @pl.when(((x ^ me[1]) & 1) == core)
+        def _():
+            for (block, i), place, (_, dx) in zip(blocks, places, offsets):
+                (keep if dx % 2 == core else give)[place] = block[i]
 
 
 def score_call(kernel, shards, train, out_shapes, others=(), lead=(), weight=1):
@@ -178,11 +174,11 @@
 
 
 def blocks_shape(count, train, queries):
-    return jax.ShapeDtypeStruct((count, queries, train.shape[1]), jnp.bfloat16)
+    return jax.ShapeDtypeStruct((count, queries, train.shape[1]), jnp.float32)
 
 
 def local(query_grads, train_grads, basis_out, basis_in, eigen):
-    me = lax.axis_index("ex").astype(jnp.int32).reshape(1)
+    me = jnp.stack([lax.axis_index("ex"), lax.axis_index("layer")]).astype(jnp.int32)
     queries = query_grads.shape[1]
     own = precondition(query_grads, basis_out, basis_in, eigen)
     x2 = move(own, 0, 2)
@@ -212,14 +208,18 @@
         (2, 1), (-1, 2), (1, 2), (2, 2),
     ]
     shards = [shard(z2_xl), shard(both_xl, 0), shard(both_xl, 2)]
-    shapes = [blocks_shape(3, train_grads, queries), jax.ShapeDtypeStruct(train_grads.shape, train_grads.dtype)]
-    third, train = score_call(keep_kernel, shards, train_grads, shapes)
-    third, train, *z2_x2 = in_order(third, train, *z2_x2)
+    third = score_call(next_kernel, shards, train_grads, blocks_shape(3, train_grads, queries))
+    third, *z2_x2 = in_order(third, *z2_x2)
     shards = [shard(z2_xr), shard(zl_x2), shard(zr_x2), [(half, 0) for half in z2_x2]]
     kernel = lambda own, count, *refs: last_kernel(own, count, offsets, *refs)
-    shape = blocks_shape(SIDE * SIDE, train_grads, queries)
-    parts = score_call(kernel, shards, train, shape, [first, second, third], [me])
-    parts = lax.all_to_all(parts, "layer", split_axis=0, concat_axis=0, tiled=True)
+    shapes = [blocks_shape(SIDE * SIDE // 2, train_grads, queries)] * 2
+    keep, give = score_call(kernel, shards, train_grads, shapes, [first, second, third], [me])
+    count = lax.axis_size("layer")
+    parts = keep + lax.ppermute(give, "layer", [(i, i ^ 1) for i in range(count)])
+    groups = [list(range(core, count, 2)) for core in range(2)]
+    parts = lax.all_to_all(
+        parts.astype(jnp.bfloat16), "layer", split_axis=0, concat_axis=0, tiled=True, axis_index_groups=groups
+    )
     return jnp.sum(parts.astype(jnp.float32), axis=0)
 
 

time: 109 us -> 107 us (0.982)
  blocking collectives: 17.4 us -> 10.2 us
  starting transfers between devices: 29.3 us -> 32.7 us
  waiting for transfers between devices: 36.9 us -> 38.4 us
    all_to_all x1, blocking collectives: 17.4 us -> 10.2 us  [local(): lax.all_to_all(parts.astype(jnp.bfloat16), 'layer', split_axis=0, concat_...]
    ppermute x0 -> x1, starting transfers between devices: none -> 3.35 us  [local(): lax.ppermute(give, 'layer', [(i, i ^ 1) for i in range(count)])]
    ppermute x0 -> x1, waiting for transfers between devices: none -> 1.54 us  [local(): lax.ppermute(give, 'layer', [(i, i ^ 1) for i in range(count)])]
    unnamed x10 -> x14, local copies, waits for them, and re-layouts: 7.81 us -> 8.62 us
  transfers between devices with their start and end apart: 15 -> 16, of which waited for: 5 -> 6; matrix products, arithmetic and copies ran while one was open for 0% -> 0% of each run, Pallas kernels for 7% -> 7%
where the time goes in v5:
time: 107 us
  waiting for transfers between devices  38.4 us (36%)
  starting transfers between devices  32.7 us (31%)
  Pallas kernels  15.9 us (15%)
  blocking collectives  10.2 us (10%)
  local copies, waits for them, and re-layouts  8.62 us (8%)
    ppermute x15, waiting for transfers between devices, move(): lax.ppermute(value, 'ex', [(z * SIDE + x, to(z, x)) for z in range(SIDE)...  36.9 us
    ppermute x15, starting transfers between devices, move(): lax.ppermute(value, 'ex', [(z * SIDE + x, to(z, x)) for z in range(SIDE)...  29.3 us
    pallas_call x4, Pallas kernels, score_call(): pl.pallas_call(functools.partial(kernel, shards, len(arrays)), out_shape=...  10.6 us
    all_to_all x1, blocking collectives, local(): lax.all_to_all(parts.astype(jnp.bfloat16), 'layer', split_axis=0, concat_...  10.2 us
    unnamed x14, local copies, waits for them, and re-layouts  8.62 us
    pallas_call x1, Pallas kernels, precondition(): pl.pallas_call(precondition_kernel, out_shape=jax.ShapeDtypeStruct(raw.sh...  4.34 us
    ppermute x1, starting transfers between devices, local(): lax.ppermute(give, 'layer', [(i, i ^ 1) for i in range(count)])  3.35 us
  transfers between devices with their start and end apart: 16, of which 6 were waited for; matrix products, arithmetic and copies ran while one was open for 0% of the time, Pallas kernels for 7%

profile of v5, /device:TPU:1, one launch (start us, length us, event | category | flops | bytes accessed | tf_op | source)
XLA Modules:
  0.0 106.8 jit_solution(9548921109425533047)
XLA Ops:
  0.0 4.3 %shard_map.55.refs_0_ = bf16[2,32,4096]{2,1,0:T(8,128)(2,1)} custom-call(bf16[2,32,4096]{2,1,0:T(8,128)(2,1)} %raw.1, f32[2,64,64]{2,1,0:T(8,128)} %basis_out.1, f32[2,64,64]{2,1,0:T(8,128)} %basis_in.1, f32[2,64,64]{2,1,0:T(8,128)} %eigen.1), custom_call_target="tpu_custom_call" | custom-call | tf_op jit(solution)/shard_map/pallas_call | solution.py:78
  4.3 3.8 %collective-permute-start = (bf16[2,32,4096]{2,1,0:T(8,128)(2,1)}, bf16[2,32,4096]{2,1,0:T(8,128)(2,1)S(1)}, u32[]{:S(2)}, u32[]{:S(2)}) collective-permute-start(bf16[2,32,4096]{2,1,0:T(8,128)(2,1)} %shard_map.55.refs_0_), channel_id=1, source_target_pairs={{0,4},{1,5},{2,6},{3,7},{4,8},{5,9},{6,10},{7,11},{8,12},{9,13},{1... | collective-permute-start | bytes 1572872 | tf_op jit(solution)/shard_map/ppermute | solution.py:91
  8.2 3.0 %collective-permute-start.1 = (bf16[2,32,4096]{2,1,0:T(8,128)(2,1)}, bf16[2,32,4096]{2,1,0:T(8,128)(2,1)S(1)}, u32[]{:S(2)}, u32[]{:S(2)}) collective-permute-start(bf16[2,32,4096]{2,1,0:T(8,128)(2,1)} %shard_map.55.refs_0_), channel_id=1, source_target_pairs={{0,12},{1,13},{2,14},{3,15},{4,0},{5,1},{6,2},{7,3},{8,4},{9,5},{1... | collective-permute-start | bytes 1572872 | tf_op jit(solution)/shard_map/ppermute | solution.py:91
  11.2 2.7 %collective-permute-start.4 = (bf16[2,32,4096]{2,1,0:T(8,128)(2,1)}, bf16[2,32,4096]{2,1,0:T(8,128)(2,1)S(1)}, u32[]{:S(2)}, u32[]{:S(2)}) collective-permute-start(bf16[2,32,4096]{2,1,0:T(8,128)(2,1)} %shard_map.55.refs_0_), channel_id=1, source_target_pairs={{0,2},{1,3},{2,0},{3,1},{4,6},{5,7},{6,4},{7,5},{8,10},{9,11},{10,... | collective-permute-start | bytes 1572872 | tf_op jit(solution)/shard_map/ppermute | solution.py:91
  13.9 0.3 collective-permute-start.5
  14.2 2.4 %collective-permute-start.6 = (bf16[2,32,4096]{2,1,0:T(8,128)(2,1)}, bf16[2,32,4096]{2,1,0:T(8,128)(2,1)S(1)}, u32[]{:S(2)}, u32[]{:S(2)}) collective-permute-start(bf16[2,32,4096]{2,1,0:T(8,128)(2,1)} %shard_map.55.refs_0_), channel_id=1, source_target_pairs={{0,3},{1,0},{2,1},{3,2},{4,7},{5,4},{6,5},{7,6},{8,11},{9,8},{10,9... | collective-permute-start | bytes 1572872 | tf_op jit(solution)/shard_map/ppermute | solution.py:91
  16.6 10.5 %collective-permute-done.refs_0_ = bf16[2,32,4096]{2,1,0:T(8,128)(2,1)S(1)} collective-permute-done((bf16[2,32,4096]{2,1,0:T(8,128)(2,1)}, bf16[2,32,4096]{2,1,0:T(8,128)(2,1)S(1)}, u32[]{:S(2)}, u32[]{:S(2)}) %collective-permute-start) | collective-permute-done | bytes 524320 | tf_op jit(solution)/shard_map/ppermute | solution.py:91
  27.1 8.6 %collective-permute-done.1.refs_1_ = bf16[2,32,4096]{2,1,0:T(8,128)(2,1)S(1)} collective-permute-done((bf16[2,32,4096]{2,1,0:T(8,128)(2,1)}, bf16[2,32,4096]{2,1,0:T(8,128)(2,1)S(1)}, u32[]{:S(2)}, u32[]{:S(2)}) %collective-permute-start.1) | collective-permute-done | bytes 524320 | tf_op jit(solution)/shard_map/ppermute | solution.py:91
  35.9 3.0 %collective-permute-start.2 = (bf16[1,32,4096]{2,1,0:T(8,128)(2,1)S(1)}, bf16[1,32,4096]{2,1,0:T(8,128)(2,1)S(1)}, u32[]{:S(2)}, u32[]{:S(2)}) collective-permute-start(bf16[1,32,4096]{2,1,0:T(8,128)(2,1)S(1)} %get-tuple-element.31), channel_id=1, source_target_pairs={{0,4},{1,5},{2,6},{3,7},{4,8},{5,9},{6,10},{7,11},{8,12},{9,13},{1... | collective-permute-start | bytes 786440 | tf_op jit(solution)/shard_map/ppermute | solution.py:91
  38.8 0.7 collective-permute-start.3
  39.5 2.5 %collective-permute-start.8 = (bf16[4,32,4096]{2,1,0:T(8,128)(2,1)S(1)}, bf16[4,32,4096]{2,1,0:T(8,128)(2,1)S(1)}, u32[]{:S(2)}, u32[]{:S(2)}) collective-permute-start(bf16[4,32,4096]{2,1,0:T(8,128)(2,1)S(1)} %get-tuple-element.33.refs_4_), channel_id=1, source_target_pairs={{0,3},{1,0},{2,1},{3,2},{4,7},{5,4},{6,5},{7,6},{8,11},{9,8},{10,9... | collective-permute-start | bytes 3145736 | tf_op jit(solution)/shard_map/ppermute | solution.py:91
  42.0 3.4 %copy-done = bf16[2,512,4096]{2,1,0:T(8,128)(2,1)S(1)} copy-done((bf16[2,512,4096]{2,1,0:T(8,128)(2,1)S(1)}, bf16[2,512,4096]{2,1,0:T(8,128)(2,1)}, u32[]{:S(2)}) %copy-start) | copy-done | bytes 8388632
  45.4 1.0 copy-done.2
  46.4 2.4 %shard_map.57.refs_7_ = f32[6,32,512]{2,1,0:T(8,128)S(1)} custom-call(bf16[2,32,4096]{2,1,0:T(8,128)(2,1)S(1)} %copy-done.2, bf16[2,32,4096]{2,1,0:T(8,128)(2,1)S(1)} %collective-permute-done.5.refs_1_, bf16[2,32,4096]{2,1,0:T(8,128)(2,1)S(1)} %collective-permute-done.6.refs_2_, bf16[2,32,4096]{2,1,0:T(8,128)(2,1)S(1)} %collective-permute-done.4.refs_3_, ...), custom_call_target="tpu_custom_call" | custom-call | flops 1100000000 | bytes 1024 | tf_op jit(solution)/shard_map/pallas_call | solution.py:162
  48.8 1.9 %collective-permute-done.2.refs_0_ = bf16[1,32,4096]{2,1,0:T(8,128)(2,1)S(1)} collective-permute-done((bf16[1,32,4096]{2,1,0:T(8,128)(2,1)S(1)}, bf16[1,32,4096]{2,1,0:T(8,128)(2,1)S(1)}, u32[]{:S(2)}, u32[]{:S(2)}) %collective-permute-start.2) | collective-permute-done | bytes 262176 | tf_op jit(solution)/shard_map/ppermute | solution.py:91
  50.7 2.7 %collective-permute-start.11 = (bf16[2,32,4096]{2,1,0:T(8,128)(2,1)S(1)}, bf16[2,32,4096]{2,1,0:T(8,128)(2,1)S(1)}, u32[]{:S(2)}, u32[]{:S(2)}) collective-permute-start(bf16[2,32,4096]{2,1,0:T(8,128)(2,1)S(1)} %collective-permute-done.4.refs_3_), channel_id=1, source_target_pairs={{0,4},{1,5},{2,6},{3,7},{4,8},{5,9},{6,10},{7,11},{8,12},{9,13},{1... | collective-permute-start | bytes 1572872 | tf_op jit(solution)/shard_map/ppermute | solution.py:91
  53.4 0.9 collective-permute-start.12
  54.3 1.3 %collective-permute-start.7 = (bf16[2,32,4096]{2,1,0:T(8,128)(2,1)S(1)}, bf16[2,32,4096]{2,1,0:T(8,128)(2,1)S(1)}, u32[]{:S(2)}, u32[]{:S(2)}) collective-permute-start(bf16[2,32,4096]{2,1,0:T(8,128)(2,1)S(1)} %shard_map.58.refs_0_), channel_id=1, source_target_pairs={{0,1},{1,2},{2,3},{3,0},{4,5},{5,6},{6,7},{7,4},{8,9},{9,10},{10,1... | collective-permute-start | bytes 1572872 | tf_op jit(solution)/shard_map/ppermute | solution.py:91
  55.6 7.3 %collective-permute-done.8.refs_1_ = bf16[4,32,4096]{2,1,0:T(8,128)(2,1)S(1)} collective-permute-done((bf16[4,32,4096]{2,1,0:T(8,128)(2,1)S(1)}, bf16[4,32,4096]{2,1,0:T(8,128)(2,1)S(1)}, u32[]{:S(2)}, u32[]{:S(2)}) %collective-permute-start.8) | collective-permute-done | bytes 1048608 | tf_op jit(solution)/shard_map/ppermute | solution.py:91
  62.9 3.4 %collective-permute-start.9 = (bf16[2,32,4096]{2,1,0:T(8,128)(2,1)S(1)}, bf16[2,32,4096]{2,1,0:T(8,128)(2,1)S(1)}, u32[]{:S(2)}, u32[]{:S(2)}) collective-permute-start(bf16[2,32,4096]{2,1,0:T(8,128)(2,1)S(1)} %shard_map.58.refs_0_), channel_id=1, source_target_pairs={{0,3},{1,0},{2,1},{3,2},{4,7},{5,4},{6,5},{7,6},{8,11},{9,8},{10,9... | collective-permute-start | bytes 1572872 | tf_op jit(solution)/shard_map/ppermute | solution.py:91
  66.3 2.4 %shard_map.59.refs_8_ = f32[3,32,512]{2,1,0:T(8,128)S(1)} custom-call(bf16[2,32,4096]{2,1,0:T(8,128)(2,1)S(1)} %shard_map.58.refs_0_, bf16[4,32,4096]{2,1,0:T(8,128)(2,1)S(1)} %collective-permute-done.8.refs_1_, bf16[2,512,4096]{2,1,0:T(8,128)(2,1)S(1)} %bitcast.3), custom_call_target="tpu_custom_call" | custom-call | flops 1100000000 | bytes 1024 | tf_op jit(solution)/shard_map/pallas_call | solution.py:162
  68.7 8.6 %collective-permute-done.7.refs_0_ = bf16[2,32,4096]{2,1,0:T(8,128)(2,1)S(1)} collective-permute-done((bf16[2,32,4096]{2,1,0:T(8,128)(2,1)S(1)}, bf16[2,32,4096]{2,1,0:T(8,128)(2,1)S(1)}, u32[]{:S(2)}, u32[]{:S(2)}) %collective-permute-start.7) | collective-permute-done | bytes 524320 | tf_op jit(solution)/shard_map/ppermute | solution.py:91
  77.3 0.8 copy-done.3
  78.1 0.9 shard_map.61
  79.0 2.7 %collective-permute-start.14 = (bf16[1,32,4096]{2,1,0:T(8,128)(2,1)}, bf16[1,32,4096]{2,1,0:T(8,128)(2,1)}, u32[]{:S(2)}, u32[]{:S(2)}) collective-permute-start(bf16[1,32,4096]{2,1,0:T(8,128)(2,1)} %get-tuple-element.45), channel_id=1, source_target_pairs={{0,3},{1,0},{2,1},{3,2},{4,7},{5,4},{6,5},{7,6},{8,11},{9,8},{10,9... | collective-permute-start | bytes 786440 | tf_op jit(solution)/shard_map/ppermute | solution.py:91
  81.7 3.4 %copy-done.1 = bf16[2,512,4096]{2,1,0:T(8,128)(2,1)S(1)} copy-done((bf16[2,512,4096]{2,1,0:T(8,128)(2,1)S(1)}, bf16[2,512,4096]{2,1,0:T(8,128)(2,1)}, u32[]{:S(2)}) %copy-start.1) | copy-done | bytes 8388632
  85.1 2.4 %shard_map.60.refs_9_ = f32[3,32,512]{2,1,0:T(8,128)S(1)} custom-call(bf16[2,32,4096]{2,1,0:T(8,128)(2,1)S(1)} %collective-permute-done.7.refs_0_, bf16[4,32,4096]{2,1,0:T(8,128)(2,1)S(1)} %collective-permute-done.10.refs_1_, bf16[2,512,4096]{2,1,0:T(8,128)(2,1)S(1)} %copy-done.1), custom_call_target="tpu_custom_call" | custom-call | flops 1100000000 | bytes 1024 | tf_op jit(solution)/shard_map/pallas_call | solution.py:162
  87.5 3.4 %shard_map.62 = (f32[8,32,512]{2,1,0:T(8,128)S(1)}, f32[8,32,512]{2,1,0:T(8,128)S(1)}) custom-call(s32[2]{0:T(128)S(1)} %pad_add_fusion.refs_0_, bf16[2,32,4096]{2,1,0:T(8,128)(2,1)S(1)} %collective-permute-done.9.refs_1_, bf16[2,32,4096]{2,1,0:T(8,128)(2,1)S(1)} %collective-permute-done.11.refs_2_, bf16[2,32,4096]{2,1,0:T(8,128)(2,1)S(1)} %copy-done.4, ...), custom_call_target="tpu_custom_call" | custom-call | flops 1100000000 | bytes 1024 | tf_op jit(solution)/shard_map/pallas_call | solution.py:162
  90.9 3.4 %collective-permute-start.15 = (f32[8,32,512]{2,1,0:T(8,128)S(1)}, f32[8,32,512]{2,1,0:T(8,128)S(1)}, u32[]{:S(2)}, u32[]{:S(2)}) collective-permute-start(f32[8,32,512]{2,1,0:T(8,128)S(1)} %get-tuple-element.52), channel_id=1, source_target_pairs={{0,16},{16,0},{32,48},{48,32},{64,80},{80,64},{96,112},{112,96},{1... | collective-permute-start | bytes 1572872 | tf_op jit(solution)/shard_map/ppermute | solution.py:218
  94.3 1.5 %collective-permute-done.15 = f32[8,32,512]{2,1,0:T(8,128)S(1)} collective-permute-done((f32[8,32,512]{2,1,0:T(8,128)S(1)}, f32[8,32,512]{2,1,0:T(8,128)S(1)}, u32[]{:S(2)}, u32[]{:S(2)}) %collective-permute-start.15) | collective-permute-done | bytes 524320 | tf_op jit(solution)/shard_map/ppermute | solution.py:218
  95.9 10.2 %all_to_all.5 = bf16[8,32,512]{2,1,0:T(8,128)(2,1)S(1)} all-to-all(bf16[8,32,512]{2,1,0:T(8,128)(2,1)S(1)} %add_convert_fusion), channel_id=1, replica_groups={{0,32,64,96,128,160,192,224},{16,48,80,112,144,176,208,240},{1,33,65,97..., dimensions={0} | all-to-all | bytes 524288 | tf_op jit(solution)/shard_map/all_to_all | solution.py:220
  106.1 0.7 convert_reduce_fusion
  (27 shorter events, 0.4 us)
Async XLA Ops:
  4.3 22.8 %collective-permute-start = (bf16[2,32,4096]{2,1,0:T(8,128)(2,1)}, bf16[2,32,4096]{2,1,0:T(8,128)(2,1)S(1)}, u32[]{:S(2)}, u32[]{:S(2)}) collective-permute-start(bf16[2,32,4096]{2,1,0:T(8,128)(2,1)} %shard_map.55.refs_0_), channel_id=1, source_target_pairs={{0,4},{1,5},{2,6},{3,7},{4,8},{5,9},{6,10},{7,11},{8,12},{9,13},{1... | collective-permute-start | bytes 1572872 | tf_op jit(solution)/shard_map/ppermute | solution.py:91
  8.2 27.6 %collective-permute-start.1 = (bf16[2,32,4096]{2,1,0:T(8,128)(2,1)}, bf16[2,32,4096]{2,1,0:T(8,128)(2,1)S(1)}, u32[]{:S(2)}, u32[]{:S(2)}) collective-permute-start(bf16[2,32,4096]{2,1,0:T(8,128)(2,1)} %shard_map.55.refs_0_), channel_id=1, source_target_pairs={{0,12},{1,13},{2,14},{3,15},{4,0},{5,1},{6,2},{7,3},{8,4},{9,5},{1... | collective-permute-start | bytes 1572872 | tf_op jit(solution)/shard_map/ppermute | solution.py:91
  11.2 28.3 %collective-permute-start.4 = (bf16[2,32,4096]{2,1,0:T(8,128)(2,1)}, bf16[2,32,4096]{2,1,0:T(8,128)(2,1)S(1)}, u32[]{:S(2)}, u32[]{:S(2)}) collective-permute-start(bf16[2,32,4096]{2,1,0:T(8,128)(2,1)} %shard_map.55.refs_0_), channel_id=1, source_target_pairs={{0,2},{1,3},{2,0},{3,1},{4,6},{5,7},{6,4},{7,5},{8,10},{9,11},{10,... | collective-permute-start | bytes 1572872 | tf_op jit(solution)/shard_map/ppermute | solution.py:91
  13.9 28.1 %collective-permute-start.5 = (bf16[2,32,4096]{2,1,0:T(8,128)(2,1)}, bf16[2,32,4096]{2,1,0:T(8,128)(2,1)S(1)}, u32[]{:S(2)}, u32[]{:S(2)}) collective-permute-start(bf16[2,32,4096]{2,1,0:T(8,128)(2,1)} %shard_map.55.refs_0_), channel_id=1, source_target_pairs={{0,1},{1,2},{2,3},{3,0},{4,5},{5,6},{6,7},{7,4},{8,9},{9,10},{10,1... | collective-permute-start | bytes 1572872 | tf_op jit(solution)/shard_map/ppermute | solution.py:91
  14.2 27.8 %collective-permute-start.6 = (bf16[2,32,4096]{2,1,0:T(8,128)(2,1)}, bf16[2,32,4096]{2,1,0:T(8,128)(2,1)S(1)}, u32[]{:S(2)}, u32[]{:S(2)}) collective-permute-start(bf16[2,32,4096]{2,1,0:T(8,128)(2,1)} %shard_map.55.refs_0_), channel_id=1, source_target_pairs={{0,3},{1,0},{2,1},{3,2},{4,7},{5,4},{6,5},{7,6},{8,11},{9,8},{10,9... | collective-permute-start | bytes 1572872 | tf_op jit(solution)/shard_map/ppermute | solution.py:91
  35.9 14.9 %collective-permute-start.2 = (bf16[1,32,4096]{2,1,0:T(8,128)(2,1)S(1)}, bf16[1,32,4096]{2,1,0:T(8,128)(2,1)S(1)}, u32[]{:S(2)}, u32[]{:S(2)}) collective-permute-start(bf16[1,32,4096]{2,1,0:T(8,128)(2,1)S(1)} %get-tuple-element.31), channel_id=1, source_target_pairs={{0,4},{1,5},{2,6},{3,7},{4,8},{5,9},{6,10},{7,11},{8,12},{9,13},{1... | collective-permute-start | bytes 786440 | tf_op jit(solution)/shard_map/ppermute | solution.py:91
  38.8 11.9 %collective-permute-start.3 = (bf16[1,32,4096]{2,1,0:T(8,128)(2,1)S(1)}, bf16[1,32,4096]{2,1,0:T(8,128)(2,1)S(1)}, u32[]{:S(2)}, u32[]{:S(2)}) collective-permute-start(bf16[1,32,4096]{2,1,0:T(8,128)(2,1)S(1)} %get-tuple-element.32), channel_id=1, source_target_pairs={{0,12},{1,13},{2,14},{3,15},{4,0},{5,1},{6,2},{7,3},{8,4},{9,5},{1... | collective-permute-start | bytes 786440 | tf_op jit(solution)/shard_map/ppermute | solution.py:91
  39.5 23.4 %collective-permute-start.8 = (bf16[4,32,4096]{2,1,0:T(8,128)(2,1)S(1)}, bf16[4,32,4096]{2,1,0:T(8,128)(2,1)S(1)}, u32[]{:S(2)}, u32[]{:S(2)}) collective-permute-start(bf16[4,32,4096]{2,1,0:T(8,128)(2,1)S(1)} %get-tuple-element.33.refs_4_), channel_id=1, source_target_pairs={{0,3},{1,0},{2,1},{3,2},{4,7},{5,4},{6,5},{7,6},{8,11},{9,8},{10,9... | collective-permute-start | bytes 3145736 | tf_op jit(solution)/shard_map/ppermute | solution.py:91
  42.0 36.1 %collective-permute-start.10 = (bf16[4,32,4096]{2,1,0:T(8,128)(2,1)S(1)}, bf16[4,32,4096]{2,1,0:T(8,128)(2,1)S(1)}, u32[]{:S(2)}, u32[]{:S(2)}) collective-permute-start(bf16[4,32,4096]{2,1,0:T(8,128)(2,1)S(1)} %get-tuple-element.33.refs_4_), channel_id=1, source_target_pairs={{0,1},{1,2},{2,3},{3,0},{4,5},{5,6},{6,7},{7,4},{8,9},{9,10},{10,1... | collective-permute-start | bytes 3145736 | tf_op jit(solution)/shard_map/ppermute | solution.py:91
  42.0 3.4 %copy-start = (bf16[2,512,4096]{2,1,0:T(8,128)(2,1)S(1)}, bf16[2,512,4096]{2,1,0:T(8,128)(2,1)}, u32[]{:S(2)}) copy-start(bf16[2,512,4096]{2,1,0:T(8,128)(2,1)} %refs_6_.1) | copy-start | bytes 25165828
  45.4 1.0 copy-start.2
  46.4 19.9 %slice-start = ((s8[8388608]{0:T(1024)(128)(4,1)}), s8[4194304]{0:T(1024)(128)(4,1)S(1)}, s32[]{:S(2)}) async-start(s8[8388608]{0:T(1024)(128)(4,1)} %bitcast.2), calls=%async_computation.1 | async-start | bytes 8388608
  48.8 17.5 %slice-start.1 = ((s8[8388608]{0:T(1024)(128)(4,1)}), s8[4194304]{0:T(1024)(128)(4,1)S(1)}, s32[]{:S(2)}) async-start(s8[8388608]{0:T(1024)(128)(4,1)} %bitcast.2), calls=%async_computation.2 | async-start | bytes 8388608
  50.7 26.6 %collective-permute-start.11 = (bf16[2,32,4096]{2,1,0:T(8,128)(2,1)S(1)}, bf16[2,32,4096]{2,1,0:T(8,128)(2,1)S(1)}, u32[]{:S(2)}, u32[]{:S(2)}) collective-permute-start(bf16[2,32,4096]{2,1,0:T(8,128)(2,1)S(1)} %collective-permute-done.4.refs_3_), channel_id=1, source_target_pairs={{0,4},{1,5},{2,6},{3,7},{4,8},{5,9},{6,10},{7,11},{8,12},{9,13},{1... | collective-permute-start | bytes 1572872 | tf_op jit(solution)/shard_map/ppermute | solution.py:91
  53.4 23.9 %collective-permute-start.12 = (bf16[2,32,4096]{2,1,0:T(8,128)(2,1)S(1)}, bf16[2,32,4096]{2,1,0:T(8,128)(2,1)S(1)}, u32[]{:S(2)}, u32[]{:S(2)}) collective-permute-start(bf16[2,32,4096]{2,1,0:T(8,128)(2,1)S(1)} %collective-permute-done.4.refs_3_), channel_id=1, source_target_pairs={{0,12},{1,13},{2,14},{3,15},{4,0},{5,1},{6,2},{7,3},{8,4},{9,5},{1... | collective-permute-start | bytes 1572872 | tf_op jit(solution)/shard_map/ppermute | solution.py:91
  54.3 22.9 %collective-permute-start.7 = (bf16[2,32,4096]{2,1,0:T(8,128)(2,1)S(1)}, bf16[2,32,4096]{2,1,0:T(8,128)(2,1)S(1)}, u32[]{:S(2)}, u32[]{:S(2)}) collective-permute-start(bf16[2,32,4096]{2,1,0:T(8,128)(2,1)S(1)} %shard_map.58.refs_0_), channel_id=1, source_target_pairs={{0,1},{1,2},{2,3},{3,0},{4,5},{5,6},{6,7},{7,4},{8,9},{9,10},{10,1... | collective-permute-start | bytes 1572872 | tf_op jit(solution)/shard_map/ppermute | solution.py:91
  62.9 15.2 %collective-permute-start.9 = (bf16[2,32,4096]{2,1,0:T(8,128)(2,1)S(1)}, bf16[2,32,4096]{2,1,0:T(8,128)(2,1)S(1)}, u32[]{:S(2)}, u32[]{:S(2)}) collective-permute-start(bf16[2,32,4096]{2,1,0:T(8,128)(2,1)S(1)} %shard_map.58.refs_0_), channel_id=1, source_target_pairs={{0,3},{1,0},{2,1},{3,2},{4,7},{5,4},{6,5},{7,6},{8,11},{9,8},{10,9... | collective-permute-start | bytes 1572872 | tf_op jit(solution)/shard_map/ppermute | solution.py:91
  77.3 0.8 copy-start.3
  79.0 8.5 %collective-permute-start.13 = (bf16[1,32,4096]{2,1,0:T(8,128)(2,1)}, bf16[1,32,4096]{2,1,0:T(8,128)(2,1)S(1)}, u32[]{:S(2)}, u32[]{:S(2)}) collective-permute-start(bf16[1,32,4096]{2,1,0:T(8,128)(2,1)} %get-tuple-element.44), channel_id=1, source_target_pairs={{0,1},{1,2},{2,3},{3,0},{4,5},{5,6},{6,7},{7,4},{8,9},{9,10},{10,1... | collective-permute-start | bytes 786440 | tf_op jit(solution)/shard_map/ppermute | solution.py:91
  79.0 8.5 %collective-permute-start.14 = (bf16[1,32,4096]{2,1,0:T(8,128)(2,1)}, bf16[1,32,4096]{2,1,0:T(8,128)(2,1)}, u32[]{:S(2)}, u32[]{:S(2)}) collective-permute-start(bf16[1,32,4096]{2,1,0:T(8,128)(2,1)} %get-tuple-element.45), channel_id=1, source_target_pairs={{0,3},{1,0},{2,1},{3,2},{4,7},{5,4},{6,5},{7,6},{8,11},{9,8},{10,9... | collective-permute-start | bytes 786440 | tf_op jit(solution)/shard_map/ppermute | solution.py:91
  81.7 3.4 %copy-start.1 = (bf16[2,512,4096]{2,1,0:T(8,128)(2,1)S(1)}, bf16[2,512,4096]{2,1,0:T(8,128)(2,1)}, u32[]{:S(2)}) copy-start(bf16[2,512,4096]{2,1,0:T(8,128)(2,1)} %refs_6_.1) | copy-start | bytes 25165828
  85.1 2.4 %copy-start.4 = (bf16[2,32,4096]{2,1,0:T(8,128)(2,1)S(1)}, bf16[2,32,4096]{2,1,0:T(8,128)(2,1)}, u32[]{:S(2)}) copy-start(bf16[2,32,4096]{2,1,0:T(8,128)(2,1)} %copy-done.3) | copy-start | bytes 1572868
  90.9 4.9 %collective-permute-start.15 = (f32[8,32,512]{2,1,0:T(8,128)S(1)}, f32[8,32,512]{2,1,0:T(8,128)S(1)}, u32[]{:S(2)}, u32[]{:S(2)}) collective-permute-start(f32[8,32,512]{2,1,0:T(8,128)S(1)} %get-tuple-element.52), channel_id=1, source_target_pairs={{0,16},{16,0},{32,48},{48,32},{64,80},{80,64},{96,112},{112,96},{1... | collective-permute-start | bytes 1572872 | tf_op jit(solution)/shard_map/ppermute | solution.py:218

commit v6 on v5

--- a/solution.py
+++ b/solution.py
@@ -184,14 +184,14 @@
     x2 = move(own, 0, 2)
     xr, xl = move(own, 0, -1), move(own, 0, 1)
     zr, zl = move(own, -1, 0), move(own, 1, 0)
-    zl, zr = in_order(zl, zr)
+    zl, zr, xl, xr = in_order(zl, zr, xl, xr)
     zl_half, zr_half, both = arrange([zl, zr], [[(0, 0)], [(1, 1)], [(0, 0), (0, 1), (1, 0), (1, 1)]])
     both_xr, both_xl = move(both, 0, -1), move(both, 0, 1)
     z2b, z2a = move(zr_half, -1, 0), move(zl_half, 1, 0)
     shards = [shard(own), shard(xl), shard(xr), shard(x2), shard(both, 0), shard(both, 2)]
-    first = score_call(next_kernel, shards, train_grads, blocks_shape(6, train_grads, queries))
+    first = score_call(next_kernel, shards, train_grads, blocks_shape(6, train_grads, queries), weight=10)
     z2a, z2b, x2, first = in_order(z2a, z2b, x2, first)
-    (z2,) = arrange([z2a, z2b], [[(0, 0), (1, 0)]], weight=20)
+    (z2,) = arrange([z2a, z2b], [[(0, 0), (1, 0)]])
     z2_xl = move(z2, 0, 1)
     zr_x2, zl_x2 = move(x2, -1, 0), move(x2, 1, 0)
     z2, both_xr = in_order(z2, both_xr)
@@ -209,7 +209,7 @@
     ]
     shards = [shard(z2_xl), shard(both_xl, 0), shard(both_xl, 2)]
     third = score_call(next_kernel, shards, train_grads, blocks_shape(3, train_grads, queries))
-    third, *z2_x2 = in_order(third, *z2_x2)
+
     shards = [shard(z2_xr), shard(zl_x2), shard(zr_x2), [(half, 0) for half in z2_x2]]
     kernel = lambda own, count, *refs: last_kernel(own, count, offsets, *refs)
     shapes = [blocks_shape(SIDE * SIDE // 2, train_grads, queries)] * 2

time: 107 us -> 106 us (level)
  waiting for transfers between devices: 38.4 us -> 34.6 us
  starting transfers between devices: 32.7 us -> 34.1 us
  blocking collectives: 10.2 us -> 11.5 us
    ppermute x15, waiting for transfers between devices: 36.9 us -> 33 us  [move(): lax.ppermute(value, 'ex', [(z * SIDE + x, to(z, x)) for z in range(SIDE)...]
    ppermute x15, starting transfers between devices: 29.3 us -> 32.3 us  [move(): lax.ppermute(value, 'ex', [(z * SIDE + x, to(z, x)) for z in range(SIDE)...]
    ppermute x1, starting transfers between devices: 3.35 us -> 1.72 us  [local(): lax.ppermute(give, 'layer', [(i, i ^ 1) for i in range(count)])]
    all_to_all x1, blocking collectives: 10.2 us -> 11.5 us  [local(): lax.all_to_all(parts.astype(jnp.bfloat16), 'layer', split_axis=0, concat_...]
    unnamed x14 -> x12, local copies, waits for them, and re-layouts: 8.62 us -> 7.82 us
where the time goes in v6:
time: 106 us; the launch traced here: 105 us
  waiting for transfers between devices  34.6 us (33%)
  starting transfers between devices  34.1 us (32%)
  Pallas kernels  16 us (15%)
  blocking collectives  11.5 us (11%)
  local copies, waits for them, and re-layouts  7.82 us (7%)
    ppermute x15, waiting for transfers between devices, move(): lax.ppermute(value, 'ex', [(z * SIDE + x, to(z, x)) for z in range(SIDE)...  33 us
    ppermute x15, starting transfers between devices, move(): lax.ppermute(value, 'ex', [(z * SIDE + x, to(z, x)) for z in range(SIDE)...  32.3 us
    all_to_all x1, blocking collectives, local(): lax.all_to_all(parts.astype(jnp.bfloat16), 'layer', split_axis=0, concat_...  11.5 us
    pallas_call x4, Pallas kernels, score_call(): pl.pallas_call(functools.partial(kernel, shards, len(arrays)), out_shape=...  10.7 us
    unnamed x12, local copies, waits for them, and re-layouts  7.82 us
    pallas_call x1, Pallas kernels, precondition(): pl.pallas_call(precondition_kernel, out_shape=jax.ShapeDtypeStruct(raw.sh...  4.34 us
  transfers between devices with their start and end apart: 16, of which 6 were waited for; matrix products, arithmetic and copies ran while one was open for 0% of the time, Pallas kernels for 7%

profile of v6, /device:TPU:1, one launch (start us, length us, event | category | flops | bytes accessed | tf_op | source)
XLA Modules:
  0.0 104.8 jit_solution(8770120698990415877)
XLA Ops:
  0.0 4.3 %shard_map.55.refs_0_ = bf16[2,32,4096]{2,1,0:T(8,128)(2,1)} custom-call(bf16[2,32,4096]{2,1,0:T(8,128)(2,1)} %raw.1, f32[2,64,64]{2,1,0:T(8,128)} %basis_out.1, f32[2,64,64]{2,1,0:T(8,128)} %basis_in.1, f32[2,64,64]{2,1,0:T(8,128)} %eigen.1), custom_call_target="tpu_custom_call" | custom-call | tf_op jit(solution)/shard_map/pallas_call | solution.py:78
  4.3 3.8 %collective-permute-start = (bf16[2,32,4096]{2,1,0:T(8,128)(2,1)}, bf16[2,32,4096]{2,1,0:T(8,128)(2,1)S(1)}, u32[]{:S(2)}, u32[]{:S(2)}) collective-permute-start(bf16[2,32,4096]{2,1,0:T(8,128)(2,1)} %shard_map.55.refs_0_), channel_id=1, source_target_pairs={{0,4},{1,5},{2,6},{3,7},{4,8},{5,9},{6,10},{7,11},{8,12},{9,13},{1... | collective-permute-start | bytes 1572872 | tf_op jit(solution)/shard_map/ppermute | solution.py:91
  8.2 3.0 %collective-permute-start.1 = (bf16[2,32,4096]{2,1,0:T(8,128)(2,1)}, bf16[2,32,4096]{2,1,0:T(8,128)(2,1)S(1)}, u32[]{:S(2)}, u32[]{:S(2)}) collective-permute-start(bf16[2,32,4096]{2,1,0:T(8,128)(2,1)} %shard_map.55.refs_0_), channel_id=1, source_target_pairs={{0,12},{1,13},{2,14},{3,15},{4,0},{5,1},{6,2},{7,3},{8,4},{9,5},{1... | collective-permute-start | bytes 1572872 | tf_op jit(solution)/shard_map/ppermute | solution.py:91
  11.2 1.2 %collective-permute-start.2 = (bf16[2,32,4096]{2,1,0:T(8,128)(2,1)}, bf16[2,32,4096]{2,1,0:T(8,128)(2,1)S(1)}, u32[]{:S(2)}, u32[]{:S(2)}) collective-permute-start(bf16[2,32,4096]{2,1,0:T(8,128)(2,1)} %shard_map.55.refs_0_), channel_id=1, source_target_pairs={{0,1},{1,2},{2,3},{3,0},{4,5},{5,6},{6,7},{7,4},{8,9},{9,10},{10,1... | collective-permute-start | bytes 1572872 | tf_op jit(solution)/shard_map/ppermute | solution.py:91
  12.4 1.5 %collective-permute-start.3 = (bf16[2,32,4096]{2,1,0:T(8,128)(2,1)}, bf16[2,32,4096]{2,1,0:T(8,128)(2,1)S(1)}, u32[]{:S(2)}, u32[]{:S(2)}) collective-permute-start(bf16[2,32,4096]{2,1,0:T(8,128)(2,1)} %shard_map.55.refs_0_), channel_id=1, source_target_pairs={{0,3},{1,0},{2,1},{3,2},{4,7},{5,4},{6,5},{7,6},{8,11},{9,8},{10,9... | collective-permute-start | bytes 1572872 | tf_op jit(solution)/shard_map/ppermute | solution.py:91
  13.9 1.5 %collective-permute-start.6 = (bf16[2,32,4096]{2,1,0:T(8,128)(2,1)}, bf16[2,32,4096]{2,1,0:T(8,128)(2,1)S(1)}, u32[]{:S(2)}, u32[]{:S(2)}) collective-permute-start(bf16[2,32,4096]{2,1,0:T(8,128)(2,1)} %shard_map.55.refs_0_), channel_id=1, source_target_pairs={{0,2},{1,3},{2,0},{3,1},{4,6},{5,7},{6,4},{7,5},{8,10},{9,11},{10,... | collective-permute-start | bytes 1572872 | tf_op jit(solution)/shard_map/ppermute | solution.py:91
  15.4 11.7 %collective-permute-done.refs_0_ = bf16[2,32,4096]{2,1,0:T(8,128)(2,1)S(1)} collective-permute-done((bf16[2,32,4096]{2,1,0:T(8,128)(2,1)}, bf16[2,32,4096]{2,1,0:T(8,128)(2,1)S(1)}, u32[]{:S(2)}, u32[]{:S(2)}) %collective-permute-start) | collective-permute-done | bytes 524320 | tf_op jit(solution)/shard_map/ppermute | solution.py:91
  27.1 8.6 %collective-permute-done.1.refs_1_ = bf16[2,32,4096]{2,1,0:T(8,128)(2,1)S(1)} collective-permute-done((bf16[2,32,4096]{2,1,0:T(8,128)(2,1)}, bf16[2,32,4096]{2,1,0:T(8,128)(2,1)S(1)}, u32[]{:S(2)}, u32[]{:S(2)}) %collective-permute-start.1) | collective-permute-done | bytes 524320 | tf_op jit(solution)/shard_map/ppermute | solution.py:91
  35.8 0.1 shard_map.56
  35.9 2.5 %collective-permute-start.8 = (bf16[4,32,4096]{2,1,0:T(8,128)(2,1)S(1)}, bf16[4,32,4096]{2,1,0:T(8,128)(2,1)S(1)}, u32[]{:S(2)}, u32[]{:S(2)}) collective-permute-start(bf16[4,32,4096]{2,1,0:T(8,128)(2,1)S(1)} %get-tuple-element.34.refs_4_), channel_id=1, source_target_pairs={{0,3},{1,0},{2,1},{3,2},{4,7},{5,4},{6,5},{7,6},{8,11},{9,8},{10,9... | collective-permute-start | bytes 3145736 | tf_op jit(solution)/shard_map/ppermute | solution.py:91
  38.4 2.9 %collective-permute-start.4 = (bf16[1,32,4096]{2,1,0:T(8,128)(2,1)S(1)}, bf16[1,32,4096]{2,1,0:T(8,128)(2,1)S(1)}, u32[]{:S(2)}, u32[]{:S(2)}) collective-permute-start(bf16[1,32,4096]{2,1,0:T(8,128)(2,1)S(1)} %get-tuple-element.30), channel_id=1, source_target_pairs={{0,4},{1,5},{2,6},{3,7},{4,8},{5,9},{6,10},{7,11},{8,12},{9,13},{1... | collective-permute-start | bytes 786440 | tf_op jit(solution)/shard_map/ppermute | solution.py:91
  41.3 0.7 collective-permute-start.5
  42.0 3.4 %copy-done = bf16[2,512,4096]{2,1,0:T(8,128)(2,1)S(1)} copy-done((bf16[2,512,4096]{2,1,0:T(8,128)(2,1)S(1)}, bf16[2,512,4096]{2,1,0:T(8,128)(2,1)}, u32[]{:S(2)}) %copy-start) | copy-done | bytes 8388632
  45.4 1.0 copy-done.3
  46.4 2.4 %shard_map.57.refs_7_ = f32[6,32,512]{2,1,0:T(8,128)S(1)} custom-call(bf16[2,32,4096]{2,1,0:T(8,128)(2,1)S(1)} %copy-done.3, bf16[2,32,4096]{2,1,0:T(8,128)(2,1)S(1)} %collective-permute-done.2.refs_1_, bf16[2,32,4096]{2,1,0:T(8,128)(2,1)S(1)} %collective-permute-done.3.refs_2_, bf16[2,32,4096]{2,1,0:T(8,128)(2,1)S(1)} %collective-permute-done.6.refs_3_, ...), custom_call_target="tpu_custom_call" | custom-call | flops 11000000512 | bytes 1024 | tf_op jit(solution)/shard_map/pallas_call | solution.py:162
  48.9 4.6 %collective-permute-start.11 = (bf16[2,32,4096]{2,1,0:T(8,128)(2,1)S(1)}, bf16[2,32,4096]{2,1,0:T(8,128)(2,1)S(1)}, u32[]{:S(2)}, u32[]{:S(2)}) collective-permute-start(bf16[2,32,4096]{2,1,0:T(8,128)(2,1)S(1)} %collective-permute-done.6.refs_3_), channel_id=1, source_target_pairs={{0,4},{1,5},{2,6},{3,7},{4,8},{5,9},{6,10},{7,11},{8,12},{9,13},{1... | collective-permute-start | bytes 1572872 | tf_op jit(solution)/shard_map/ppermute | solution.py:91
  53.5 3.6 %collective-permute-start.7 = (bf16[2,32,4096]{2,1,0:T(8,128)(2,1)S(1)}, bf16[2,32,4096]{2,1,0:T(8,128)(2,1)S(1)}, u32[]{:S(2)}, u32[]{:S(2)}) collective-permute-start(bf16[2,32,4096]{2,1,0:T(8,128)(2,1)S(1)} %shard_map.58.refs_0_), channel_id=1, source_target_pairs={{0,1},{1,2},{2,3},{3,0},{4,5},{5,6},{6,7},{7,4},{8,9},{9,10},{10,1... | collective-permute-start | bytes 1572872 | tf_op jit(solution)/shard_map/ppermute | solution.py:91
  57.1 2.5 %collective-permute-done.8.refs_1_ = bf16[4,32,4096]{2,1,0:T(8,128)(2,1)S(1)} collective-permute-done((bf16[4,32,4096]{2,1,0:T(8,128)(2,1)S(1)}, bf16[4,32,4096]{2,1,0:T(8,128)(2,1)S(1)}, u32[]{:S(2)}, u32[]{:S(2)}) %collective-permute-start.8) | collective-permute-done | bytes 1048608 | tf_op jit(solution)/shard_map/ppermute | solution.py:91
  59.6 2.0 %collective-permute-start.9 = (bf16[2,32,4096]{2,1,0:T(8,128)(2,1)S(1)}, bf16[2,32,4096]{2,1,0:T(8,128)(2,1)S(1)}, u32[]{:S(2)}, u32[]{:S(2)}) collective-permute-start(bf16[2,32,4096]{2,1,0:T(8,128)(2,1)S(1)} %shard_map.58.refs_0_), channel_id=1, source_target_pairs={{0,3},{1,0},{2,1},{3,2},{4,7},{5,4},{6,5},{7,6},{8,11},{9,8},{10,9... | collective-permute-start | bytes 1572872 | tf_op jit(solution)/shard_map/ppermute | solution.py:91
  61.7 2.4 %shard_map.59.refs_8_ = f32[3,32,512]{2,1,0:T(8,128)S(1)} custom-call(bf16[2,32,4096]{2,1,0:T(8,128)(2,1)S(1)} %shard_map.58.refs_0_, bf16[4,32,4096]{2,1,0:T(8,128)(2,1)S(1)} %collective-permute-done.8.refs_1_, bf16[2,512,4096]{2,1,0:T(8,128)(2,1)S(1)} %copy-done.1), custom_call_target="tpu_custom_call" | custom-call | flops 1100000000 | bytes 1024 | tf_op jit(solution)/shard_map/pallas_call | solution.py:162
  64.0 8.6 %collective-permute-done.7.refs_0_ = bf16[2,32,4096]{2,1,0:T(8,128)(2,1)S(1)} collective-permute-done((bf16[2,32,4096]{2,1,0:T(8,128)(2,1)S(1)}, bf16[2,32,4096]{2,1,0:T(8,128)(2,1)S(1)}, u32[]{:S(2)}, u32[]{:S(2)}) %collective-permute-start.7) | collective-permute-done | bytes 524320 | tf_op jit(solution)/shard_map/ppermute | solution.py:91
  72.6 0.9 shard_map.60
  73.5 4.9 %collective-permute-start.13 = (bf16[1,32,4096]{2,1,0:T(8,128)(2,1)}, bf16[1,32,4096]{2,1,0:T(8,128)(2,1)}, u32[]{:S(2)}, u32[]{:S(2)}) collective-permute-start(bf16[1,32,4096]{2,1,0:T(8,128)(2,1)} %get-tuple-element.44), channel_id=1, source_target_pairs={{0,1},{1,2},{2,3},{3,0},{4,5},{5,6},{6,7},{7,4},{8,9},{9,10},{10,1... | collective-permute-start | bytes 786440 | tf_op jit(solution)/shard_map/ppermute | solution.py:91
  78.5 3.4 %copy-done.2 = bf16[2,512,4096]{2,1,0:T(8,128)(2,1)S(1)} copy-done((bf16[2,512,4096]{2,1,0:T(8,128)(2,1)S(1)}, bf16[2,512,4096]{2,1,0:T(8,128)(2,1)}, u32[]{:S(2)}) %copy-start.2) | copy-done | bytes 8388632
  81.9 2.4 %shard_map.61.refs_9_ = f32[3,32,512]{2,1,0:T(8,128)S(1)} custom-call(bf16[2,32,4096]{2,1,0:T(8,128)(2,1)S(1)} %collective-permute-done.7.refs_0_, bf16[4,32,4096]{2,1,0:T(8,128)(2,1)S(1)} %collective-permute-done.10.refs_1_, bf16[2,512,4096]{2,1,0:T(8,128)(2,1)S(1)} %copy-done.2), custom_call_target="tpu_custom_call" | custom-call | flops 1100000000 | bytes 1024 | tf_op jit(solution)/shard_map/pallas_call | solution.py:162
  84.3 1.5 %collective-permute-done.14.refs_5_ = bf16[1,32,4096]{2,1,0:T(8,128)(2,1)} collective-permute-done((bf16[1,32,4096]{2,1,0:T(8,128)(2,1)}, bf16[1,32,4096]{2,1,0:T(8,128)(2,1)}, u32[]{:S(2)}, u32[]{:S(2)}) %collective-permute-start.14) | collective-permute-done | bytes 262176 | tf_op jit(solution)/shard_map/ppermute | solution.py:91
  85.8 3.5 %shard_map.62 = (f32[8,32,512]{2,1,0:T(8,128)S(1)}, f32[8,32,512]{2,1,0:T(8,128)S(1)}) custom-call(s32[2]{0:T(128)S(1)} %pad_add_fusion.refs_0_, bf16[2,32,4096]{2,1,0:T(8,128)(2,1)S(1)} %collective-permute-done.9.refs_1_, bf16[2,32,4096]{2,1,0:T(8,128)(2,1)S(1)} %collective-permute-done.11.refs_2_, ...), custom_call_target="tpu_custom_call" | custom-call | flops 1100000000 | bytes 1024 | tf_op jit(solution)/shard_map/pallas_call | solution.py:162
  89.3 1.7 %collective-permute-start.15 = (f32[8,32,512]{2,1,0:T(8,128)S(1)}, f32[8,32,512]{2,1,0:T(8,128)S(1)}, u32[]{:S(2)}, u32[]{:S(2)}) collective-permute-start(f32[8,32,512]{2,1,0:T(8,128)S(1)} %get-tuple-element.50), channel_id=1, source_target_pairs={{0,16},{16,0},{32,48},{48,32},{64,80},{80,64},{96,112},{112,96},{1... | collective-permute-start | bytes 1572872 | tf_op jit(solution)/shard_map/ppermute | solution.py:218
  91.1 1.5 %collective-permute-done.15 = f32[8,32,512]{2,1,0:T(8,128)S(1)} collective-permute-done((f32[8,32,512]{2,1,0:T(8,128)S(1)}, f32[8,32,512]{2,1,0:T(8,128)S(1)}, u32[]{:S(2)}, u32[]{:S(2)}) %collective-permute-start.15) | collective-permute-done | bytes 524320 | tf_op jit(solution)/shard_map/ppermute | solution.py:218
  92.6 0.1 add_convert_fusion
  92.7 11.5 %all_to_all.5 = bf16[8,32,512]{2,1,0:T(8,128)(2,1)S(1)} all-to-all(bf16[8,32,512]{2,1,0:T(8,128)(2,1)S(1)} %add_convert_fusion), channel_id=1, replica_groups={{0,32,64,96,128,160,192,224},{16,48,80,112,144,176,208,240},{1,33,65,97..., dimensions={0} | all-to-all | bytes 524288 | tf_op jit(solution)/shard_map/all_to_all | solution.py:220
  104.2 0.7 convert_reduce_fusion
  (24 shorter events, 0.2 us)
Async XLA Ops:
  4.3 22.8 %collective-permute-start = (bf16[2,32,4096]{2,1,0:T(8,128)(2,1)}, bf16[2,32,4096]{2,1,0:T(8,128)(2,1)S(1)}, u32[]{:S(2)}, u32[]{:S(2)}) collective-permute-start(bf16[2,32,4096]{2,1,0:T(8,128)(2,1)} %shard_map.55.refs_0_), channel_id=1, source_target_pairs={{0,4},{1,5},{2,6},{3,7},{4,8},{5,9},{6,10},{7,11},{8,12},{9,13},{1... | collective-permute-start | bytes 1572872 | tf_op jit(solution)/shard_map/ppermute | solution.py:91
  8.2 27.6 %collective-permute-start.1 = (bf16[2,32,4096]{2,1,0:T(8,128)(2,1)}, bf16[2,32,4096]{2,1,0:T(8,128)(2,1)S(1)}, u32[]{:S(2)}, u32[]{:S(2)}) collective-permute-start(bf16[2,32,4096]{2,1,0:T(8,128)(2,1)} %shard_map.55.refs_0_), channel_id=1, source_target_pairs={{0,12},{1,13},{2,14},{3,15},{4,0},{5,1},{6,2},{7,3},{8,4},{9,5},{1... | collective-permute-start | bytes 1572872 | tf_op jit(solution)/shard_map/ppermute | solution.py:91
  11.2 24.6 %collective-permute-start.2 = (bf16[2,32,4096]{2,1,0:T(8,128)(2,1)}, bf16[2,32,4096]{2,1,0:T(8,128)(2,1)S(1)}, u32[]{:S(2)}, u32[]{:S(2)}) collective-permute-start(bf16[2,32,4096]{2,1,0:T(8,128)(2,1)} %shard_map.55.refs_0_), channel_id=1, source_target_pairs={{0,1},{1,2},{2,3},{3,0},{4,5},{5,6},{6,7},{7,4},{8,9},{9,10},{10,1... | collective-permute-start | bytes 1572872 | tf_op jit(solution)/shard_map/ppermute | solution.py:91
  12.4 23.4 %collective-permute-start.3 = (bf16[2,32,4096]{2,1,0:T(8,128)(2,1)}, bf16[2,32,4096]{2,1,0:T(8,128)(2,1)S(1)}, u32[]{:S(2)}, u32[]{:S(2)}) collective-permute-start(bf16[2,32,4096]{2,1,0:T(8,128)(2,1)} %shard_map.55.refs_0_), channel_id=1, source_target_pairs={{0,3},{1,0},{2,1},{3,2},{4,7},{5,4},{6,5},{7,6},{8,11},{9,8},{10,9... | collective-permute-start | bytes 1572872 | tf_op jit(solution)/shard_map/ppermute | solution.py:91
  13.9 28.1 %collective-permute-start.6 = (bf16[2,32,4096]{2,1,0:T(8,128)(2,1)}, bf16[2,32,4096]{2,1,0:T(8,128)(2,1)S(1)}, u32[]{:S(2)}, u32[]{:S(2)}) collective-permute-start(bf16[2,32,4096]{2,1,0:T(8,128)(2,1)} %shard_map.55.refs_0_), channel_id=1, source_target_pairs={{0,2},{1,3},{2,0},{3,1},{4,6},{5,7},{6,4},{7,5},{8,10},{9,11},{10,... | collective-permute-start | bytes 1572872 | tf_op jit(solution)/shard_map/ppermute | solution.py:91
  35.9 23.8 %collective-permute-start.8 = (bf16[4,32,4096]{2,1,0:T(8,128)(2,1)S(1)}, bf16[4,32,4096]{2,1,0:T(8,128)(2,1)S(1)}, u32[]{:S(2)}, u32[]{:S(2)}) collective-permute-start(bf16[4,32,4096]{2,1,0:T(8,128)(2,1)S(1)} %get-tuple-element.34.refs_4_), channel_id=1, source_target_pairs={{0,3},{1,0},{2,1},{3,2},{4,7},{5,4},{6,5},{7,6},{8,11},{9,8},{10,9... | collective-permute-start | bytes 3145736 | tf_op jit(solution)/shard_map/ppermute | solution.py:91
  38.4 34.2 %collective-permute-start.10 = (bf16[4,32,4096]{2,1,0:T(8,128)(2,1)S(1)}, bf16[4,32,4096]{2,1,0:T(8,128)(2,1)S(1)}, u32[]{:S(2)}, u32[]{:S(2)}) collective-permute-start(bf16[4,32,4096]{2,1,0:T(8,128)(2,1)S(1)} %get-tuple-element.34.refs_4_), channel_id=1, source_target_pairs={{0,1},{1,2},{2,3},{3,0},{4,5},{5,6},{6,7},{7,4},{8,9},{9,10},{10,1... | collective-permute-start | bytes 3145736 | tf_op jit(solution)/shard_map/ppermute | solution.py:91
  38.4 10.4 %collective-permute-start.4 = (bf16[1,32,4096]{2,1,0:T(8,128)(2,1)S(1)}, bf16[1,32,4096]{2,1,0:T(8,128)(2,1)S(1)}, u32[]{:S(2)}, u32[]{:S(2)}) collective-permute-start(bf16[1,32,4096]{2,1,0:T(8,128)(2,1)S(1)} %get-tuple-element.30), channel_id=1, source_target_pairs={{0,4},{1,5},{2,6},{3,7},{4,8},{5,9},{6,10},{7,11},{8,12},{9,13},{1... | collective-permute-start | bytes 786440 | tf_op jit(solution)/shard_map/ppermute | solution.py:91
  41.3 7.5 %collective-permute-start.5 = (bf16[1,32,4096]{2,1,0:T(8,128)(2,1)S(1)}, bf16[1,32,4096]{2,1,0:T(8,128)(2,1)S(1)}, u32[]{:S(2)}, u32[]{:S(2)}) collective-permute-start(bf16[1,32,4096]{2,1,0:T(8,128)(2,1)S(1)} %get-tuple-element.31), channel_id=1, source_target_pairs={{0,12},{1,13},{2,14},{3,15},{4,0},{5,1},{6,2},{7,3},{8,4},{9,5},{1... | collective-permute-start | bytes 786440 | tf_op jit(solution)/shard_map/ppermute | solution.py:91
  42.0 3.4 %copy-start = (bf16[2,512,4096]{2,1,0:T(8,128)(2,1)S(1)}, bf16[2,512,4096]{2,1,0:T(8,128)(2,1)}, u32[]{:S(2)}) copy-start(bf16[2,512,4096]{2,1,0:T(8,128)(2,1)} %refs_6_.1) | copy-start | bytes 25165828
  45.4 1.0 copy-start.3
  46.4 15.2 %copy-start.1 = (bf16[2,512,4096]{2,1,0:T(8,128)(2,1)S(1)}, bf16[2,512,4096]{2,1,0:T(8,128)(2,1)}, u32[]{:S(2)}) copy-start(bf16[2,512,4096]{2,1,0:T(8,128)(2,1)} %refs_6_.1) | copy-start | bytes 25165828
  48.8 23.8 %copy-start.4 = (f32[6,32,512]{2,1,0:T(8,128)}, f32[6,32,512]{2,1,0:T(8,128)S(1)}, u32[]{:S(2)}) copy-start(f32[6,32,512]{2,1,0:T(8,128)S(1)} %shard_map.57.refs_7_) | copy-start | bytes 1179652
  48.9 23.7 %collective-permute-start.11 = (bf16[2,32,4096]{2,1,0:T(8,128)(2,1)S(1)}, bf16[2,32,4096]{2,1,0:T(8,128)(2,1)S(1)}, u32[]{:S(2)}, u32[]{:S(2)}) collective-permute-start(bf16[2,32,4096]{2,1,0:T(8,128)(2,1)S(1)} %collective-permute-done.6.refs_3_), channel_id=1, source_target_pairs={{0,4},{1,5},{2,6},{3,7},{4,8},{5,9},{6,10},{7,11},{8,12},{9,13},{1... | collective-permute-start | bytes 1572872 | tf_op jit(solution)/shard_map/ppermute | solution.py:91
  53.4 19.2 %collective-permute-start.12 = (bf16[2,32,4096]{2,1,0:T(8,128)(2,1)S(1)}, bf16[2,32,4096]{2,1,0:T(8,128)(2,1)S(1)}, u32[]{:S(2)}, u32[]{:S(2)}) collective-permute-start(bf16[2,32,4096]{2,1,0:T(8,128)(2,1)S(1)} %collective-permute-done.6.refs_3_), channel_id=1, source_target_pairs={{0,12},{1,13},{2,14},{3,15},{4,0},{5,1},{6,2},{7,3},{8,4},{9,5},{1... | collective-permute-start | bytes 1572872 | tf_op jit(solution)/shard_map/ppermute | solution.py:91
  53.5 19.1 %collective-permute-start.7 = (bf16[2,32,4096]{2,1,0:T(8,128)(2,1)S(1)}, bf16[2,32,4096]{2,1,0:T(8,128)(2,1)S(1)}, u32[]{:S(2)}, u32[]{:S(2)}) collective-permute-start(bf16[2,32,4096]{2,1,0:T(8,128)(2,1)S(1)} %shard_map.58.refs_0_), channel_id=1, source_target_pairs={{0,1},{1,2},{2,3},{3,0},{4,5},{5,6},{6,7},{7,4},{8,9},{9,10},{10,1... | collective-permute-start | bytes 1572872 | tf_op jit(solution)/shard_map/ppermute | solution.py:91
  59.6 13.0 %collective-permute-start.9 = (bf16[2,32,4096]{2,1,0:T(8,128)(2,1)S(1)}, bf16[2,32,4096]{2,1,0:T(8,128)(2,1)S(1)}, u32[]{:S(2)}, u32[]{:S(2)}) collective-permute-start(bf16[2,32,4096]{2,1,0:T(8,128)(2,1)S(1)} %shard_map.58.refs_0_), channel_id=1, source_target_pairs={{0,3},{1,0},{2,1},{3,2},{4,7},{5,4},{6,5},{7,6},{8,11},{9,8},{10,9... | collective-permute-start | bytes 1572872 | tf_op jit(solution)/shard_map/ppermute | solution.py:91
  73.5 10.8 %collective-permute-start.13 = (bf16[1,32,4096]{2,1,0:T(8,128)(2,1)}, bf16[1,32,4096]{2,1,0:T(8,128)(2,1)}, u32[]{:S(2)}, u32[]{:S(2)}) collective-permute-start(bf16[1,32,4096]{2,1,0:T(8,128)(2,1)} %get-tuple-element.44), channel_id=1, source_target_pairs={{0,1},{1,2},{2,3},{3,0},{4,5},{5,6},{6,7},{7,4},{8,9},{9,10},{10,1... | collective-permute-start | bytes 786440 | tf_op jit(solution)/shard_map/ppermute | solution.py:91
  78.4 7.4 %collective-permute-start.14 = (bf16[1,32,4096]{2,1,0:T(8,128)(2,1)}, bf16[1,32,4096]{2,1,0:T(8,128)(2,1)}, u32[]{:S(2)}, u32[]{:S(2)}) collective-permute-start(bf16[1,32,4096]{2,1,0:T(8,128)(2,1)} %get-tuple-element.45), channel_id=1, source_target_pairs={{0,3},{1,0},{2,1},{3,2},{4,7},{5,4},{6,5},{7,6},{8,11},{9,8},{10,9... | collective-permute-start | bytes 786440 | tf_op jit(solution)/shard_map/ppermute | solution.py:91
  78.5 3.4 %copy-start.2 = (bf16[2,512,4096]{2,1,0:T(8,128)(2,1)S(1)}, bf16[2,512,4096]{2,1,0:T(8,128)(2,1)}, u32[]{:S(2)}) copy-start(bf16[2,512,4096]{2,1,0:T(8,128)(2,1)} %refs_6_.1) | copy-start | bytes 25165828
  81.9 3.9 %copy-start.5 = (f32[6,32,512]{2,1,0:T(8,128)S(1)}, f32[6,32,512]{2,1,0:T(8,128)}, u32[]{:S(2)}) copy-start(f32[6,32,512]{2,1,0:T(8,128)} %copy-done.4) | copy-start | bytes 1179652
  89.3 3.3 %collective-permute-start.15 = (f32[8,32,512]{2,1,0:T(8,128)S(1)}, f32[8,32,512]{2,1,0:T(8,128)S(1)}, u32[]{:S(2)}, u32[]{:S(2)}) collective-permute-start(f32[8,32,512]{2,1,0:T(8,128)S(1)} %get-tuple-element.50), channel_id=1, source_target_pairs={{0,16},{16,0},{32,48},{48,32},{64,80},{80,64},{96,112},{112,96},{1... | collective-permute-start | bytes 1572872 | tf_op jit(solution)/shard_map/ppermute | solution.py:218

commit v7 on v6

--- a/solution.py
+++ b/solution.py
@@ -191,15 +191,15 @@
     shards = [shard(own), shard(xl), shard(xr), shard(x2), shard(both, 0), shard(both, 2)]
     first = score_call(next_kernel, shards, train_grads, blocks_shape(6, train_grads, queries), weight=10)
     z2a, z2b, x2, first = in_order(z2a, z2b, x2, first)
-    (z2,) = arrange([z2a, z2b], [[(0, 0), (1, 0)]])
+    (z2,) = arrange([z2a, z2b], [[(0, 0), (1, 0)]], weight=0)
     z2_xl = move(z2, 0, 1)
     zr_x2, zl_x2 = move(x2, -1, 0), move(x2, 1, 0)
     z2, both_xr = in_order(z2, both_xr)
     z2_xr = move(z2, 0, -1)
     shards = [shard(z2), shard(both_xr, 0), shard(both_xr, 2)]
-    second = score_call(next_kernel, shards, train_grads, blocks_shape(3, train_grads, queries))
+    second = score_call(next_kernel, shards, train_grads, blocks_shape(3, train_grads, queries), weight=4)
     z2_xl, z2_xr, both_xl, zl_x2, zr_x2, second = in_order(z2_xl, z2_xr, both_xl, zl_x2, zr_x2, second)
-    halves = arrange([z2_xl, z2_xr], [[(0, 0)], [(1, 1)]])
+    halves = arrange([z2_xl, z2_xr], [[(0, 0)], [(1, 1)]], weight=0)
     z2_x2 = move(halves[0], 0, 1), move(halves[1], 0, -1)
     offsets = [
         (0, 0), (0, -1), (0, 1), (0, 2), (-1, 0), (1, 0),
@@ -208,7 +208,7 @@
         (2, 1), (-1, 2), (1, 2), (2, 2),
     ]
     shards = [shard(z2_xl), shard(both_xl, 0), shard(both_xl, 2)]
-    third = score_call(next_kernel, shards, train_grads, blocks_shape(3, train_grads, queries))
+    third = score_call(next_kernel, shards, train_grads, blocks_shape(3, train_grads, queries), weight=8)
 
     shards = [shard(z2_xr), shard(zl_x2), shard(zr_x2), [(half, 0) for half in z2_x2]]
     kernel = lambda own, count, *refs: last_kernel(own, count, offsets, *refs)

time: 106 us -> 105 us (level)
  waiting for transfers between devices: 34.6 us -> 37.5 us
  Pallas kernels: 16 us -> 14.7 us
    ppermute x15, waiting for transfers between devices: 33 us -> 35.9 us  [move(): lax.ppermute(value, 'ex', [(z * SIDE + x, to(z, x)) for z in range(SIDE)...]
  transfers between devices with their start and end apart: 16 -> 16, of which waited for: 6 -> 7; matrix products, arithmetic and copies ran while one was open for 0% -> 0% of each run, Pallas kernels for 7% -> 7%
where the time goes in v7:
time: 105 us; the launch traced here: 104 us
  waiting for transfers between devices  37.5 us (36%)
  starting transfers between devices  33.6 us (32%)
  Pallas kernels  14.7 us (14%)
  blocking collectives  10.5 us (10%)
  local copies, waits for them, and re-layouts  6.85 us (7%)
    ppermute x15, waiting for transfers between devices, move(): lax.ppermute(value, 'ex', [(z * SIDE + x, to(z, x)) for z in range(SIDE)...  35.9 us
    ppermute x15, starting transfers between devices, move(): lax.ppermute(value, 'ex', [(z * SIDE + x, to(z, x)) for z in range(SIDE)...  31.9 us
    all_to_all x1, blocking collectives, local(): lax.all_to_all(parts.astype(jnp.bfloat16), 'layer', split_axis=0, concat_...  10.5 us
    pallas_call x4, Pallas kernels, score_call(): pl.pallas_call(functools.partial(kernel, shards, len(arrays)), out_shape=...  10.2 us
    unnamed x12, local copies, waits for them, and re-layouts  6.85 us
    pallas_call x1, Pallas kernels, precondition(): pl.pallas_call(precondition_kernel, out_shape=jax.ShapeDtypeStruct(raw.sh...  4.34 us
  transfers between devices with their start and end apart: 16, of which 7 were waited for; matrix products, arithmetic and copies ran while one was open for 0% of the time, Pallas kernels for 7%

profile of v7, /device:TPU:1, one launch (start us, length us, event | category | flops | bytes accessed | tf_op | source)
XLA Modules:
  0.0 104.1 jit_solution(17288165916500361685)
XLA Ops:
  0.0 4.3 %shard_map.55.refs_0_ = bf16[2,32,4096]{2,1,0:T(8,128)(2,1)} custom-call(bf16[2,32,4096]{2,1,0:T(8,128)(2,1)} %raw.1, f32[2,64,64]{2,1,0:T(8,128)} %basis_out.1, f32[2,64,64]{2,1,0:T(8,128)} %basis_in.1, f32[2,64,64]{2,1,0:T(8,128)} %eigen.1), custom_call_target="tpu_custom_call" | custom-call | tf_op jit(solution)/shard_map/pallas_call | solution.py:78
  4.3 3.8 %collective-permute-start = (bf16[2,32,4096]{2,1,0:T(8,128)(2,1)}, bf16[2,32,4096]{2,1,0:T(8,128)(2,1)S(1)}, u32[]{:S(2)}, u32[]{:S(2)}) collective-permute-start(bf16[2,32,4096]{2,1,0:T(8,128)(2,1)} %shard_map.55.refs_0_), channel_id=1, source_target_pairs={{0,4},{1,5},{2,6},{3,7},{4,8},{5,9},{6,10},{7,11},{8,12},{9,13},{1... | collective-permute-start | bytes 1572872 | tf_op jit(solution)/shard_map/ppermute | solution.py:91
  8.2 3.0 %collective-permute-start.1 = (bf16[2,32,4096]{2,1,0:T(8,128)(2,1)}, bf16[2,32,4096]{2,1,0:T(8,128)(2,1)S(1)}, u32[]{:S(2)}, u32[]{:S(2)}) collective-permute-start(bf16[2,32,4096]{2,1,0:T(8,128)(2,1)} %shard_map.55.refs_0_), channel_id=1, source_target_pairs={{0,12},{1,13},{2,14},{3,15},{4,0},{5,1},{6,2},{7,3},{8,4},{9,5},{1... | collective-permute-start | bytes 1572872 | tf_op jit(solution)/shard_map/ppermute | solution.py:91
  11.2 1.2 %collective-permute-start.2 = (bf16[2,32,4096]{2,1,0:T(8,128)(2,1)}, bf16[2,32,4096]{2,1,0:T(8,128)(2,1)S(1)}, u32[]{:S(2)}, u32[]{:S(2)}) collective-permute-start(bf16[2,32,4096]{2,1,0:T(8,128)(2,1)} %shard_map.55.refs_0_), channel_id=1, source_target_pairs={{0,1},{1,2},{2,3},{3,0},{4,5},{5,6},{6,7},{7,4},{8,9},{9,10},{10,1... | collective-permute-start | bytes 1572872 | tf_op jit(solution)/shard_map/ppermute | solution.py:91
  12.4 1.5 %collective-permute-start.3 = (bf16[2,32,4096]{2,1,0:T(8,128)(2,1)}, bf16[2,32,4096]{2,1,0:T(8,128)(2,1)S(1)}, u32[]{:S(2)}, u32[]{:S(2)}) collective-permute-start(bf16[2,32,4096]{2,1,0:T(8,128)(2,1)} %shard_map.55.refs_0_), channel_id=1, source_target_pairs={{0,3},{1,0},{2,1},{3,2},{4,7},{5,4},{6,5},{7,6},{8,11},{9,8},{10,9... | collective-permute-start | bytes 1572872 | tf_op jit(solution)/shard_map/ppermute | solution.py:91
  13.9 1.5 %collective-permute-start.6 = (bf16[2,32,4096]{2,1,0:T(8,128)(2,1)}, bf16[2,32,4096]{2,1,0:T(8,128)(2,1)S(1)}, u32[]{:S(2)}, u32[]{:S(2)}) collective-permute-start(bf16[2,32,4096]{2,1,0:T(8,128)(2,1)} %shard_map.55.refs_0_), channel_id=1, source_target_pairs={{0,2},{1,3},{2,0},{3,1},{4,6},{5,7},{6,4},{7,5},{8,10},{9,11},{10,... | collective-permute-start | bytes 1572872 | tf_op jit(solution)/shard_map/ppermute | solution.py:91
  15.4 11.7 %collective-permute-done.refs_0_ = bf16[2,32,4096]{2,1,0:T(8,128)(2,1)S(1)} collective-permute-done((bf16[2,32,4096]{2,1,0:T(8,128)(2,1)}, bf16[2,32,4096]{2,1,0:T(8,128)(2,1)S(1)}, u32[]{:S(2)}, u32[]{:S(2)}) %collective-permute-start) | collective-permute-done | bytes 524320 | tf_op jit(solution)/shard_map/ppermute | solution.py:91
  27.1 8.6 %collective-permute-done.1.refs_1_ = bf16[2,32,4096]{2,1,0:T(8,128)(2,1)S(1)} collective-permute-done((bf16[2,32,4096]{2,1,0:T(8,128)(2,1)}, bf16[2,32,4096]{2,1,0:T(8,128)(2,1)S(1)}, u32[]{:S(2)}, u32[]{:S(2)}) %collective-permute-start.1) | collective-permute-done | bytes 524320 | tf_op jit(solution)/shard_map/ppermute | solution.py:91
  35.9 0.7 copy-done.3
  36.6 0.7 copy-done.5
  37.3 2.5 %collective-permute-start.8 = (bf16[4,32,4096]{2,1,0:T(8,128)(2,1)S(1)}, bf16[4,32,4096]{2,1,0:T(8,128)(2,1)S(1)}, u32[]{:S(2)}, u32[]{:S(2)}) collective-permute-start(bf16[4,32,4096]{2,1,0:T(8,128)(2,1)S(1)} %get-tuple-element.34.refs_4_), channel_id=1, source_target_pairs={{0,3},{1,0},{2,1},{3,2},{4,7},{5,4},{6,5},{7,6},{8,11},{9,8},{10,9... | collective-permute-start | bytes 3145736 | tf_op jit(solution)/shard_map/ppermute | solution.py:91
  39.7 2.9 %collective-permute-start.4 = (bf16[1,32,4096]{2,1,0:T(8,128)(2,1)}, bf16[1,32,4096]{2,1,0:T(8,128)(2,1)S(1)}, u32[]{:S(2)}, u32[]{:S(2)}) collective-permute-start(bf16[1,32,4096]{2,1,0:T(8,128)(2,1)} %copy-done.5), channel_id=1, source_target_pairs={{0,4},{1,5},{2,6},{3,7},{4,8},{5,9},{6,10},{7,11},{8,12},{9,13},{1... | collective-permute-start | bytes 786440 | tf_op jit(solution)/shard_map/ppermute | solution.py:91
  42.7 0.7 collective-permute-start.5
  43.3 3.4 %copy-done = bf16[2,512,4096]{2,1,0:T(8,128)(2,1)S(1)} copy-done((bf16[2,512,4096]{2,1,0:T(8,128)(2,1)S(1)}, bf16[2,512,4096]{2,1,0:T(8,128)(2,1)}, u32[]{:S(2)}) %copy-start) | copy-done | bytes 8388632
  46.7 1.0 copy-done.2
  47.7 1.0 copy-done.4
  48.8 2.4 %shard_map.57.refs_7_ = f32[6,32,512]{2,1,0:T(8,128)S(1)} custom-call(bf16[2,32,4096]{2,1,0:T(8,128)(2,1)S(1)} %copy-done.2, bf16[2,32,4096]{2,1,0:T(8,128)(2,1)S(1)} %collective-permute-done.2.refs_1_, bf16[2,32,4096]{2,1,0:T(8,128)(2,1)S(1)} %copy-done.4, bf16[2,32,4096]{2,1,0:T(8,128)(2,1)S(1)} %collective-permute-done.6.refs_3_, ...), custom_call_target="tpu_custom_call" | custom-call | flops 11000000512 | bytes 1024 | tf_op jit(solution)/shard_map/pallas_call | solution.py:162
  51.2 3.7 %collective-permute-start.11 = (bf16[2,32,4096]{2,1,0:T(8,128)(2,1)S(1)}, bf16[2,32,4096]{2,1,0:T(8,128)(2,1)S(1)}, u32[]{:S(2)}, u32[]{:S(2)}) collective-permute-start(bf16[2,32,4096]{2,1,0:T(8,128)(2,1)S(1)} %collective-permute-done.6.refs_3_), channel_id=1, source_target_pairs={{0,4},{1,5},{2,6},{3,7},{4,8},{5,9},{6,10},{7,11},{8,12},{9,13},{1... | collective-permute-start | bytes 1572872 | tf_op jit(solution)/shard_map/ppermute | solution.py:91
  54.9 3.6 %collective-permute-start.7 = (bf16[2,32,4096]{2,1,0:T(8,128)(2,1)S(1)}, bf16[2,32,4096]{2,1,0:T(8,128)(2,1)S(1)}, u32[]{:S(2)}, u32[]{:S(2)}) collective-permute-start(bf16[2,32,4096]{2,1,0:T(8,128)(2,1)S(1)} %shard_map.58.refs_0_), channel_id=1, source_target_pairs={{0,1},{1,2},{2,3},{3,0},{4,5},{5,6},{6,7},{7,4},{8,9},{9,10},{10,1... | collective-permute-start | bytes 1572872 | tf_op jit(solution)/shard_map/ppermute | solution.py:91
  58.6 2.4 %collective-permute-done.8.refs_1_ = bf16[4,32,4096]{2,1,0:T(8,128)(2,1)S(1)} collective-permute-done((bf16[4,32,4096]{2,1,0:T(8,128)(2,1)S(1)}, bf16[4,32,4096]{2,1,0:T(8,128)(2,1)S(1)}, u32[]{:S(2)}, u32[]{:S(2)}) %collective-permute-start.8) | collective-permute-done | bytes 1048608 | tf_op jit(solution)/shard_map/ppermute | solution.py:91
  61.0 2.0 %collective-permute-start.9 = (bf16[2,32,4096]{2,1,0:T(8,128)(2,1)S(1)}, bf16[2,32,4096]{2,1,0:T(8,128)(2,1)S(1)}, u32[]{:S(2)}, u32[]{:S(2)}) collective-permute-start(bf16[2,32,4096]{2,1,0:T(8,128)(2,1)S(1)} %shard_map.58.refs_0_), channel_id=1, source_target_pairs={{0,3},{1,0},{2,1},{3,2},{4,7},{5,4},{6,5},{7,6},{8,11},{9,8},{10,9... | collective-permute-start | bytes 1572872 | tf_op jit(solution)/shard_map/ppermute | solution.py:91
  63.0 2.4 %shard_map.59.refs_8_ = f32[3,32,512]{2,1,0:T(8,128)S(1)} custom-call(bf16[2,32,4096]{2,1,0:T(8,128)(2,1)S(1)} %shard_map.58.refs_0_, bf16[4,32,4096]{2,1,0:T(8,128)(2,1)S(1)} %collective-permute-done.8.refs_1_, bf16[2,512,4096]{2,1,0:T(8,128)(2,1)S(1)} %copy-done.1), custom_call_target="tpu_custom_call" | custom-call | flops 4400000000 | bytes 1024 | tf_op jit(solution)/shard_map/pallas_call | solution.py:162
  65.4 8.5 %collective-permute-done.7.refs_0_ = bf16[2,32,4096]{2,1,0:T(8,128)(2,1)S(1)} collective-permute-done((bf16[2,32,4096]{2,1,0:T(8,128)(2,1)S(1)}, bf16[2,32,4096]{2,1,0:T(8,128)(2,1)S(1)}, u32[]{:S(2)}, u32[]{:S(2)}) %collective-permute-start.7) | collective-permute-done | bytes 524320 | tf_op jit(solution)/shard_map/ppermute | solution.py:91
  74.0 5.4 %collective-permute-start.13 = (bf16[1,32,4096]{2,1,0:T(8,128)(2,1)S(1)}, bf16[1,32,4096]{2,1,0:T(8,128)(2,1)S(1)}, u32[]{:S(2)}, u32[]{:S(2)}) collective-permute-start(bf16[1,32,4096]{2,1,0:T(8,128)(2,1)S(1)} %get-tuple-element.44), channel_id=1, source_target_pairs={{0,1},{1,2},{2,3},{3,0},{4,5},{5,6},{6,7},{7,4},{8,9},{9,10},{10,1... | collective-permute-start | bytes 786440 | tf_op jit(solution)/shard_map/ppermute | solution.py:91
  79.4 2.4 %shard_map.61.refs_9_ = f32[3,32,512]{2,1,0:T(8,128)S(1)} custom-call(bf16[2,32,4096]{2,1,0:T(8,128)(2,1)S(1)} %collective-permute-done.7.refs_0_, bf16[4,32,4096]{2,1,0:T(8,128)(2,1)S(1)} %collective-permute-done.10.refs_1_, bf16[2,512,4096]{2,1,0:T(8,128)(2,1)S(1)} %copy-done.1), custom_call_target="tpu_custom_call" | custom-call | flops 8800000000 | bytes 1024 | tf_op jit(solution)/shard_map/pallas_call | solution.py:162
  81.8 2.8 %collective-permute-done.13.refs_4_ = bf16[1,32,4096]{2,1,0:T(8,128)(2,1)S(1)} collective-permute-done((bf16[1,32,4096]{2,1,0:T(8,128)(2,1)S(1)}, bf16[1,32,4096]{2,1,0:T(8,128)(2,1)S(1)}, u32[]{:S(2)}, u32[]{:S(2)}) %collective-permute-start.13) | collective-permute-done | bytes 262176 | tf_op jit(solution)/shard_map/ppermute | solution.py:91
  84.6 1.9 %collective-permute-done.14.refs_5_ = bf16[1,32,4096]{2,1,0:T(8,128)(2,1)S(1)} collective-permute-done((bf16[1,32,4096]{2,1,0:T(8,128)(2,1)S(1)}, bf16[1,32,4096]{2,1,0:T(8,128)(2,1)S(1)}, u32[]{:S(2)}, u32[]{:S(2)}) %collective-permute-start.14) | collective-permute-done | bytes 262176 | tf_op jit(solution)/shard_map/ppermute | solution.py:91
  86.5 3.0 %shard_map.62 = (f32[8,32,512]{2,1,0:T(8,128)S(1)}, f32[8,32,512]{2,1,0:T(8,128)S(1)}) custom-call(s32[2]{0:T(128)S(1)} %pad_add_fusion.refs_0_, bf16[2,32,4096]{2,1,0:T(8,128)(2,1)S(1)} %collective-permute-done.9.refs_1_, bf16[2,32,4096]{2,1,0:T(8,128)(2,1)S(1)} %collective-permute-done.11.refs_2_, ...), custom_call_target="tpu_custom_call" | custom-call | flops 1100000000 | bytes 1024 | tf_op jit(solution)/shard_map/pallas_call | solution.py:162
  89.5 1.7 %collective-permute-start.15 = (f32[8,32,512]{2,1,0:T(8,128)S(1)}, f32[8,32,512]{2,1,0:T(8,128)S(1)}, u32[]{:S(2)}, u32[]{:S(2)}) collective-permute-start(f32[8,32,512]{2,1,0:T(8,128)S(1)} %get-tuple-element.50), channel_id=1, source_target_pairs={{0,16},{16,0},{32,48},{48,32},{64,80},{80,64},{96,112},{112,96},{1... | collective-permute-start | bytes 1572872 | tf_op jit(solution)/shard_map/ppermute | solution.py:218
  91.2 1.5 %collective-permute-done.15 = f32[8,32,512]{2,1,0:T(8,128)S(1)} collective-permute-done((f32[8,32,512]{2,1,0:T(8,128)S(1)}, f32[8,32,512]{2,1,0:T(8,128)S(1)}, u32[]{:S(2)}, u32[]{:S(2)}) %collective-permute-start.15) | collective-permute-done | bytes 524320 | tf_op jit(solution)/shard_map/ppermute | solution.py:218
  92.9 10.5 %all_to_all.5 = bf16[8,32,512]{2,1,0:T(8,128)(2,1)S(1)} all-to-all(bf16[8,32,512]{2,1,0:T(8,128)(2,1)S(1)} %add_convert_fusion), channel_id=1, replica_groups={{0,32,64,96,128,160,192,224},{16,48,80,112,144,176,208,240},{1,33,65,97..., dimensions={0} | all-to-all | bytes 524288 | tf_op jit(solution)/shard_map/all_to_all | solution.py:220
  103.4 0.7 convert_reduce_fusion
  (24 shorter events, 0.4 us)
Async XLA Ops:
  4.3 22.8 %collective-permute-start = (bf16[2,32,4096]{2,1,0:T(8,128)(2,1)}, bf16[2,32,4096]{2,1,0:T(8,128)(2,1)S(1)}, u32[]{:S(2)}, u32[]{:S(2)}) collective-permute-start(bf16[2,32,4096]{2,1,0:T(8,128)(2,1)} %shard_map.55.refs_0_), channel_id=1, source_target_pairs={{0,4},{1,5},{2,6},{3,7},{4,8},{5,9},{6,10},{7,11},{8,12},{9,13},{1... | collective-permute-start | bytes 1572872 | tf_op jit(solution)/shard_map/ppermute | solution.py:91
  8.2 27.6 %collective-permute-start.1 = (bf16[2,32,4096]{2,1,0:T(8,128)(2,1)}, bf16[2,32,4096]{2,1,0:T(8,128)(2,1)S(1)}, u32[]{:S(2)}, u32[]{:S(2)}) collective-permute-start(bf16[2,32,4096]{2,1,0:T(8,128)(2,1)} %shard_map.55.refs_0_), channel_id=1, source_target_pairs={{0,12},{1,13},{2,14},{3,15},{4,0},{5,1},{6,2},{7,3},{8,4},{9,5},{1... | collective-permute-start | bytes 1572872 | tf_op jit(solution)/shard_map/ppermute | solution.py:91
  11.2 24.6 %collective-permute-start.2 = (bf16[2,32,4096]{2,1,0:T(8,128)(2,1)}, bf16[2,32,4096]{2,1,0:T(8,128)(2,1)S(1)}, u32[]{:S(2)}, u32[]{:S(2)}) collective-permute-start(bf16[2,32,4096]{2,1,0:T(8,128)(2,1)} %shard_map.55.refs_0_), channel_id=1, source_target_pairs={{0,1},{1,2},{2,3},{3,0},{4,5},{5,6},{6,7},{7,4},{8,9},{9,10},{10,1... | collective-permute-start | bytes 1572872 | tf_op jit(solution)/shard_map/ppermute | solution.py:91
  12.4 23.4 %collective-permute-start.3 = (bf16[2,32,4096]{2,1,0:T(8,128)(2,1)}, bf16[2,32,4096]{2,1,0:T(8,128)(2,1)S(1)}, u32[]{:S(2)}, u32[]{:S(2)}) collective-permute-start(bf16[2,32,4096]{2,1,0:T(8,128)(2,1)} %shard_map.55.refs_0_), channel_id=1, source_target_pairs={{0,3},{1,0},{2,1},{3,2},{4,7},{5,4},{6,5},{7,6},{8,11},{9,8},{10,9... | collective-permute-start | bytes 1572872 | tf_op jit(solution)/shard_map/ppermute | solution.py:91
  13.9 29.4 %collective-permute-start.6 = (bf16[2,32,4096]{2,1,0:T(8,128)(2,1)}, bf16[2,32,4096]{2,1,0:T(8,128)(2,1)S(1)}, u32[]{:S(2)}, u32[]{:S(2)}) collective-permute-start(bf16[2,32,4096]{2,1,0:T(8,128)(2,1)} %shard_map.55.refs_0_), channel_id=1, source_target_pairs={{0,2},{1,3},{2,0},{3,1},{4,6},{5,7},{6,4},{7,5},{8,10},{9,11},{10,... | collective-permute-start | bytes 1572872 | tf_op jit(solution)/shard_map/ppermute | solution.py:91
  35.8 0.8 copy-start.3
  36.6 0.7 copy-start.5
  37.3 23.7 %collective-permute-start.8 = (bf16[4,32,4096]{2,1,0:T(8,128)(2,1)S(1)}, bf16[4,32,4096]{2,1,0:T(8,128)(2,1)S(1)}, u32[]{:S(2)}, u32[]{:S(2)}) collective-permute-start(bf16[4,32,4096]{2,1,0:T(8,128)(2,1)S(1)} %get-tuple-element.34.refs_4_), channel_id=1, source_target_pairs={{0,3},{1,0},{2,1},{3,2},{4,7},{5,4},{6,5},{7,6},{8,11},{9,8},{10,9... | collective-permute-start | bytes 3145736 | tf_op jit(solution)/shard_map/ppermute | solution.py:91
  39.7 34.2 %collective-permute-start.10 = (bf16[4,32,4096]{2,1,0:T(8,128)(2,1)S(1)}, bf16[4,32,4096]{2,1,0:T(8,128)(2,1)S(1)}, u32[]{:S(2)}, u32[]{:S(2)}) collective-permute-start(bf16[4,32,4096]{2,1,0:T(8,128)(2,1)S(1)} %get-tuple-element.34.refs_4_), channel_id=1, source_target_pairs={{0,1},{1,2},{2,3},{3,0},{4,5},{5,6},{6,7},{7,4},{8,9},{9,10},{10,1... | collective-permute-start | bytes 3145736 | tf_op jit(solution)/shard_map/ppermute | solution.py:91
  39.7 11.5 %collective-permute-start.4 = (bf16[1,32,4096]{2,1,0:T(8,128)(2,1)}, bf16[1,32,4096]{2,1,0:T(8,128)(2,1)S(1)}, u32[]{:S(2)}, u32[]{:S(2)}) collective-permute-start(bf16[1,32,4096]{2,1,0:T(8,128)(2,1)} %copy-done.5), channel_id=1, source_target_pairs={{0,4},{1,5},{2,6},{3,7},{4,8},{5,9},{6,10},{7,11},{8,12},{9,13},{1... | collective-permute-start | bytes 786440 | tf_op jit(solution)/shard_map/ppermute | solution.py:91
  42.7 8.5 %collective-permute-start.5 = (bf16[1,32,4096]{2,1,0:T(8,128)(2,1)S(1)}, bf16[1,32,4096]{2,1,0:T(8,128)(2,1)S(1)}, u32[]{:S(2)}, u32[]{:S(2)}) collective-permute-start(bf16[1,32,4096]{2,1,0:T(8,128)(2,1)S(1)} %get-tuple-element.31), channel_id=1, source_target_pairs={{0,12},{1,13},{2,14},{3,15},{4,0},{5,1},{6,2},{7,3},{8,4},{9,5},{1... | collective-permute-start | bytes 786440 | tf_op jit(solution)/shard_map/ppermute | solution.py:91
  43.3 3.4 %copy-start = (bf16[2,512,4096]{2,1,0:T(8,128)(2,1)S(1)}, bf16[2,512,4096]{2,1,0:T(8,128)(2,1)}, u32[]{:S(2)}) copy-start(bf16[2,512,4096]{2,1,0:T(8,128)(2,1)} %refs_6_.1) | copy-start | bytes 25165828
  46.7 1.0 %copy-start.2 = (bf16[2,32,4096]{2,1,0:T(8,128)(2,1)S(1)}, bf16[2,32,4096]{2,1,0:T(8,128)(2,1)}, u32[]{:S(2)}) copy-start(bf16[2,32,4096]{2,1,0:T(8,128)(2,1)} %shard_map.55.refs_0_) | copy-start | bytes 1572868
  47.7 1.0 %copy-start.4 = (bf16[2,32,4096]{2,1,0:T(8,128)(2,1)S(1)}, bf16[2,32,4096]{2,1,0:T(8,128)(2,1)}, u32[]{:S(2)}) copy-start(bf16[2,32,4096]{2,1,0:T(8,128)(2,1)} %copy-done.3) | copy-start | bytes 1572868
  48.8 14.3 %copy-start.1 = (bf16[2,512,4096]{2,1,0:T(8,128)(2,1)S(1)}, bf16[2,512,4096]{2,1,0:T(8,128)(2,1)}, u32[]{:S(2)}) copy-start(bf16[2,512,4096]{2,1,0:T(8,128)(2,1)} %refs_6_.1) | copy-start | bytes 25165828
  51.2 22.7 %collective-permute-start.11 = (bf16[2,32,4096]{2,1,0:T(8,128)(2,1)S(1)}, bf16[2,32,4096]{2,1,0:T(8,128)(2,1)S(1)}, u32[]{:S(2)}, u32[]{:S(2)}) collective-permute-start(bf16[2,32,4096]{2,1,0:T(8,128)(2,1)S(1)} %collective-permute-done.6.refs_3_), channel_id=1, source_target_pairs={{0,4},{1,5},{2,6},{3,7},{4,8},{5,9},{6,10},{7,11},{8,12},{9,13},{1... | collective-permute-start | bytes 1572872 | tf_op jit(solution)/shard_map/ppermute | solution.py:91
  54.9 19.0 %collective-permute-start.12 = (bf16[2,32,4096]{2,1,0:T(8,128)(2,1)S(1)}, bf16[2,32,4096]{2,1,0:T(8,128)(2,1)S(1)}, u32[]{:S(2)}, u32[]{:S(2)}) collective-permute-start(bf16[2,32,4096]{2,1,0:T(8,128)(2,1)S(1)} %collective-permute-done.6.refs_3_), channel_id=1, source_target_pairs={{0,12},{1,13},{2,14},{3,15},{4,0},{5,1},{6,2},{7,3},{8,4},{9,5},{1... | collective-permute-start | bytes 1572872 | tf_op jit(solution)/shard_map/ppermute | solution.py:91
  54.9 19.0 %collective-permute-start.7 = (bf16[2,32,4096]{2,1,0:T(8,128)(2,1)S(1)}, bf16[2,32,4096]{2,1,0:T(8,128)(2,1)S(1)}, u32[]{:S(2)}, u32[]{:S(2)}) collective-permute-start(bf16[2,32,4096]{2,1,0:T(8,128)(2,1)S(1)} %shard_map.58.refs_0_), channel_id=1, source_target_pairs={{0,1},{1,2},{2,3},{3,0},{4,5},{5,6},{6,7},{7,4},{8,9},{9,10},{10,1... | collective-permute-start | bytes 1572872 | tf_op jit(solution)/shard_map/ppermute | solution.py:91
  61.0 13.0 %collective-permute-start.9 = (bf16[2,32,4096]{2,1,0:T(8,128)(2,1)S(1)}, bf16[2,32,4096]{2,1,0:T(8,128)(2,1)S(1)}, u32[]{:S(2)}, u32[]{:S(2)}) collective-permute-start(bf16[2,32,4096]{2,1,0:T(8,128)(2,1)S(1)} %shard_map.58.refs_0_), channel_id=1, source_target_pairs={{0,3},{1,0},{2,1},{3,2},{4,7},{5,4},{6,5},{7,6},{8,11},{9,8},{10,9... | collective-permute-start | bytes 1572872 | tf_op jit(solution)/shard_map/ppermute | solution.py:91
  74.0 10.6 %collective-permute-start.13 = (bf16[1,32,4096]{2,1,0:T(8,128)(2,1)S(1)}, bf16[1,32,4096]{2,1,0:T(8,128)(2,1)S(1)}, u32[]{:S(2)}, u32[]{:S(2)}) collective-permute-start(bf16[1,32,4096]{2,1,0:T(8,128)(2,1)S(1)} %get-tuple-element.44), channel_id=1, source_target_pairs={{0,1},{1,2},{2,3},{3,0},{4,5},{5,6},{6,7},{7,4},{8,9},{9,10},{10,1... | collective-permute-start | bytes 786440 | tf_op jit(solution)/shard_map/ppermute | solution.py:91
  79.4 7.1 %collective-permute-start.14 = (bf16[1,32,4096]{2,1,0:T(8,128)(2,1)S(1)}, bf16[1,32,4096]{2,1,0:T(8,128)(2,1)S(1)}, u32[]{:S(2)}, u32[]{:S(2)}) collective-permute-start(bf16[1,32,4096]{2,1,0:T(8,128)(2,1)S(1)} %get-tuple-element.45), channel_id=1, source_target_pairs={{0,3},{1,0},{2,1},{3,2},{4,7},{5,4},{6,5},{7,6},{8,11},{9,8},{10,9... | collective-permute-start | bytes 786440 | tf_op jit(solution)/shard_map/ppermute | solution.py:91
  89.5 3.3 %collective-permute-start.15 = (f32[8,32,512]{2,1,0:T(8,128)S(1)}, f32[8,32,512]{2,1,0:T(8,128)S(1)}, u32[]{:S(2)}, u32[]{:S(2)}) collective-permute-start(f32[8,32,512]{2,1,0:T(8,128)S(1)} %get-tuple-element.50), channel_id=1, source_target_pairs={{0,16},{16,0},{32,48},{48,32},{64,80},{80,64},{96,112},{112,96},{1... | collective-permute-start | bytes 1572872 | tf_op jit(solution)/shard_map/ppermute | solution.py:218

commit v8 on v6

--- a/solution.py
+++ b/solution.py
@@ -197,7 +197,7 @@
     z2, both_xr = in_order(z2, both_xr)
     z2_xr = move(z2, 0, -1)
     shards = [shard(z2), shard(both_xr, 0), shard(both_xr, 2)]
-    second = score_call(next_kernel, shards, train_grads, blocks_shape(3, train_grads, queries))
+    second = score_call(next_kernel, shards, train_grads, blocks_shape(3, train_grads, queries), weight=6)
     z2_xl, z2_xr, both_xl, zl_x2, zr_x2, second = in_order(z2_xl, z2_xr, both_xl, zl_x2, zr_x2, second)
     halves = arrange([z2_xl, z2_xr], [[(0, 0)], [(1, 1)]])
     z2_x2 = move(halves[0], 0, 1), move(halves[1], 0, -1)
@@ -208,7 +208,7 @@
         (2, 1), (-1, 2), (1, 2), (2, 2),
     ]
     shards = [shard(z2_xl), shard(both_xl, 0), shard(both_xl, 2)]
-    third = score_call(next_kernel, shards, train_grads, blocks_shape(3, train_grads, queries))
+    third = score_call(next_kernel, shards, train_grads, blocks_shape(3, train_grads, queries), weight=6)
 
     shards = [shard(z2_xr), shard(zl_x2), shard(zr_x2), [(half, 0) for half in z2_x2]]
     kernel = lambda own, count, *refs: last_kernel(own, count, offsets, *refs)

time: 106 us -> 104 us (0.981)
  local copies, waits for them, and re-layouts: 7.82 us -> 4.43 us
  waiting for transfers between devices: 34.6 us -> 37.7 us
  Pallas kernels: 16 us -> 14.7 us
    unnamed x12 -> x6, local copies, waits for them, and re-layouts: 7.82 us -> 4.43 us
    ppermute x15, waiting for transfers between devices: 33 us -> 36.2 us  [move(): lax.ppermute(value, 'ex', [(z * SIDE + x, to(z, x)) for z in range(SIDE)...]
  transfers between devices with their start and end apart: 16 -> 16, of which waited for: 6 -> 7; matrix products, arithmetic and copies ran while one was open for 0% -> 0% of each run, Pallas kernels for 7% -> 7%
where the time goes in v8:
time: 104 us; the launch traced here: 103 us
  waiting for transfers between devices  37.7 us (36%)
  starting transfers between devices  34.1 us (33%)
  Pallas kernels  14.7 us (14%)
  blocking collectives  11.1 us (11%)
  local copies, waits for them, and re-layouts  4.43 us (4%)
    ppermute x15, waiting for transfers between devices, move(): lax.ppermute(value, 'ex', [(z * SIDE + x, to(z, x)) for z in range(SIDE)...  36.2 us
    ppermute x15, starting transfers between devices, move(): lax.ppermute(value, 'ex', [(z * SIDE + x, to(z, x)) for z in range(SIDE)...  32.4 us
    all_to_all x1, blocking collectives, local(): lax.all_to_all(parts.astype(jnp.bfloat16), 'layer', split_axis=0, concat_...  11.1 us
    pallas_call x4, Pallas kernels, score_call(): pl.pallas_call(functools.partial(kernel, shards, len(arrays)), out_shape=...  10.2 us
    unnamed x6, local copies, waits for them, and re-layouts  4.43 us
    pallas_call x1, Pallas kernels, precondition(): pl.pallas_call(precondition_kernel, out_shape=jax.ShapeDtypeStruct(raw.sh...  4.33 us
  transfers between devices with their start and end apart: 16, of which 7 were waited for; matrix products, arithmetic and copies ran while one was open for 0% of the time, Pallas kernels for 7%

profile of v8, /device:TPU:1, one launch (start us, length us, event | category | flops | bytes accessed | tf_op | source)
XLA Modules:
  0.0 103.0 jit_solution(558061898004814329)
XLA Ops:
  0.0 4.3 %shard_map.55.refs_0_ = bf16[2,32,4096]{2,1,0:T(8,128)(2,1)} custom-call(bf16[2,32,4096]{2,1,0:T(8,128)(2,1)} %raw.1, f32[2,64,64]{2,1,0:T(8,128)} %basis_out.1, f32[2,64,64]{2,1,0:T(8,128)} %basis_in.1, f32[2,64,64]{2,1,0:T(8,128)} %eigen.1), custom_call_target="tpu_custom_call" | custom-call | tf_op jit(solution)/shard_map/pallas_call | solution.py:78
  4.3 3.8 %collective-permute-start = (bf16[2,32,4096]{2,1,0:T(8,128)(2,1)}, bf16[2,32,4096]{2,1,0:T(8,128)(2,1)S(1)}, u32[]{:S(2)}, u32[]{:S(2)}) collective-permute-start(bf16[2,32,4096]{2,1,0:T(8,128)(2,1)} %shard_map.55.refs_0_), channel_id=1, source_target_pairs={{0,4},{1,5},{2,6},{3,7},{4,8},{5,9},{6,10},{7,11},{8,12},{9,13},{1... | collective-permute-start | bytes 1572872 | tf_op jit(solution)/shard_map/ppermute | solution.py:91
  8.2 3.0 %collective-permute-start.1 = (bf16[2,32,4096]{2,1,0:T(8,128)(2,1)}, bf16[2,32,4096]{2,1,0:T(8,128)(2,1)S(1)}, u32[]{:S(2)}, u32[]{:S(2)}) collective-permute-start(bf16[2,32,4096]{2,1,0:T(8,128)(2,1)} %shard_map.55.refs_0_), channel_id=1, source_target_pairs={{0,12},{1,13},{2,14},{3,15},{4,0},{5,1},{6,2},{7,3},{8,4},{9,5},{1... | collective-permute-start | bytes 1572872 | tf_op jit(solution)/shard_map/ppermute | solution.py:91
  11.2 1.2 %collective-permute-start.2 = (bf16[2,32,4096]{2,1,0:T(8,128)(2,1)}, bf16[2,32,4096]{2,1,0:T(8,128)(2,1)S(1)}, u32[]{:S(2)}, u32[]{:S(2)}) collective-permute-start(bf16[2,32,4096]{2,1,0:T(8,128)(2,1)} %shard_map.55.refs_0_), channel_id=1, source_target_pairs={{0,1},{1,2},{2,3},{3,0},{4,5},{5,6},{6,7},{7,4},{8,9},{9,10},{10,1... | collective-permute-start | bytes 1572872 | tf_op jit(solution)/shard_map/ppermute | solution.py:91
  12.4 1.5 %collective-permute-start.3 = (bf16[2,32,4096]{2,1,0:T(8,128)(2,1)}, bf16[2,32,4096]{2,1,0:T(8,128)(2,1)S(1)}, u32[]{:S(2)}, u32[]{:S(2)}) collective-permute-start(bf16[2,32,4096]{2,1,0:T(8,128)(2,1)} %shard_map.55.refs_0_), channel_id=1, source_target_pairs={{0,3},{1,0},{2,1},{3,2},{4,7},{5,4},{6,5},{7,6},{8,11},{9,8},{10,9... | collective-permute-start | bytes 1572872 | tf_op jit(solution)/shard_map/ppermute | solution.py:91
  13.9 1.5 %collective-permute-start.6 = (bf16[2,32,4096]{2,1,0:T(8,128)(2,1)}, bf16[2,32,4096]{2,1,0:T(8,128)(2,1)S(1)}, u32[]{:S(2)}, u32[]{:S(2)}) collective-permute-start(bf16[2,32,4096]{2,1,0:T(8,128)(2,1)} %shard_map.55.refs_0_), channel_id=1, source_target_pairs={{0,2},{1,3},{2,0},{3,1},{4,6},{5,7},{6,4},{7,5},{8,10},{9,11},{10,... | collective-permute-start | bytes 1572872 | tf_op jit(solution)/shard_map/ppermute | solution.py:91
  15.4 11.7 %collective-permute-done.refs_0_ = bf16[2,32,4096]{2,1,0:T(8,128)(2,1)S(1)} collective-permute-done((bf16[2,32,4096]{2,1,0:T(8,128)(2,1)}, bf16[2,32,4096]{2,1,0:T(8,128)(2,1)S(1)}, u32[]{:S(2)}, u32[]{:S(2)}) %collective-permute-start) | collective-permute-done | bytes 524320 | tf_op jit(solution)/shard_map/ppermute | solution.py:91
  27.1 8.6 %collective-permute-done.1.refs_1_ = bf16[2,32,4096]{2,1,0:T(8,128)(2,1)S(1)} collective-permute-done((bf16[2,32,4096]{2,1,0:T(8,128)(2,1)}, bf16[2,32,4096]{2,1,0:T(8,128)(2,1)S(1)}, u32[]{:S(2)}, u32[]{:S(2)}) %collective-permute-start.1) | collective-permute-done | bytes 524320 | tf_op jit(solution)/shard_map/ppermute | solution.py:91
  35.8 0.1 shard_map.56
  35.9 2.5 %collective-permute-start.8 = (bf16[4,32,4096]{2,1,0:T(8,128)(2,1)S(1)}, bf16[4,32,4096]{2,1,0:T(8,128)(2,1)S(1)}, u32[]{:S(2)}, u32[]{:S(2)}) collective-permute-start(bf16[4,32,4096]{2,1,0:T(8,128)(2,1)S(1)} %get-tuple-element.34.refs_4_), channel_id=1, source_target_pairs={{0,3},{1,0},{2,1},{3,2},{4,7},{5,4},{6,5},{7,6},{8,11},{9,8},{10,9... | collective-permute-start | bytes 3145736 | tf_op jit(solution)/shard_map/ppermute | solution.py:91
  38.4 0.1 pad_add_fusion.refs_0_
  38.5 3.0 %collective-permute-start.4 = (bf16[1,32,4096]{2,1,0:T(8,128)(2,1)S(1)}, bf16[1,32,4096]{2,1,0:T(8,128)(2,1)S(1)}, u32[]{:S(2)}, u32[]{:S(2)}) collective-permute-start(bf16[1,32,4096]{2,1,0:T(8,128)(2,1)S(1)} %get-tuple-element.30), channel_id=1, source_target_pairs={{0,4},{1,5},{2,6},{3,7},{4,8},{5,9},{6,10},{7,11},{8,12},{9,13},{1... | collective-permute-start | bytes 786440 | tf_op jit(solution)/shard_map/ppermute | solution.py:91
  41.5 0.7 collective-permute-start.5
  42.2 3.4 %copy-done = bf16[2,512,4096]{2,1,0:T(8,128)(2,1)S(1)} copy-done((bf16[2,512,4096]{2,1,0:T(8,128)(2,1)S(1)}, bf16[2,512,4096]{2,1,0:T(8,128)(2,1)}, u32[]{:S(2)}) %copy-start) | copy-done | bytes 8388632
  45.5 1.0 %copy-done.2 = bf16[2,32,4096]{2,1,0:T(8,128)(2,1)S(1)} copy-done((bf16[2,32,4096]{2,1,0:T(8,128)(2,1)S(1)}, bf16[2,32,4096]{2,1,0:T(8,128)(2,1)}, u32[]{:S(2)}) %copy-start.2) | copy-done | bytes 524312
  46.6 2.4 %shard_map.57.refs_7_ = f32[6,32,512]{2,1,0:T(8,128)S(1)} custom-call(bf16[2,32,4096]{2,1,0:T(8,128)(2,1)S(1)} %copy-done.2, bf16[2,32,4096]{2,1,0:T(8,128)(2,1)S(1)} %collective-permute-done.2.refs_1_, bf16[2,32,4096]{2,1,0:T(8,128)(2,1)S(1)} %collective-permute-done.3.refs_2_, bf16[2,32,4096]{2,1,0:T(8,128)(2,1)S(1)} %collective-permute-done.6.refs_3_, ...), custom_call_target="tpu_custom_call" | custom-call | flops 11000000512 | bytes 1024 | tf_op jit(solution)/shard_map/pallas_call | solution.py:162
  49.0 4.6 %collective-permute-start.11 = (bf16[2,32,4096]{2,1,0:T(8,128)(2,1)S(1)}, bf16[2,32,4096]{2,1,0:T(8,128)(2,1)S(1)}, u32[]{:S(2)}, u32[]{:S(2)}) collective-permute-start(bf16[2,32,4096]{2,1,0:T(8,128)(2,1)S(1)} %collective-permute-done.6.refs_3_), channel_id=1, source_target_pairs={{0,4},{1,5},{2,6},{3,7},{4,8},{5,9},{6,10},{7,11},{8,12},{9,13},{1... | collective-permute-start | bytes 1572872 | tf_op jit(solution)/shard_map/ppermute | solution.py:91
  53.6 3.5 %collective-permute-start.7 = (bf16[2,32,4096]{2,1,0:T(8,128)(2,1)S(1)}, bf16[2,32,4096]{2,1,0:T(8,128)(2,1)S(1)}, u32[]{:S(2)}, u32[]{:S(2)}) collective-permute-start(bf16[2,32,4096]{2,1,0:T(8,128)(2,1)S(1)} %shard_map.58.refs_0_), channel_id=1, source_target_pairs={{0,1},{1,2},{2,3},{3,0},{4,5},{5,6},{6,7},{7,4},{8,9},{9,10},{10,1... | collective-permute-start | bytes 1572872 | tf_op jit(solution)/shard_map/ppermute | solution.py:91
  57.2 2.5 %collective-permute-done.8.refs_1_ = bf16[4,32,4096]{2,1,0:T(8,128)(2,1)S(1)} collective-permute-done((bf16[4,32,4096]{2,1,0:T(8,128)(2,1)S(1)}, bf16[4,32,4096]{2,1,0:T(8,128)(2,1)S(1)}, u32[]{:S(2)}, u32[]{:S(2)}) %collective-permute-start.8) | collective-permute-done | bytes 1048608 | tf_op jit(solution)/shard_map/ppermute | solution.py:91
  59.6 2.0 %collective-permute-start.9 = (bf16[2,32,4096]{2,1,0:T(8,128)(2,1)S(1)}, bf16[2,32,4096]{2,1,0:T(8,128)(2,1)S(1)}, u32[]{:S(2)}, u32[]{:S(2)}) collective-permute-start(bf16[2,32,4096]{2,1,0:T(8,128)(2,1)S(1)} %shard_map.58.refs_0_), channel_id=1, source_target_pairs={{0,3},{1,0},{2,1},{3,2},{4,7},{5,4},{6,5},{7,6},{8,11},{9,8},{10,9... | collective-permute-start | bytes 1572872 | tf_op jit(solution)/shard_map/ppermute | solution.py:91
  61.6 2.4 %shard_map.59.refs_8_ = f32[3,32,512]{2,1,0:T(8,128)S(1)} custom-call(bf16[2,32,4096]{2,1,0:T(8,128)(2,1)S(1)} %shard_map.58.refs_0_, bf16[4,32,4096]{2,1,0:T(8,128)(2,1)S(1)} %collective-permute-done.8.refs_1_, bf16[2,512,4096]{2,1,0:T(8,128)(2,1)S(1)} %copy-done.1), custom_call_target="tpu_custom_call" | custom-call | flops 6600000000 | bytes 1024 | tf_op jit(solution)/shard_map/pallas_call | solution.py:162
  64.0 8.7 %collective-permute-done.7.refs_0_ = bf16[2,32,4096]{2,1,0:T(8,128)(2,1)S(1)} collective-permute-done((bf16[2,32,4096]{2,1,0:T(8,128)(2,1)S(1)}, bf16[2,32,4096]{2,1,0:T(8,128)(2,1)S(1)}, u32[]{:S(2)}, u32[]{:S(2)}) %collective-permute-start.7) | collective-permute-done | bytes 524320 | tf_op jit(solution)/shard_map/ppermute | solution.py:91
  72.7 5.0 %collective-permute-start.13 = (bf16[1,32,4096]{2,1,0:T(8,128)(2,1)S(1)}, bf16[1,32,4096]{2,1,0:T(8,128)(2,1)S(1)}, u32[]{:S(2)}, u32[]{:S(2)}) collective-permute-start(bf16[1,32,4096]{2,1,0:T(8,128)(2,1)S(1)} %get-tuple-element.44), channel_id=1, source_target_pairs={{0,1},{1,2},{2,3},{3,0},{4,5},{5,6},{6,7},{7,4},{8,9},{9,10},{10,1... | collective-permute-start | bytes 786440 | tf_op jit(solution)/shard_map/ppermute | solution.py:91
  77.8 2.4 %shard_map.61.refs_9_ = f32[3,32,512]{2,1,0:T(8,128)S(1)} custom-call(bf16[2,32,4096]{2,1,0:T(8,128)(2,1)S(1)} %collective-permute-done.7.refs_0_, bf16[4,32,4096]{2,1,0:T(8,128)(2,1)S(1)} %collective-permute-done.10.refs_1_, bf16[2,512,4096]{2,1,0:T(8,128)(2,1)S(1)} %copy-done.1), custom_call_target="tpu_custom_call" | custom-call | flops 6600000000 | bytes 1024 | tf_op jit(solution)/shard_map/pallas_call | solution.py:162
  80.1 2.8 %collective-permute-done.13.refs_4_ = bf16[1,32,4096]{2,1,0:T(8,128)(2,1)S(1)} collective-permute-done((bf16[1,32,4096]{2,1,0:T(8,128)(2,1)S(1)}, bf16[1,32,4096]{2,1,0:T(8,128)(2,1)S(1)}, u32[]{:S(2)}, u32[]{:S(2)}) %collective-permute-start.13) | collective-permute-done | bytes 262176 | tf_op jit(solution)/shard_map/ppermute | solution.py:91
  82.9 1.9 %collective-permute-done.14.refs_5_ = bf16[1,32,4096]{2,1,0:T(8,128)(2,1)S(1)} collective-permute-done((bf16[1,32,4096]{2,1,0:T(8,128)(2,1)S(1)}, bf16[1,32,4096]{2,1,0:T(8,128)(2,1)S(1)}, u32[]{:S(2)}, u32[]{:S(2)}) %collective-permute-start.14) | collective-permute-done | bytes 262176 | tf_op jit(solution)/shard_map/ppermute | solution.py:91
  84.8 3.0 %shard_map.62 = (f32[8,32,512]{2,1,0:T(8,128)S(1)}, f32[8,32,512]{2,1,0:T(8,128)S(1)}) custom-call(s32[2]{0:T(128)S(1)} %pad_add_fusion.refs_0_, bf16[2,32,4096]{2,1,0:T(8,128)(2,1)S(1)} %collective-permute-done.9.refs_1_, bf16[2,32,4096]{2,1,0:T(8,128)(2,1)S(1)} %collective-permute-done.11.refs_2_, ...), custom_call_target="tpu_custom_call" | custom-call | flops 1100000000 | bytes 1024 | tf_op jit(solution)/shard_map/pallas_call | solution.py:162
  87.8 1.7 %collective-permute-start.15 = (f32[8,32,512]{2,1,0:T(8,128)S(1)}, f32[8,32,512]{2,1,0:T(8,128)S(1)}, u32[]{:S(2)}, u32[]{:S(2)}) collective-permute-start(f32[8,32,512]{2,1,0:T(8,128)S(1)} %get-tuple-element.50), channel_id=1, source_target_pairs={{0,16},{16,0},{32,48},{48,32},{64,80},{80,64},{96,112},{112,96},{1... | collective-permute-start | bytes 1572872 | tf_op jit(solution)/shard_map/ppermute | solution.py:218
  89.6 1.5 %collective-permute-done.15 = f32[8,32,512]{2,1,0:T(8,128)S(1)} collective-permute-done((f32[8,32,512]{2,1,0:T(8,128)S(1)}, f32[8,32,512]{2,1,0:T(8,128)S(1)}, u32[]{:S(2)}, u32[]{:S(2)}) %collective-permute-start.15) | collective-permute-done | bytes 524320 | tf_op jit(solution)/shard_map/ppermute | solution.py:218
  91.1 0.1 add_convert_fusion
  91.2 11.1 %all_to_all.5 = bf16[8,32,512]{2,1,0:T(8,128)(2,1)S(1)} all-to-all(bf16[8,32,512]{2,1,0:T(8,128)(2,1)S(1)} %add_convert_fusion), channel_id=1, replica_groups={{0,32,64,96,128,160,192,224},{16,48,80,112,144,176,208,240},{1,33,65,97..., dimensions={0} | all-to-all | bytes 524288 | tf_op jit(solution)/shard_map/all_to_all | solution.py:220
  102.3 0.7 convert_reduce_fusion
  (18 shorter events, 0.1 us)
Async XLA Ops:
  4.3 22.8 %collective-permute-start = (bf16[2,32,4096]{2,1,0:T(8,128)(2,1)}, bf16[2,32,4096]{2,1,0:T(8,128)(2,1)S(1)}, u32[]{:S(2)}, u32[]{:S(2)}) collective-permute-start(bf16[2,32,4096]{2,1,0:T(8,128)(2,1)} %shard_map.55.refs_0_), channel_id=1, source_target_pairs={{0,4},{1,5},{2,6},{3,7},{4,8},{5,9},{6,10},{7,11},{8,12},{9,13},{1... | collective-permute-start | bytes 1572872 | tf_op jit(solution)/shard_map/ppermute | solution.py:91
  8.2 27.6 %collective-permute-start.1 = (bf16[2,32,4096]{2,1,0:T(8,128)(2,1)}, bf16[2,32,4096]{2,1,0:T(8,128)(2,1)S(1)}, u32[]{:S(2)}, u32[]{:S(2)}) collective-permute-start(bf16[2,32,4096]{2,1,0:T(8,128)(2,1)} %shard_map.55.refs_0_), channel_id=1, source_target_pairs={{0,12},{1,13},{2,14},{3,15},{4,0},{5,1},{6,2},{7,3},{8,4},{9,5},{1... | collective-permute-start | bytes 1572872 | tf_op jit(solution)/shard_map/ppermute | solution.py:91
  11.2 24.6 %collective-permute-start.2 = (bf16[2,32,4096]{2,1,0:T(8,128)(2,1)}, bf16[2,32,4096]{2,1,0:T(8,128)(2,1)S(1)}, u32[]{:S(2)}, u32[]{:S(2)}) collective-permute-start(bf16[2,32,4096]{2,1,0:T(8,128)(2,1)} %shard_map.55.refs_0_), channel_id=1, source_target_pairs={{0,1},{1,2},{2,3},{3,0},{4,5},{5,6},{6,7},{7,4},{8,9},{9,10},{10,1... | collective-permute-start | bytes 1572872 | tf_op jit(solution)/shard_map/ppermute | solution.py:91
  12.4 23.4 %collective-permute-start.3 = (bf16[2,32,4096]{2,1,0:T(8,128)(2,1)}, bf16[2,32,4096]{2,1,0:T(8,128)(2,1)S(1)}, u32[]{:S(2)}, u32[]{:S(2)}) collective-permute-start(bf16[2,32,4096]{2,1,0:T(8,128)(2,1)} %shard_map.55.refs_0_), channel_id=1, source_target_pairs={{0,3},{1,0},{2,1},{3,2},{4,7},{5,4},{6,5},{7,6},{8,11},{9,8},{10,9... | collective-permute-start | bytes 1572872 | tf_op jit(solution)/shard_map/ppermute | solution.py:91
  13.9 28.3 %collective-permute-start.6 = (bf16[2,32,4096]{2,1,0:T(8,128)(2,1)}, bf16[2,32,4096]{2,1,0:T(8,128)(2,1)S(1)}, u32[]{:S(2)}, u32[]{:S(2)}) collective-permute-start(bf16[2,32,4096]{2,1,0:T(8,128)(2,1)} %shard_map.55.refs_0_), channel_id=1, source_target_pairs={{0,2},{1,3},{2,0},{3,1},{4,6},{5,7},{6,4},{7,5},{8,10},{9,11},{10,... | collective-permute-start | bytes 1572872 | tf_op jit(solution)/shard_map/ppermute | solution.py:91
  35.9 23.8 %collective-permute-start.8 = (bf16[4,32,4096]{2,1,0:T(8,128)(2,1)S(1)}, bf16[4,32,4096]{2,1,0:T(8,128)(2,1)S(1)}, u32[]{:S(2)}, u32[]{:S(2)}) collective-permute-start(bf16[4,32,4096]{2,1,0:T(8,128)(2,1)S(1)} %get-tuple-element.34.refs_4_), channel_id=1, source_target_pairs={{0,3},{1,0},{2,1},{3,2},{4,7},{5,4},{6,5},{7,6},{8,11},{9,8},{10,9... | collective-permute-start | bytes 3145736 | tf_op jit(solution)/shard_map/ppermute | solution.py:91
  38.5 34.2 %collective-permute-start.10 = (bf16[4,32,4096]{2,1,0:T(8,128)(2,1)S(1)}, bf16[4,32,4096]{2,1,0:T(8,128)(2,1)S(1)}, u32[]{:S(2)}, u32[]{:S(2)}) collective-permute-start(bf16[4,32,4096]{2,1,0:T(8,128)(2,1)S(1)} %get-tuple-element.34.refs_4_), channel_id=1, source_target_pairs={{0,1},{1,2},{2,3},{3,0},{4,5},{5,6},{6,7},{7,4},{8,9},{9,10},{10,1... | collective-permute-start | bytes 3145736 | tf_op jit(solution)/shard_map/ppermute | solution.py:91
  38.5 10.5 %collective-permute-start.4 = (bf16[1,32,4096]{2,1,0:T(8,128)(2,1)S(1)}, bf16[1,32,4096]{2,1,0:T(8,128)(2,1)S(1)}, u32[]{:S(2)}, u32[]{:S(2)}) collective-permute-start(bf16[1,32,4096]{2,1,0:T(8,128)(2,1)S(1)} %get-tuple-element.30), channel_id=1, source_target_pairs={{0,4},{1,5},{2,6},{3,7},{4,8},{5,9},{6,10},{7,11},{8,12},{9,13},{1... | collective-permute-start | bytes 786440 | tf_op jit(solution)/shard_map/ppermute | solution.py:91
  41.5 7.5 %collective-permute-start.5 = (bf16[1,32,4096]{2,1,0:T(8,128)(2,1)S(1)}, bf16[1,32,4096]{2,1,0:T(8,128)(2,1)S(1)}, u32[]{:S(2)}, u32[]{:S(2)}) collective-permute-start(bf16[1,32,4096]{2,1,0:T(8,128)(2,1)S(1)} %get-tuple-element.31), channel_id=1, source_target_pairs={{0,12},{1,13},{2,14},{3,15},{4,0},{5,1},{6,2},{7,3},{8,4},{9,5},{1... | collective-permute-start | bytes 786440 | tf_op jit(solution)/shard_map/ppermute | solution.py:91
  42.2 3.4 %copy-start = (bf16[2,512,4096]{2,1,0:T(8,128)(2,1)S(1)}, bf16[2,512,4096]{2,1,0:T(8,128)(2,1)}, u32[]{:S(2)}) copy-start(bf16[2,512,4096]{2,1,0:T(8,128)(2,1)} %refs_6_.1) | copy-start | bytes 25165828
  45.5 1.0 %copy-start.2 = (bf16[2,32,4096]{2,1,0:T(8,128)(2,1)S(1)}, bf16[2,32,4096]{2,1,0:T(8,128)(2,1)}, u32[]{:S(2)}) copy-start(bf16[2,32,4096]{2,1,0:T(8,128)(2,1)} %shard_map.55.refs_0_) | copy-start | bytes 1572868
  46.6 15.1 %copy-start.1 = (bf16[2,512,4096]{2,1,0:T(8,128)(2,1)S(1)}, bf16[2,512,4096]{2,1,0:T(8,128)(2,1)}, u32[]{:S(2)}) copy-start(bf16[2,512,4096]{2,1,0:T(8,128)(2,1)} %refs_6_.1) | copy-start | bytes 25165828
  49.0 23.7 %collective-permute-start.11 = (bf16[2,32,4096]{2,1,0:T(8,128)(2,1)S(1)}, bf16[2,32,4096]{2,1,0:T(8,128)(2,1)S(1)}, u32[]{:S(2)}, u32[]{:S(2)}) collective-permute-start(bf16[2,32,4096]{2,1,0:T(8,128)(2,1)S(1)} %collective-permute-done.6.refs_3_), channel_id=1, source_target_pairs={{0,4},{1,5},{2,6},{3,7},{4,8},{5,9},{6,10},{7,11},{8,12},{9,13},{1... | collective-permute-start | bytes 1572872 | tf_op jit(solution)/shard_map/ppermute | solution.py:91
  53.6 19.1 %collective-permute-start.12 = (bf16[2,32,4096]{2,1,0:T(8,128)(2,1)S(1)}, bf16[2,32,4096]{2,1,0:T(8,128)(2,1)S(1)}, u32[]{:S(2)}, u32[]{:S(2)}) collective-permute-start(bf16[2,32,4096]{2,1,0:T(8,128)(2,1)S(1)} %collective-permute-done.6.refs_3_), channel_id=1, source_target_pairs={{0,12},{1,13},{2,14},{3,15},{4,0},{5,1},{6,2},{7,3},{8,4},{9,5},{1... | collective-permute-start | bytes 1572872 | tf_op jit(solution)/shard_map/ppermute | solution.py:91
  53.6 19.0 %collective-permute-start.7 = (bf16[2,32,4096]{2,1,0:T(8,128)(2,1)S(1)}, bf16[2,32,4096]{2,1,0:T(8,128)(2,1)S(1)}, u32[]{:S(2)}, u32[]{:S(2)}) collective-permute-start(bf16[2,32,4096]{2,1,0:T(8,128)(2,1)S(1)} %shard_map.58.refs_0_), channel_id=1, source_target_pairs={{0,1},{1,2},{2,3},{3,0},{4,5},{5,6},{6,7},{7,4},{8,9},{9,10},{10,1... | collective-permute-start | bytes 1572872 | tf_op jit(solution)/shard_map/ppermute | solution.py:91
  59.6 13.1 %collective-permute-start.9 = (bf16[2,32,4096]{2,1,0:T(8,128)(2,1)S(1)}, bf16[2,32,4096]{2,1,0:T(8,128)(2,1)S(1)}, u32[]{:S(2)}, u32[]{:S(2)}) collective-permute-start(bf16[2,32,4096]{2,1,0:T(8,128)(2,1)S(1)} %shard_map.58.refs_0_), channel_id=1, source_target_pairs={{0,3},{1,0},{2,1},{3,2},{4,7},{5,4},{6,5},{7,6},{8,11},{9,8},{10,9... | collective-permute-start | bytes 1572872 | tf_op jit(solution)/shard_map/ppermute | solution.py:91
  72.7 10.2 %collective-permute-start.13 = (bf16[1,32,4096]{2,1,0:T(8,128)(2,1)S(1)}, bf16[1,32,4096]{2,1,0:T(8,128)(2,1)S(1)}, u32[]{:S(2)}, u32[]{:S(2)}) collective-permute-start(bf16[1,32,4096]{2,1,0:T(8,128)(2,1)S(1)} %get-tuple-element.44), channel_id=1, source_target_pairs={{0,1},{1,2},{2,3},{3,0},{4,5},{5,6},{6,7},{7,4},{8,9},{9,10},{10,1... | collective-permute-start | bytes 786440 | tf_op jit(solution)/shard_map/ppermute | solution.py:91
  77.8 7.1 %collective-permute-start.14 = (bf16[1,32,4096]{2,1,0:T(8,128)(2,1)S(1)}, bf16[1,32,4096]{2,1,0:T(8,128)(2,1)S(1)}, u32[]{:S(2)}, u32[]{:S(2)}) collective-permute-start(bf16[1,32,4096]{2,1,0:T(8,128)(2,1)S(1)} %get-tuple-element.45), channel_id=1, source_target_pairs={{0,3},{1,0},{2,1},{3,2},{4,7},{5,4},{6,5},{7,6},{8,11},{9,8},{10,9... | collective-permute-start | bytes 786440 | tf_op jit(solution)/shard_map/ppermute | solution.py:91
  87.8 3.3 %collective-permute-start.15 = (f32[8,32,512]{2,1,0:T(8,128)S(1)}, f32[8,32,512]{2,1,0:T(8,128)S(1)}, u32[]{:S(2)}, u32[]{:S(2)}) collective-permute-start(f32[8,32,512]{2,1,0:T(8,128)S(1)} %get-tuple-element.50), channel_id=1, source_target_pairs={{0,16},{16,0},{32,48},{48,32},{64,80},{80,64},{96,112},{112,96},{1... | collective-permute-start | bytes 1572872 | tf_op jit(solution)/shard_map/ppermute | solution.py:218
